TPU v7x, 128 devices: a whole 4x4x4 slice. The times are simulated.
128 devices in a mesh: track: 16 (over y, z), strip: 8 (over x, core).
Axes of the slice: x: 4, y: 4, z: 4, core: 2. Of those that a mesh axis runs over, the one named last changes fastest.
Arguments:
- cube: float32 [512, 2560, 224], P('track', 'strip'), may hold values from -64 to 64
- mask: int32 [64, 320], P('track', 'strip'), may hold values 0 or 1
Outputs:
- filtered: float32 [512, 2560, 224], P('track', 'strip')
All inputs are finite; a program needn't handle non-finite values. No bound on the sum of `mask` on one device may be relied on, other than what follows from the above.
Results may differ from a plain program's by a relative error of at most 0.00019.
Values sent between devices are 32-bit elements; how exact they have to be, the bound alone decides.
No kernel may reach another device: no remote copies, remote signals or barrier semaphores. Data moves between devices by JAX's collectives and lax.ppermute only.
A program may use at most 128 MiB of HBM per device.

v0:
```python
import functools

import jax
import jax.numpy as jnp
from jax import lax
from jax.experimental import pallas as pl
from jax.experimental.pallas import tpu as pltpu
from jax.sharding import PartitionSpec as P

TILE = 8
W = 256
F32 = jnp.float32
BF16 = jnp.bfloat16
ROWS = 8
VMEM_LIMIT = 48 * 2**20


def split(x):
    high = x.astype(BF16)
    return high, (x - high.astype(F32)).astype(BF16)


def split3(x):
    high = x.astype(BF16)
    rest = x - high.astype(F32)
    middle = rest.astype(BF16)
    return high, middle, (rest - middle.astype(F32)).astype(BF16)


def dot(a, b):
    return lax.dot_general(a, b, (((1,), (0,)), ((), ())), preferred_element_type=F32)


def dot_t(a, b):
    return lax.dot_general(a, b, (((0,), (0,)), ((), ())), preferred_element_type=F32)


def dot3(a, b):
    a_high, a_low = split(a)
    b_high, b_low = split(b)
    return dot(
        jnp.concatenate([a_high, a_high, a_low], 1),
        jnp.concatenate([b_high, b_low, b_high], 0),
    )


def dot6(a, b):
    ah, am, al = split3(a)
    bh, bm, bl = split3(b)
    return dot(
        jnp.concatenate([ah, ah, am, ah, am, al], 1),
        jnp.concatenate([bh, bm, bh, bl, bm, bh], 0),
    )


def fill_validity(mask_ref, tile_row, out_ref):
    for c in range(out_ref.shape[0] // TILE):
        value = mask_ref[tile_row, c].astype(F32)
        out_ref[c * TILE : (c + 1) * TILE, :] = jnp.full((TILE, out_ref.shape[1]), value, F32)


def gram_kernel(mask_ref, cube_ref, pixel_ref, pair_ref, last_row, valid, seam, pixels, pairs):
    step = pl.program_id(0)
    cols, bands = cube_ref.shape[1:]

    @pl.when(step == 0)
    def _():
        last_row[...] = jnp.zeros_like(last_row)
        valid[...] = jnp.zeros_like(valid)
        pixel_ref[...] = jnp.zeros_like(pixel_ref)
        pair_ref[...] = jnp.zeros_like(pair_ref)

    seam[...] = valid[...]
    fill_validity(mask_ref, step, valid)
    seam[...] = seam[...] * valid[...]
    previous = last_row[...]
    for r in range(ROWS):
        pixel = cube_ref[r] * valid[:, :bands]
        weight = seam if r == 0 else valid
        difference = pixel - previous
        if r == 0:
            difference = difference * seam[:, :bands]
        previous = pixel
        at = slice(r * cols, (r + 1) * cols)
        for value, ones, buffer in ((pixel, valid, pixels), (difference, weight, pairs)):
            high, low = split(jnp.concatenate([value, ones[:, : W - bands]], 1))
            buffer[at, :W] = high
            buffer[at, W:] = low
    last_row[...] = previous
    for ref, buffer in ((pixel_ref, pixels), (pair_ref, pairs)):
        ref[:, : 2 * W] += dot_t(buffer[:, :W], buffer[...])
        ref[:, 2 * W :] += dot_t(buffer[:, W:], buffer[:, W:])


def grams(cube, mask):
    rows, cols, bands = cube.shape
    return pl.pallas_call(
        gram_kernel,
        out_shape=[jax.ShapeDtypeStruct((W, 3 * W), F32)] * 2,
        grid=(rows // ROWS,),
        in_specs=[
            pl.BlockSpec(memory_space=pltpu.SMEM),
            pl.BlockSpec((ROWS, cols, bands), lambda i: (i, 0, 0)),
        ],
        out_specs=[pl.BlockSpec((W, 3 * W), lambda i: (0, 0))] * 2,
        scratch_shapes=[
            pltpu.VMEM((cols, bands), F32),
            pltpu.VMEM((cols, W), F32),
            pltpu.VMEM((cols, W), F32),
            pltpu.VMEM((ROWS * cols, 2 * W), BF16),
            pltpu.VMEM((ROWS * cols, 2 * W), BF16),
        ],
        compiler_params=pltpu.CompilerParams(vmem_limit_bytes=VMEM_LIMIT),
        cost_estimate=pl.CostEstimate(flops=6 * 2 * rows * cols * W * W, bytes_accessed=4 * rows * cols * W, transcendentals=0),
        name="grams",
    )(mask, cube)


def indices(shape):
    return lax.broadcasted_iota(jnp.int32, shape, 0), lax.broadcasted_iota(jnp.int32, shape, 1)


def pack_kernel(core_ref, mask_ref, cube_ref, below_ref, pixel_ref, pair_ref, mine_ref, other_ref, valid, packed):
    bands = cube_ref.shape[2]
    half = bands // 2
    fill_validity(mask_ref, mask_ref.shape[0] - 1, valid)
    weight = valid[...] * jnp.broadcast_to(below_ref[:, bands : bands + 1], valid.shape)
    difference = (below_ref[:, :bands] - cube_ref[0]) * weight[:, :bands]
    high, low = split(jnp.concatenate([difference, weight[:, : W - bands]], 1))
    both = jnp.concatenate([high, low], 1)

    def whole(ref, cross, lows):
        cross = cross + ref[:, : 2 * W]
        mixed = cross[:, W:]
        return cross[:, :W] + mixed + mixed.T + (lows + ref[:, 2 * W :])

    pair = whole(pair_ref, dot_t(high, both), dot_t(low, low))
    pixel = whole(pixel_ref, jnp.zeros((W, 2 * W), F32), jnp.zeros((W, W), F32))
    row, column = indices((W, W))
    out = jnp.where(column <= row, pair, 0.0)
    moved = pltpu.roll(pixel, 1, 1)
    out = jnp.where((column > row) & (column <= bands + 1), moved, out)
    pair_sum = pltpu.roll(pair, 2, 1)
    out = jnp.where(column == bands + 2, pair_sum, out)
    counts = jnp.where(row == 0, pixel[bands : bands + 1, bands : bands + 1], 0.0)
    counts = jnp.where(row == 1, pair[bands : bands + 1, bands : bands + 1], counts)
    out = jnp.where(column == bands + 3, counts, out)
    packed[...] = out
    core = core_ref[0]
    mine_ref[...] = packed[pl.ds(pl.multiple_of(core * half, 8), half), :]
    other_ref[...] = packed[pl.ds(pl.multiple_of((1 - core) * half, 8), half), :]


def pack(core, cube, mask, below, pixel, pair):
    rows, cols, bands = cube.shape
    vmem = lambda a: pl.BlockSpec(a.shape, lambda i: (0,) * a.ndim)
    half = jax.ShapeDtypeStruct((bands // 2, W), F32)
    return pl.pallas_call(
        pack_kernel,
        out_shape=[half, half],
        grid=(1,),
        in_specs=[
            pl.BlockSpec(memory_space=pltpu.SMEM),
            pl.BlockSpec(memory_space=pltpu.SMEM),
            pl.BlockSpec((1, cols, bands), lambda i: (rows - 1, 0, 0)),
            vmem(below),
            vmem(pixel),
            vmem(pair),
        ],
        out_specs=[vmem(half), vmem(half)],
        scratch_shapes=[pltpu.VMEM((cols, W), F32), pltpu.VMEM((W, W), F32)],
        compiler_params=pltpu.CompilerParams(vmem_limit_bytes=VMEM_LIMIT),
        name="pack",
    )(core, mask, cube, below, pixel, pair)


def square_sum(x):
    return jnp.sum(x * x)


def solve_kernel(bands, core_ref, mine_ref, other_ref, gain_ref, mean_ref, left, right):
    half = bands // 2
    core = core_ref[0]
    packed = jnp.concatenate([mine_ref[...], other_ref[...]], 0)
    swapped = jnp.concatenate([other_ref[...], mine_ref[...]], 0)
    packed = jnp.where(core == 0, packed, swapped)
    packed = jnp.concatenate([packed, jnp.zeros((W - bands, W), F32)], 0)
    row, column = indices((W, W))
    on_diagonal = row == column
    inside = (row < bands) & (column < bands)
    pixel_count = packed[0:1, bands + 3 : bands + 4]
    pair_count = packed[1:2, bands + 3 : bands + 4]

    def whole(triangle):
        return triangle + triangle.T - jnp.where(on_diagonal, triangle, 0.0)

    pixel = whole(jnp.where((column >= row) & (column <= bands), pltpu.roll(packed, W - 1, 1), 0.0))
    lower = jnp.where((column <= row) & inside, packed, 0.0)
    sums = jnp.where((column == bands) & (row < bands), pltpu.roll(packed, W - 2, 1), 0.0)
    pair = whole(lower + sums)

    def covariance(square, count):
        total = square[bands : bands + 1, :]
        total_rows = square[:, bands : bands + 1]
        return jnp.where(inside, (square - total_rows * total / count) / (count - 1.0), 0.0)

    signal = covariance(pixel, pixel_count)
    noise = covariance(pair, pair_count)
    combined = signal + noise
    mean_ref[...] = pixel[bands : bands + 1, :] / pixel_count
    diagonal = jnp.where(on_diagonal, combined, 0.0)
    scale_row = lax.rsqrt(jnp.where(column[0:1] < bands, jnp.sum(diagonal, 0, keepdims=True), 1.0))
    scale_column = lax.rsqrt(jnp.where(row[:, 0:1] < bands, jnp.sum(diagonal, 1, keepdims=True), 1.0))
    identity = jnp.where(on_diagonal, 1.0, 0.0)
    matrix = jnp.where(inside, combined * scale_column * scale_row, identity)
    target = noise * scale_column * scale_row

    start = 1.0 / jnp.max(jnp.sum(jnp.abs(matrix), 1, keepdims=True))
    left[:W, :] = start * identity
    left[W:, :] = identity - start * matrix

    def more(carry):
        count, size = carry
        return (count < 24) & (size > 4e-6)

    def squaring(carry):
        count, _ = carry
        new = dot3(left[...], left[W:, :])
        left[:W, :] = left[:W, :] + new[:W]
        left[W:, :] = new[W:]
        return count + 1, square_sum(new[W:])

    lax.while_loop(more, squaring, (0, jnp.float32(1e9)))
    inverse = left[:W, :]
    right[...] = dot3(inverse, target)

    def refining(carry):
        count, _ = carry
        residual = target - dot6(matrix, right[...])
        change = dot3(left[:W, :], residual)
        gain = right[...] + change
        right[...] = gain
        return count + 1, square_sum(change) / square_sum(gain)

    def rough(carry):
        count, size = carry
        return (count < 8) & jnp.logical_not(size <= 1e-6)

    _, size = lax.while_loop(rough, refining, (0, jnp.float32(1e9)))

    @pl.when(jnp.logical_not(size <= 1e-6))
    def _():
        left[:W, :] = matrix
        right[...] = target

        def eliminate(k, _):
            here = row[:, 0:1] == k
            pivot_left = left[pl.ds(k, 1), :]
            pivot_right = right[pl.ds(k, 1), :]
            values = jnp.sum(jnp.where(column == k, left[:W, :], 0.0), 1, keepdims=True)
            pivot = jnp.sum(jnp.where(here, values, 0.0))
            factor = jnp.where(here, (values - 1.0) / pivot, values / pivot)
            left[:W, :] = left[:W, :] - factor * pivot_left
            right[...] = right[...] - factor * pivot_right
            return 0

        lax.fori_loop(0, bands, eliminate, 0)

    gain = right[...] * scale_column * (1.0 / scale_row)
    high, low = split(gain)
    gain_ref[:, :W] = high
    gain_ref[:, W:] = low


def solve(core, mine, other, bands):
    vmem = lambda a: pl.BlockSpec(a.shape, lambda i: (0,) * a.ndim)
    outs = [jax.ShapeDtypeStruct((W, 2 * W), BF16), jax.ShapeDtypeStruct((1, W), F32)]
    return pl.pallas_call(
        functools.partial(solve_kernel, bands),
        out_shape=outs,
        grid=(1,),
        in_specs=[pl.BlockSpec(memory_space=pltpu.SMEM), vmem(mine), vmem(other)],
        out_specs=[vmem(a) for a in outs],
        scratch_shapes=[pltpu.VMEM((2 * W, W), F32), pltpu.VMEM((W, W), F32)],
        compiler_params=pltpu.CompilerParams(vmem_limit_bytes=VMEM_LIMIT),
        name="solve",
    )(core, mine, other)


def filter_kernel(mask_ref, gain_ref, mean_ref, cube_ref, out_ref, valid):
    bands = cube_ref.shape[2]
    fill_validity(mask_ref, pl.program_id(0), valid)
    mean = mean_ref[:, :bands]
    high_gain = gain_ref[:bands, :bands]
    low_gain = gain_ref[:bands, W : W + bands]
    for r in range(ROWS):
        pixel = cube_ref[r]
        high, low = split(pixel - mean)
        shifted = dot(high, high_gain) + dot(high, low_gain) + dot(low, high_gain)
        out_ref[r] = valid[:, :bands] * (pixel - shifted)


def apply_filter(cube, mask, gain, mean):
    rows, cols, bands = cube.shape
    return pl.pallas_call(
        filter_kernel,
        out_shape=jax.ShapeDtypeStruct(cube.shape, F32),
        grid=(rows // ROWS,),
        in_specs=[
            pl.BlockSpec(memory_space=pltpu.SMEM),
            pl.BlockSpec(gain.shape, lambda i: (0, 0)),
            pl.BlockSpec(mean.shape, lambda i: (0, 0)),
            pl.BlockSpec((ROWS, cols, bands), lambda i: (i, 0, 0)),
        ],
        out_specs=pl.BlockSpec((ROWS, cols, bands), lambda i: (i, 0, 0)),
        scratch_shapes=[pltpu.VMEM((cols, W), F32)],
        compiler_params=pltpu.CompilerParams(vmem_limit_bytes=VMEM_LIMIT),
        cost_estimate=pl.CostEstimate(flops=3 * 2 * rows * cols * W * W, bytes_accessed=8 * rows * cols * W, transcendentals=0),
        name="filter",
    )(mask, gain, mean, cube)


def ring(x, axis, length, stride, by):
    pairs = []
    for i in range(lax.axis_size(axis)):
        place = i // stride % length
        pairs.append((i, i + ((place + by) % length - place) * stride))
    return lax.ppermute(x, axis, pairs)


def ring_sum(x, axis, length, stride):
    return x + ring(x, axis, length, stride, 1) + ring(x, axis, length, stride, 2) + ring(x, axis, length, stride, 3)


def per_device(cube, mask):
    bands = cube.shape[2]
    size = lax.axis_size("track")
    first = jnp.repeat(mask[0].astype(F32), TILE)[:, None]
    row = jnp.concatenate([cube[0], first], 1)
    below = lax.ppermute(row, "track", [(i, i - 1) for i in range(1, size)])
    core = (lax.axis_index("strip") % 2).astype(jnp.int32)[None]
    pixel, pair = grams(cube, mask)
    mine, other = pack(core, cube, mask, below, pixel, pair)
    total = mine + ring(other, "strip", 2, 1, 1)
    total = ring_sum(total, "strip", 4, 2)
    total = ring_sum(total, "track", 4, 4)
    total = ring_sum(total, "track", 4, 1)
    gain, mean = solve(core, total, ring(total, "strip", 2, 1, 1), bands)
    return apply_filter(cube, mask, gain, mean)


def solution(mesh):
    return jax.shard_map(
        per_device,
        mesh=mesh,
        in_specs=(P("track", "strip", None), P("track", "strip")),
        out_specs=P("track", "strip", None),
        check_vma=False,
    )
```

profile of v0, /device:TPU:1, one launch (start us, length us, event | category | flops | bytes accessed | tf_op | source)
XLA Modules:
  0.0 79.0 jit_solution(8026815814067640481)
XLA Ops:
  0.0 0.7 convert_bitcast_fusion
  0.7 0.1 broadcast_in_dim.7
  0.8 0.1 broadcast_in_dim_reshape.4
  0.9 1.0 %slice_bitcast_fusion = f32[320,224]{1,0:T(8,128)S(1)} fusion(f32[32,320,224]{2,1,0:T(8,128)} %cube_ref.5), kind=kLoop, calls=%fused_computation.1 | loop fusion | bytes 573440 | tf_op jit(solution)/shard_map/squeeze | solution.py:339
  1.9 0.1 pad_maximum_fusion
  2.0 1.3 %collective-permute-start = (f32[320,225]{1,0:T(8,128)S(1)}, f32[320,225]{1,0:T(8,128)S(1)}, u32[]{:S(2)}, u32[]{:S(2)}) collective-permute-start(f32[320,225]{1,0:T(8,128)S(1)} %pad_maximum_fusion), channel_id=1, source_target_pairs={{8,0},{16,8},{24,16},{32,24},{40,32},{48,40},{56,48},{64,56},{72,6... | collective-permute-start | bytes 864008 | tf_op jit(solution)/shard_map/ppermute | solution.py:340
  3.3 0.7 copy-done
  4.0 14.3 %grams.1 = (f32[256,768]{1,0:T(8,128)S(1)}, f32[256,768]{1,0:T(8,128)S(1)}) custom-call(s32[4,40]{1,0:T(4,128)S(1)} %copy-done, f32[32,320,224]{2,1,0:T(8,128)} %cube_ref.5), custom_call_target="tpu_custom_call" | custom-call | flops 8053063680 | bytes 10485760 | tf_op jit(solution)/shard_map/grams/pallas_call | solution.py:97
  18.3 1.8 %pack.1 = (f32[112,256]{1,0:T(8,128)S(1)}, f32[112,256]{1,0:T(8,128)S(1)}) custom-call(s32[1]{0:T(128)} %bitcast.core_ref, s32[4,40]{1,0:T(4,128)S(1)} %copy-done.1, f32[32,320,224]{2,1,0:T(8,128)} %cube_ref.5, f32[320,225]{1,0:T(8,128)S(1)} %collective-permute-done.below_ref, f32[256,768]{1,0:T(8,128)S(1)} %get-tuple-element.11.pixel_ref, ...), custom_call_target="tpu_custom_call" | custom-call | tf_op jit(solution)/shard_map/pack/pallas_call | solution.py:158
  20.1 1.5 %collective-permute-start.1 = (f32[112,256]{1,0:T(8,128)S(1)}, f32[112,256]{1,0:T(8,128)S(1)}, u32[]{:S(2)}, u32[]{:S(2)}) collective-permute-start(f32[112,256]{1,0:T(8,128)S(1)} %get-tuple-element.14), channel_id=1, source_target_pairs={{0,1},{1,0},{2,3},{3,2},{4,5},{5,4},{6,7},{7,6},{8,9},{9,8},{10,11... | collective-permute-start | bytes 344072 | tf_op jit(solution)/shard_map/ppermute | solution.py:328
  21.6 1.0 %collective-permute-done.1 = f32[112,256]{1,0:T(8,128)S(1)} collective-permute-done((f32[112,256]{1,0:T(8,128)S(1)}, f32[112,256]{1,0:T(8,128)S(1)}, u32[]{:S(2)}, u32[]{:S(2)}) %collective-permute-start.1) | collective-permute-done | bytes 114720 | tf_op jit(solution)/shard_map/ppermute | solution.py:328
  22.6 2.6 %collective-permute-start.4 = (f32[112,256]{1,0:T(8,128)S(1)}, f32[112,256]{1,0:T(8,128)S(1)}, u32[]{:S(2)}, u32[]{:S(2)}) collective-permute-start(f32[112,256]{1,0:T(8,128)S(1)} %add.35), channel_id=1, source_target_pairs={{0,6},{1,7},{2,0},{3,1},{4,2},{5,3},{6,4},{7,5},{8,14},{9,15},{10,... | collective-permute-start | bytes 344072 | tf_op jit(solution)/shard_map/ppermute | solution.py:328
  25.2 0.5 collective-permute-start.3
  25.7 0.6 collective-permute-start.2
  26.3 3.4 %collective-permute-done.4 = f32[112,256]{1,0:T(8,128)S(1)} collective-permute-done((f32[112,256]{1,0:T(8,128)S(1)}, f32[112,256]{1,0:T(8,128)S(1)}, u32[]{:S(2)}, u32[]{:S(2)}) %collective-permute-start.4) | collective-permute-done | bytes 114720 | tf_op jit(solution)/shard_map/ppermute | solution.py:328
  29.7 1.1 %collective-permute-done.3 = f32[112,256]{1,0:T(8,128)S(1)} collective-permute-done((f32[112,256]{1,0:T(8,128)S(1)}, f32[112,256]{1,0:T(8,128)S(1)}, u32[]{:S(2)}, u32[]{:S(2)}) %collective-permute-start.3) | collective-permute-done | bytes 114720 | tf_op jit(solution)/shard_map/ppermute | solution.py:328
  30.8 3.4 %collective-permute-done.2 = f32[112,256]{1,0:T(8,128)S(1)} collective-permute-done((f32[112,256]{1,0:T(8,128)S(1)}, f32[112,256]{1,0:T(8,128)S(1)}, u32[]{:S(2)}, u32[]{:S(2)}) %collective-permute-start.2) | collective-permute-done | bytes 114720 | tf_op jit(solution)/shard_map/ppermute | solution.py:328
  34.3 7.6 %collective-permute-start.7 = (f32[112,256]{1,0:T(8,128)S(1)}, f32[112,256]{1,0:T(8,128)S(1)}, u32[]{:S(2)}, u32[]{:S(2)}) collective-permute-start(f32[112,256]{1,0:T(8,128)S(1)} %add_add_fusion.2), channel_id=1, source_target_pairs={{0,96},{8,104},{16,112},{24,120},{32,0},{40,8},{48,16},{56,24},{64... | collective-permute-start | bytes 344072 | tf_op jit(solution)/shard_map/ppermute | solution.py:328
  41.9 0.1 collective-permute-start.6
  41.9 0.7 collective-permute-start.5
  42.6 4.0 %collective-permute-done.7 = f32[112,256]{1,0:T(8,128)S(1)} collective-permute-done((f32[112,256]{1,0:T(8,128)S(1)}, f32[112,256]{1,0:T(8,128)S(1)}, u32[]{:S(2)}, u32[]{:S(2)}) %collective-permute-start.7) | collective-permute-done | bytes 114720 | tf_op jit(solution)/shard_map/ppermute | solution.py:328
  46.6 0.5 collective-permute-done.6
  47.1 3.3 %collective-permute-done.5 = f32[112,256]{1,0:T(8,128)S(1)} collective-permute-done((f32[112,256]{1,0:T(8,128)S(1)}, f32[112,256]{1,0:T(8,128)S(1)}, u32[]{:S(2)}, u32[]{:S(2)}) %collective-permute-start.5) | collective-permute-done | bytes 114720 | tf_op jit(solution)/shard_map/ppermute | solution.py:328
  50.5 0.4 collective-permute-start.10
  50.9 1.2 %collective-permute-start.8 = (f32[112,256]{1,0:T(8,128)S(1)}, f32[112,256]{1,0:T(8,128)S(1)}, u32[]{:S(2)}, u32[]{:S(2)}) collective-permute-start(f32[112,256]{1,0:T(8,128)S(1)} %add_add_fusion.1), channel_id=1, source_target_pairs={{0,8},{8,16},{16,24},{24,0},{32,40},{40,48},{48,56},{56,32},{64,72... | collective-permute-start | bytes 344072 | tf_op jit(solution)/shard_map/ppermute | solution.py:328
  52.0 2.5 %collective-permute-done.10 = f32[112,256]{1,0:T(8,128)S(1)} collective-permute-done((f32[112,256]{1,0:T(8,128)S(1)}, f32[112,256]{1,0:T(8,128)S(1)}, u32[]{:S(2)}, u32[]{:S(2)}) %collective-permute-start.10) | collective-permute-done | bytes 114720 | tf_op jit(solution)/shard_map/ppermute | solution.py:328
  54.5 1.6 %collective-permute-done.9 = f32[112,256]{1,0:T(8,128)S(1)} collective-permute-done((f32[112,256]{1,0:T(8,128)S(1)}, f32[112,256]{1,0:T(8,128)S(1)}, u32[]{:S(2)}, u32[]{:S(2)}) %collective-permute-start.9) | collective-permute-done | bytes 114720 | tf_op jit(solution)/shard_map/ppermute | solution.py:328
  56.1 3.6 %collective-permute-done.8 = f32[112,256]{1,0:T(8,128)S(1)} collective-permute-done((f32[112,256]{1,0:T(8,128)S(1)}, f32[112,256]{1,0:T(8,128)S(1)}, u32[]{:S(2)}, u32[]{:S(2)}) %collective-permute-start.8) | collective-permute-done | bytes 114720 | tf_op jit(solution)/shard_map/ppermute | solution.py:328
  59.7 0.8 collective-permute-start.11
  60.5 1.0 %collective-permute-done.11.other_ref = f32[112,256]{1,0:T(8,128)S(1)} collective-permute-done((f32[112,256]{1,0:T(8,128)S(1)}, f32[112,256]{1,0:T(8,128)S(1)}, u32[]{:S(2)}, u32[]{:S(2)}) %collective-permute-start.11) | collective-permute-done | bytes 114720 | tf_op jit(solution)/shard_map/ppermute | solution.py:328
  61.5 6.7 %solve.1 = (bf16[256,512]{1,0:T(8,128)(2,1)S(1)}, f32[1,256]{1,0:T(1,128)S(1)}) custom-call(s32[1]{0:T(128)} %bitcast.core_ref, f32[112,256]{1,0:T(8,128)S(1)} %add_add_fusion.mine_ref, f32[112,256]{1,0:T(8,128)S(1)} %collective-permute-done.11.other_ref), custom_call_target="tpu_custom_call" | custom-call | tf_op jit(solution)/shard_map/solve/pallas_call | solution.py:278
  68.2 10.8 %filter.1 = f32[32,320,224]{2,1,0:T(8,128)} custom-call(s32[4,40]{1,0:T(4,128)S(1)} %copy-done.1, bf16[256,512]{1,0:T(8,128)(2,1)S(1)} %get-tuple-element.15.gain_ref, f32[1,256]{1,0:T(1,128)S(1)} %get-tuple-element.16.mean_ref, f32[32,320,224]{2,1,0:T(8,128)} %cube_ref.5), custom_call_target="tpu_custom_call" | custom-call | flops 4026531840 | bytes 20971520 | tf_op jit(solution)/shard_map/filter/pallas_call | solution.py:305
  (9 shorter events, 0.1 us)
Async XLA Ops:
  2.0 16.3 %collective-permute-start = (f32[320,225]{1,0:T(8,128)S(1)}, f32[320,225]{1,0:T(8,128)S(1)}, u32[]{:S(2)}, u32[]{:S(2)}) collective-permute-start(f32[320,225]{1,0:T(8,128)S(1)} %pad_maximum_fusion), channel_id=1, source_target_pairs={{8,0},{16,8},{24,16},{32,24},{40,32},{48,40},{56,48},{64,56},{72,6... | collective-permute-start | bytes 864008 | tf_op jit(solution)/shard_map/ppermute | solution.py:340
  3.3 0.7 copy-start
  4.0 14.3 %copy-start.1 = (s32[4,40]{1,0:T(4,128)S(1)}, s32[4,40]{1,0:T(4,128)}, u32[]{:S(2)}) copy-start(s32[4,40]{1,0:T(4,128)} %mask_ref.5) | copy-start | bytes 1924
  20.1 2.5 %collective-permute-start.1 = (f32[112,256]{1,0:T(8,128)S(1)}, f32[112,256]{1,0:T(8,128)S(1)}, u32[]{:S(2)}, u32[]{:S(2)}) collective-permute-start(f32[112,256]{1,0:T(8,128)S(1)} %get-tuple-element.14), channel_id=1, source_target_pairs={{0,1},{1,0},{2,3},{3,2},{4,5},{5,4},{6,7},{7,6},{8,9},{9,8},{10,11... | collective-permute-start | bytes 344072 | tf_op jit(solution)/shard_map/ppermute | solution.py:328
  22.6 7.1 %collective-permute-start.4 = (f32[112,256]{1,0:T(8,128)S(1)}, f32[112,256]{1,0:T(8,128)S(1)}, u32[]{:S(2)}, u32[]{:S(2)}) collective-permute-start(f32[112,256]{1,0:T(8,128)S(1)} %add.35), channel_id=1, source_target_pairs={{0,6},{1,7},{2,0},{3,1},{4,2},{5,3},{6,4},{7,5},{8,14},{9,15},{10,... | collective-permute-start | bytes 344072 | tf_op jit(solution)/shard_map/ppermute | solution.py:328
  25.2 5.6 %collective-permute-start.3 = (f32[112,256]{1,0:T(8,128)S(1)}, f32[112,256]{1,0:T(8,128)S(1)}, u32[]{:S(2)}, u32[]{:S(2)}) collective-permute-start(f32[112,256]{1,0:T(8,128)S(1)} %add.35), channel_id=1, source_target_pairs={{0,4},{1,5},{2,6},{3,7},{4,0},{5,1},{6,2},{7,3},{8,12},{9,13},{10,... | collective-permute-start | bytes 344072 | tf_op jit(solution)/shard_map/ppermute | solution.py:328
  25.7 8.5 %collective-permute-start.2 = (f32[112,256]{1,0:T(8,128)S(1)}, f32[112,256]{1,0:T(8,128)S(1)}, u32[]{:S(2)}, u32[]{:S(2)}) collective-permute-start(f32[112,256]{1,0:T(8,128)S(1)} %add.35), channel_id=1, source_target_pairs={{0,2},{1,3},{2,4},{3,5},{4,6},{5,7},{6,0},{7,1},{8,10},{9,11},{10,... | collective-permute-start | bytes 344072 | tf_op jit(solution)/shard_map/ppermute | solution.py:328
  34.3 12.3 %collective-permute-start.7 = (f32[112,256]{1,0:T(8,128)S(1)}, f32[112,256]{1,0:T(8,128)S(1)}, u32[]{:S(2)}, u32[]{:S(2)}) collective-permute-start(f32[112,256]{1,0:T(8,128)S(1)} %add_add_fusion.2), channel_id=1, source_target_pairs={{0,96},{8,104},{16,112},{24,120},{32,0},{40,8},{48,16},{56,24},{64... | collective-permute-start | bytes 344072 | tf_op jit(solution)/shard_map/ppermute | solution.py:328
  41.9 5.3 %collective-permute-start.6 = (f32[112,256]{1,0:T(8,128)S(1)}, f32[112,256]{1,0:T(8,128)S(1)}, u32[]{:S(2)}, u32[]{:S(2)}) collective-permute-start(f32[112,256]{1,0:T(8,128)S(1)} %add_add_fusion.2), channel_id=1, source_target_pairs={{0,64},{8,72},{16,80},{24,88},{32,96},{40,104},{48,112},{56,120},{... | collective-permute-start | bytes 344072 | tf_op jit(solution)/shard_map/ppermute | solution.py:328
  41.9 8.5 %collective-permute-start.5 = (f32[112,256]{1,0:T(8,128)S(1)}, f32[112,256]{1,0:T(8,128)S(1)}, u32[]{:S(2)}, u32[]{:S(2)}) collective-permute-start(f32[112,256]{1,0:T(8,128)S(1)} %add_add_fusion.2), channel_id=1, source_target_pairs={{0,32},{8,40},{16,48},{24,56},{32,64},{40,72},{48,80},{56,88},{64,... | collective-permute-start | bytes 344072 | tf_op jit(solution)/shard_map/ppermute | solution.py:328
  50.5 4.0 %collective-permute-start.10 = (f32[112,256]{1,0:T(8,128)S(1)}, f32[112,256]{1,0:T(8,128)S(1)}, u32[]{:S(2)}, u32[]{:S(2)}) collective-permute-start(f32[112,256]{1,0:T(8,128)S(1)} %add_add_fusion.1), channel_id=1, source_target_pairs={{0,24},{8,0},{16,8},{24,16},{32,56},{40,32},{48,40},{56,48},{64,88... | collective-permute-start | bytes 344072 | tf_op jit(solution)/shard_map/ppermute | solution.py:328
  50.9 5.2 %collective-permute-start.9 = (f32[112,256]{1,0:T(8,128)S(1)}, f32[112,256]{1,0:T(8,128)S(1)}, u32[]{:S(2)}, u32[]{:S(2)}) collective-permute-start(f32[112,256]{1,0:T(8,128)S(1)} %add_add_fusion.1), channel_id=1, source_target_pairs={{0,16},{8,24},{16,0},{24,8},{32,48},{40,56},{48,32},{56,40},{64,80... | collective-permute-start | bytes 344072 | tf_op jit(solution)/shard_map/ppermute | solution.py:328
  50.9 8.8 %collective-permute-start.8 = (f32[112,256]{1,0:T(8,128)S(1)}, f32[112,256]{1,0:T(8,128)S(1)}, u32[]{:S(2)}, u32[]{:S(2)}) collective-permute-start(f32[112,256]{1,0:T(8,128)S(1)} %add_add_fusion.1), channel_id=1, source_target_pairs={{0,8},{8,16},{16,24},{24,0},{32,40},{40,48},{48,56},{56,32},{64,72... | collective-permute-start | bytes 344072 | tf_op jit(solution)/shard_map/ppermute | solution.py:328
  59.7 1.8 %collective-permute-start.11 = (f32[112,256]{1,0:T(8,128)S(1)}, f32[112,256]{1,0:T(8,128)S(1)}, u32[]{:S(2)}, u32[]{:S(2)}) collective-permute-start(f32[112,256]{1,0:T(8,128)S(1)} %add_add_fusion.mine_ref), channel_id=1, source_target_pairs={{0,1},{1,0},{2,3},{3,2},{4,5},{5,4},{6,7},{7,6},{8,9},{9,8},{10,11... | collective-permute-start | bytes 344072 | tf_op jit(solution)/shard_map/ppermute | solution.py:328
where the time goes:
time: 79.3 us; the launch traced here: 79 us
  Pallas kernels  33.6 us (42%)
  waiting for transfers between devices  25.3 us (32%)
  starting transfers between devices  17.3 us (22%)
  local copies, waits for them, and re-layouts  1.85 us (2%)
  other arithmetic  0.9 us (1%)
    ppermute x11, waiting for transfers between devices, ring(): return lax.ppermute(x, axis, pairs)  25.3 us
    ppermute x11, starting transfers between devices, ring(): return lax.ppermute(x, axis, pairs)  16 us
    pallas_call x1, Pallas kernels, grams(): pl.pallas_call(gram_kernel, out_shape=[jax.ShapeDtypeStruct((W, 3 * W), F...  14.3 us
    pallas_call x1, Pallas kernels, apply_filter(): pl.pallas_call(filter_kernel, out_shape=jax.ShapeDtypeStruct(cube.shape,...  10.8 us
    pallas_call x1, Pallas kernels, solve(): pl.pallas_call(functools.partial(solve_kernel, bands), out_shape=outs, gr...  6.72 us
    pallas_call x1, Pallas kernels, pack(): pl.pallas_call(pack_kernel, out_shape=[half, half], grid=(1,), in_specs=[...  1.79 us
  transfers between devices with their start and end apart: 12, of which 11 were waited for; matrix products, arithmetic and copies ran while one was open for 0% of the time, Pallas kernels for 18%

commit v1 on v0

v1 whole, which is shorter than its diff:
```python
import functools

import jax
import jax.numpy as jnp
from jax import lax
from jax.experimental import pallas as pl
from jax.experimental.pallas import tpu as pltpu
from jax.sharding import PartitionSpec as P

TILE = 8
W = 256
F32 = jnp.float32
BF16 = jnp.bfloat16
MIB = 2**20


def split(x):
    high = x.astype(BF16)
    return high, (x - high.astype(F32)).astype(BF16)


def split3(x):
    high = x.astype(BF16)
    rest = x - high.astype(F32)
    middle = rest.astype(BF16)
    return high, middle, (rest - middle.astype(F32)).astype(BF16)


def dot(a, b):
    return lax.dot_general(a, b, (((1,), (0,)), ((), ())), preferred_element_type=F32)


def dot_t(a, b):
    return lax.dot_general(a, b, (((0,), (0,)), ((), ())), preferred_element_type=F32)


def dot3(a, b):
    a_high, a_low = split(a)
    b_high, b_low = split(b)
    return dot(
        jnp.concatenate([a_high, a_high, a_low], 1),
        jnp.concatenate([b_high, b_low, b_high], 0),
    )


def dot6(a, b):
    ah, am, al = split3(a)
    bh, bm, bl = split3(b)
    return dot(
        jnp.concatenate([ah, ah, am, ah, am, al], 1),
        jnp.concatenate([bh, bm, bh, bl, bm, bh], 0),
    )


def in_vmem():
    return pl.BlockSpec(memory_space=pltpu.VMEM)


def in_hbm():
    return pl.BlockSpec(memory_space=pltpu.HBM)


def params(mib):
    return pltpu.CompilerParams(vmem_limit_bytes=mib * MIB)


def fill_validity(mask_ref, tile_row, out_ref):
    for c in range(out_ref.shape[0] // TILE):
        value = mask_ref[tile_row, c].astype(F32)
        out_ref[c * TILE : (c + 1) * TILE, :] = jnp.full((TILE, out_ref.shape[1]), value, F32)


def first_row_kernel(mask_hbm, cube_hbm, out_ref, mask, row, sems):
    bands = row.shape[2]
    copies = [
        pltpu.make_async_copy(mask_hbm, mask, sems.at[0]),
        pltpu.make_async_copy(cube_hbm.at[pl.ds(0, 1)], row, sems.at[1]),
    ]
    for copy in copies:
        copy.start()
    for copy in copies:
        copy.wait()
    fill_validity(mask, 0, out_ref)
    out_ref[:, :bands] = row[0]


def first_row(mask, cube):
    _, cols, bands = cube.shape
    return pl.pallas_call(
        first_row_kernel,
        out_shape=pltpu.VMEM((cols, W), F32),
        in_specs=[in_hbm(), in_hbm()],
        out_specs=in_vmem(),
        scratch_shapes=[
            pltpu.SMEM(mask.shape, jnp.int32),
            pltpu.VMEM((1, cols, bands), F32),
            pltpu.SemaphoreType.DMA((2,)),
        ],
        compiler_params=params(46),
        name="first_row",
    )(mask, cube)


GROUP = 4


def moments_kernel(
    mask_hbm, cube_hbm, halves_ref, valid_ref, last_ref, pixel_ref, pair_ref, rest_ref, mask, raw, seam, pairs_a, pairs_b, sems
):
    rows, cols, bands = raw.shape
    groups = rows // GROUP

    def fetch(g):
        at = pl.ds(g * GROUP, GROUP)
        return pltpu.make_async_copy(cube_hbm.at[at], raw.at[at], sems.at[g])

    mask_copy = pltpu.make_async_copy(mask_hbm, mask, sems.at[groups])
    mask_copy.start()
    for g in range(groups):
        fetch(g).start()
    pixel_ref[...] = jnp.zeros_like(pixel_ref)
    pair_ref[...] = jnp.zeros_like(pair_ref)
    for buffer in (halves_ref, pairs_a, pairs_b):
        count = buffer.shape[0]
        buffer[:, bands:W] = jnp.ones((count, W - bands), BF16)
        buffer[:, W + bands :] = jnp.zeros((count, W - bands), BF16)
    mask_copy.wait()

    def put(value, buffer, r, squares):
        high = value.astype(BF16)
        rest = value - high.astype(F32)
        buffer[r * cols : (r + 1) * cols, :bands] = high
        buffer[r * cols : (r + 1) * cols, W : W + bands] = rest.astype(BF16)
        return squares + jnp.sum((rest * rest).reshape(cols // 8, 8, bands), 0)

    def products(halves, pairs):
        pixel_ref[...] += dot_t(halves[:, :W], halves[...])
        pair_ref[...] += dot_t(pairs[:, :W], pairs[...])

    squares = [jnp.zeros((8, bands), F32)] * 2
    previous = None
    pending = None
    for g in range(groups):
        pairs = (pairs_a, pairs_b)[g % 2]
        halves = halves_ref.at[pl.ds(g * GROUP * cols, GROUP * cols)]
        if pending is not None:
            products(*pending)
        fetch(g).wait()
        for r in range(GROUP):
            row = g * GROUP + r
            valid = valid_ref.at[row // TILE]
            if row % TILE == 0:
                fill_validity(mask, row // TILE, valid)
                if row:
                    seam[...] = valid_ref[row // TILE - 1] * valid[...]
            pixel = raw[row] * valid[:, :bands]
            if row == 0:
                difference = jnp.zeros_like(pixel)
            elif row % TILE == 0:
                difference = (pixel - previous) * seam[:, :bands]
            else:
                difference = pixel - previous
            previous = pixel
            squares[0] = put(pixel, halves, r, squares[0])
            squares[1] = put(difference, pairs, r, squares[1])
        pending = (halves, pairs)
    products(*pending)
    last_ref[...] = previous
    for k in range(2):
        rest_ref[k, :, :bands] = squares[k]
        rest_ref[k, :, bands:] = jnp.zeros((8, W - bands), F32)


def moments(mask, cube):
    rows, cols, bands = cube.shape
    pixels = rows * cols
    return pl.pallas_call(
        moments_kernel,
        out_shape=[
            pltpu.VMEM((pixels, 2 * W), BF16),
            pltpu.VMEM((rows // TILE, cols, W), F32),
            pltpu.VMEM((cols, bands), F32),
            pltpu.VMEM((W, 2 * W), F32),
            pltpu.VMEM((W, 2 * W), F32),
            pltpu.VMEM((2, 8, W), F32),
        ],
        in_specs=[in_hbm(), in_hbm()],
        out_specs=[in_vmem()] * 6,
        scratch_shapes=[
            pltpu.SMEM(mask.shape, jnp.int32),
            pltpu.VMEM(cube.shape, F32),
            pltpu.VMEM((cols, W), F32),
            pltpu.VMEM((GROUP * cols, 2 * W), BF16),
            pltpu.VMEM((GROUP * cols, 2 * W), BF16),
            pltpu.SemaphoreType.DMA((rows // GROUP + 1,)),
        ],
        compiler_params=params(40),
        cost_estimate=pl.CostEstimate(flops=4 * 2 * pixels * W * W, bytes_accessed=4 * pixels * W, transcendentals=0),
        name="moments",
    )(mask, cube)


def indices(shape):
    return lax.broadcasted_iota(jnp.int32, shape, 0), lax.broadcasted_iota(jnp.int32, shape, 1)


def pack_kernel(
    core_ref, valid_ref, last_ref, below_ref, pixel_ref, pair_ref, rest_ref, mine_ref, other_ref, packed, buffer
):
    bands = last_ref.shape[1]
    half = bands // 2
    row, column = indices((W, W))
    on_diagonal = row == column
    last_valid = valid_ref[valid_ref.shape[0] - 1]
    weight = last_valid * jnp.broadcast_to(below_ref[:, bands : bands + 1], last_valid.shape)
    difference = (below_ref[:, :bands] - last_ref[...]) * weight[:, :bands]
    high, low = split(difference)
    rest = difference - high.astype(F32)
    buffer[:, bands:W] = jnp.ones((buffer.shape[0], W - bands), BF16)
    buffer[:, W + bands :] = jnp.zeros((buffer.shape[0], W - bands), BF16)
    buffer[:, :bands] = high
    buffer[:, W : W + bands] = low
    pairs = pair_ref[...] + dot_t(buffer[:, :W], buffer[...])
    squares = jnp.sum(rest * rest, 0, keepdims=True)

    def whole(parts, squares):
        mixed = parts[:, W:]
        squares = jnp.concatenate([squares, jnp.zeros((1, W - bands), F32)], 1)
        return parts[:, :W] + mixed + mixed.T + jnp.where(on_diagonal, squares, 0.0)

    pixel = whole(pixel_ref[...], jnp.sum(rest_ref[0, :, :bands], 0, keepdims=True))
    pair = whole(pairs, squares + jnp.sum(rest_ref[1, :, :bands], 0, keepdims=True))
    valid = valid_ref[:, :, :128]
    inner = jnp.sum(valid, 0)
    seams = jnp.sum(valid[1:] * valid[:-1], 0)
    pixel_count = TILE * jnp.sum(inner, 0, keepdims=True)
    pair_count = jnp.sum((TILE - 1) * inner + seams + weight[:, :128], 0, keepdims=True)
    out = jnp.where(column <= row, pair, 0.0)
    out = jnp.where((column > row) & (column <= bands + 1), pltpu.roll(pixel, 1, 1), out)
    out = jnp.where(column == bands + 2, pltpu.roll(pair, 2, 1), out)
    counts = jnp.where(row == 0, pixel_count[:, :1], 0.0)
    counts = jnp.where(row == 1, pair_count[:, :1], counts)
    packed[...] = jnp.where(column == bands + 3, counts, out)
    core = core_ref[0]
    mine_ref[...] = packed[pl.ds(pl.multiple_of(core * half, 8), half), :]
    other_ref[...] = packed[pl.ds(pl.multiple_of((1 - core) * half, 8), half), :]


def pack(core, valid, last, below, pixel, pair, rest):
    cols, bands = last.shape
    half = pltpu.VMEM((bands // 2, W), F32)
    return pl.pallas_call(
        pack_kernel,
        out_shape=[half, half],
        in_specs=[pl.BlockSpec(memory_space=pltpu.SMEM)] + [in_vmem()] * 6,
        out_specs=[in_vmem()] * 2,
        scratch_shapes=[pltpu.VMEM((W, W), F32), pltpu.VMEM((cols, 2 * W), BF16)],
        compiler_params=params(12),
        name="pack",
    )(core, valid, last, below, pixel, pair, rest)


def square_sum(x):
    return jnp.sum(x * x)


def solve_kernel(bands, core_ref, mine_ref, other_ref, weights_ref, left, right):
    core = core_ref[0]
    packed = jnp.concatenate([mine_ref[...], other_ref[...]], 0)
    swapped = jnp.concatenate([other_ref[...], mine_ref[...]], 0)
    packed = jnp.where(core == 0, packed, swapped)
    packed = jnp.concatenate([packed, jnp.zeros((W - bands, W), F32)], 0)
    row, column = indices((W, W))
    on_diagonal = row == column
    inside = (row < bands) & (column < bands)
    pixel_count = packed[0:1, bands + 3 : bands + 4]
    pair_count = packed[1:2, bands + 3 : bands + 4]

    def whole(triangle):
        return triangle + triangle.T - jnp.where(on_diagonal, triangle, 0.0)

    pixel = whole(jnp.where((column >= row) & (column <= bands), pltpu.roll(packed, W - 1, 1), 0.0))
    lower = jnp.where((column <= row) & inside, packed, 0.0)
    sums = jnp.where((column == bands) & (row < bands), pltpu.roll(packed, W - 2, 1), 0.0)
    pair = whole(lower + sums)

    def covariance(square, count):
        total = square[bands : bands + 1, :]
        total_rows = square[:, bands : bands + 1]
        return jnp.where(inside, (square - total_rows * total / count) / (count - 1.0), 0.0)

    signal = covariance(pixel, pixel_count)
    noise = covariance(pair, pair_count)
    combined = signal + noise
    mean = pixel[:, bands : bands + 1] / pixel_count
    diagonal = jnp.where(on_diagonal, combined, 0.0)
    scale_row = lax.rsqrt(jnp.where(column[0:1] < bands, jnp.sum(diagonal, 0, keepdims=True), 1.0))
    scale_column = lax.rsqrt(jnp.where(row[:, 0:1] < bands, jnp.sum(diagonal, 1, keepdims=True), 1.0))
    identity = jnp.where(on_diagonal, 1.0, 0.0)
    matrix = jnp.where(inside, combined * scale_column * scale_row, identity)
    target = noise * scale_column * scale_row

    start = 1.0 / jnp.max(jnp.sum(jnp.abs(matrix), 1, keepdims=True))
    left[:W, :] = start * identity
    left[W:, :] = identity - start * matrix

    def more(carry):
        count, size = carry
        return (count < 24) & (size > 4e-6)

    def squaring(carry):
        count, _ = carry
        new = dot3(left[...], left[W:, :])
        left[:W, :] = left[:W, :] + new[:W]
        left[W:, :] = new[W:]
        return count + 1, square_sum(new[W:])

    lax.while_loop(more, squaring, (0, jnp.float32(1e9)))
    right[...] = dot3(left[:W, :], target)

    def refining(carry):
        count, _ = carry
        residual = target - dot6(matrix, right[...])
        change = dot3(left[:W, :], residual)
        gain = right[...] + change
        right[...] = gain
        return count + 1, square_sum(change) / square_sum(gain)

    def rough(carry):
        count, size = carry
        return (count < 8) & jnp.logical_not(size <= 1e-6)

    _, size = lax.while_loop(rough, refining, (0, jnp.float32(1e9)))

    @pl.when(jnp.logical_not(size <= 1e-6))
    def _():
        left[:W, :] = matrix
        right[...] = target

        def eliminate(k, _):
            here = row[:, 0:1] == k
            pivot_left = left[pl.ds(k, 1), :]
            pivot_right = right[pl.ds(k, 1), :]
            values = jnp.sum(jnp.where(column == k, left[:W, :], 0.0), 1, keepdims=True)
            pivot = jnp.sum(jnp.where(here, values, 0.0))
            factor = jnp.where(here, (values - 1.0) / pivot, values / pivot)
            left[:W, :] = left[:W, :] - factor * pivot_left
            right[...] = right[...] - factor * pivot_right
            return 0

        lax.fori_loop(0, bands, eliminate, 0)

    gain = right[...] * scale_column * (1.0 / scale_row)
    shift = jnp.sum(jnp.where(row < bands, mean, 0.0) * gain, 0, keepdims=True)
    weights = jnp.where(row == bands, shift, jnp.where(inside, identity - gain, 0.0))
    high, low = split(weights)
    weights_ref[:W, :] = high
    weights_ref[W : 2 * W, :] = high
    weights_ref[2 * W :, :] = low


def solve(core, mine, other, bands):
    return pl.pallas_call(
        functools.partial(solve_kernel, bands),
        out_shape=pltpu.VMEM((3 * W, W), BF16),
        in_specs=[pl.BlockSpec(memory_space=pltpu.SMEM), in_vmem(), in_vmem()],
        out_specs=in_vmem(),
        scratch_shapes=[pltpu.VMEM((2 * W, W), F32), pltpu.VMEM((W, W), F32)],
        compiler_params=params(16),
        name="solve",
    )(core, mine, other)


def filter_kernel(halves_ref, valid_ref, weights_ref, out_hbm, staged, sems):
    slots, group, cols, bands = staged.shape
    groups = out_hbm.shape[0] // group

    def send(g):
        return pltpu.make_async_copy(staged.at[g % slots], out_hbm.at[pl.ds(g * group, group)], sems.at[g % slots])

    for g in range(groups):
        if g >= slots:
            send(g - slots).wait()
        halves = halves_ref[g * group * cols : (g + 1) * group * cols, :]
        result = dot(jnp.concatenate([halves, halves[:, :W]], 1), weights_ref[...])
        valid = valid_ref[g * group // TILE]
        for r in range(group):
            staged[g % slots, r] = valid[:, :bands] * result[r * cols : (r + 1) * cols, :bands]
        send(g).start()
    for g in range(groups - slots, groups):
        send(g).wait()


def apply_filter(halves, valid, weights, shape):
    rows, cols, bands = shape
    group, slots = 4, 4
    pixels = rows * cols
    return pl.pallas_call(
        filter_kernel,
        out_shape=jax.ShapeDtypeStruct(shape, F32),
        in_specs=[in_vmem()] * 3,
        out_specs=in_hbm(),
        scratch_shapes=[pltpu.VMEM((slots, group, cols, bands), F32), pltpu.SemaphoreType.DMA((slots,))],
        compiler_params=params(24),
        cost_estimate=pl.CostEstimate(flops=3 * 2 * pixels * W * W, bytes_accessed=4 * pixels * W, transcendentals=0),
        name="filter",
    )(halves, valid, weights)


RING = 4


def permute(x, target):
    track, strip = lax.axis_size("track"), lax.axis_size("strip")
    pairs = []
    for i in range(track):
        for j in range(strip):
            y, z, chip, core = target(i // RING, i % RING, j // 2, j % 2)
            pairs.append((i * strip + j, (y * RING + z) * strip + chip * 2 + core))
    return lax.ppermute(x, ("track", "strip"), pairs)


def other_core(x):
    return permute(x, lambda y, z, chip, core: (y, z, chip, 1 - core))


def ring_sum(x, axes):
    def moved(by):
        def target(y, z, chip, core):
            place = [y, z, chip]
            axis = axes[core]
            place[axis] = (place[axis] + (by if core == 0 else -by)) % RING
            return (*place, core)

        return permute(x, target)

    return lax.optimization_barrier(x + moved(1) + moved(3) + moved(2))


def per_device(cube, mask):
    bands = cube.shape[2]
    size = lax.axis_size("track")
    below = lax.ppermute(first_row(mask, cube), "track", [(i, i - 1) for i in range(1, size)])
    core = (lax.axis_index("strip") % 2).astype(jnp.int32)[None]
    halves, valid, last, pixel, pair, rest = moments(mask, cube)
    mine, other = pack(core, valid, last, below, pixel, pair, rest)
    total = mine + other_core(other)
    for axes in ((0, 1), (1, 2), (2, 0)):
        total = ring_sum(total, axes)
    weights = solve(core, total, other_core(total), bands)
    return apply_filter(halves, valid, weights, cube.shape)


def solution(mesh):
    return jax.shard_map(
        per_device,
        mesh=mesh,
        in_specs=(P("track", "strip", None), P("track", "strip")),
        out_specs=P("track", "strip", None),
        check_vma=False,
    )
```

time: 79.3 us -> 66.5 us (0.84)
  waiting for transfers between devices: 25.3 us -> 9.86 us
  starting transfers between devices: 17.3 us -> 28.3 us
  Pallas kernels: 33.6 us -> 27.1 us
  local copies, waits for them, and re-layouts: 1.85 us -> 0.68 us
  other arithmetic: 0.9 us -> 0.1 us
    ppermute x12, waiting for transfers between devices: 25.3 us -> 9.86 us  [the longest x11 9.54 us: permute(): return lax.ppermute(x, ('track', 'strip'), pairs)]
    ppermute x12, starting transfers between devices: 17.3 us -> 28.3 us  [the longest x11 27 us: permute(): return lax.ppermute(x, ('track', 'strip'), pairs)]
    pallas_call x4 -> x5, Pallas kernels: 33.6 us -> 27.1 us  [the longest x1 10.1 us: moments(): pl.pallas_call(moments_kernel, out_shape=[pltpu.VMEM((pixels, 2 * W), BF1...]
    squeeze x1 -> x0, local copies, waits for them, and re-layouts: 1 us -> none  [per_device(): row = jnp.concatenate([cube[0], first], 1)]
  transfers between devices with their start and end apart: 12 -> 12, of which waited for: 11 -> 7; matrix products, arithmetic and copies ran while one was open for 0% -> 0% of each run, Pallas kernels for 18% -> 15%
where the time goes in v1:
time: 66.5 us; the launch traced here: 66.3 us
  starting transfers between devices  28.3 us (43%)
  Pallas kernels  27.1 us (41%)
  waiting for transfers between devices  9.86 us (15%)
  local copies, waits for them, and re-layouts  0.68 us (1%)
    ppermute x11, starting transfers between devices, permute(): return lax.ppermute(x, ('track', 'strip'), pairs)  27 us
    pallas_call x1, Pallas kernels, moments(): pl.pallas_call(moments_kernel, out_shape=[pltpu.VMEM((pixels, 2 * W), BF1...  10.1 us
    ppermute x11, waiting for transfers between devices, permute(): return lax.ppermute(x, ('track', 'strip'), pairs)  9.54 us
    pallas_call x1, Pallas kernels, apply_filter(): pl.pallas_call(filter_kernel, out_shape=jax.ShapeDtypeStruct(shape, F32),...  8.43 us
    pallas_call x1, Pallas kernels, solve(): pl.pallas_call(functools.partial(solve_kernel, bands), out_shape=pltpu.VM...  6.77 us
  transfers between devices with their start and end apart: 12, of which 7 were waited for; matrix products, arithmetic and copies ran while one was open for 0% of the time, Pallas kernels for 15%

profile of v1, /device:TPU:1, one launch (start us, length us, event | category | flops | bytes accessed | tf_op | source)
XLA Modules:
  0.0 66.3 jit_solution(4629301628669919795)
XLA Ops:
  0.0 0.0 copy-start
  0.0 0.7 %copy-done = s32[4,40]{1,0:T(4,128)S(1)} copy-done((s32[4,40]{1,0:T(4,128)S(1)}, s32[4,40]{1,0:T(4,128)}, u32[]{:S(2)}) %copy-start) | copy-done | bytes 664
  0.7 1.0 %first_row.1 = f32[320,256]{1,0:T(8,128)S(1)} custom-call(s32[4,40]{1,0:T(4,128)S(1)} %copy-done, f32[32,320,224]{2,1,0:T(8,128)} %cube_hbm.3), custom_call_target="tpu_custom_call" | custom-call | tf_op jit(solution)/shard_map/first_row/pallas_call | solution.py:89
  1.7 1.3 %collective-permute-start = (f32[320,256]{1,0:T(8,128)S(1)}, f32[320,256]{1,0:T(8,128)S(1)}, u32[]{:S(2)}, u32[]{:S(2)}) collective-permute-start(f32[320,256]{1,0:T(8,128)S(1)} %first_row.1), channel_id=1, source_target_pairs={{8,0},{16,8},{24,16},{32,24},{40,32},{48,40},{56,48},{64,56},{72,6... | collective-permute-start | bytes 983048 | tf_op jit(solution)/shard_map/ppermute | solution.py:443
  3.0 0.0 copy-done.1
  3.0 10.1 %moments.1 = (bf16[10240,512]{1,0:T(8,128)(2,1)S(1)}, f32[4,320,256]{2,1,0:T(8,128)S(1)}, f32[320,224]{1,0:T(8,128)S(1)}, f32[256,512]{1,0:T(8,128)S(1)}, f32[25...) custom-call(s32[4,40]{1,0:T(4,128)S(1)} %copy-done.1, f32[32,320,224]{2,1,0:T(8,128)} %cube_hbm.3), custom_call_target="tpu_custom_call" | custom-call | flops 5368709120 | bytes 10485760 | tf_op jit(solution)/shard_map/moments/pallas_call | solution.py:177
  13.2 0.3 collective-permute-done.below_ref
  13.5 0.7 %pack.1 = (f32[112,256]{1,0:T(8,128)S(1)}, f32[112,256]{1,0:T(8,128)S(1)}) custom-call(s32[1]{0:T(128)} %bitcast.core_ref, f32[4,320,256]{2,1,0:T(8,128)S(1)} %get-tuple-element.14.valid_ref, f32[320,224]{1,0:T(8,128)S(1)} %get-tuple-element.15.last_ref, f32[320,256]{1,0:T(8,128)S(1)} %collective-permute-done.below_ref, ...), custom_call_target="tpu_custom_call" | custom-call | tf_op jit(solution)/shard_map/pack/pallas_call | solution.py:252
  14.2 1.3 %collective-permute-start.1 = (f32[112,256]{1,0:T(8,128)S(1)}, f32[112,256]{1,0:T(8,128)S(1)}, u32[]{:S(2)}, u32[]{:S(2)}) collective-permute-start(f32[112,256]{1,0:T(8,128)S(1)} %get-tuple-element.20), channel_id=1, source_target_pairs={{0,1},{1,0},{2,3},{3,2},{4,5},{5,4},{6,7},{7,6},{8,9},{9,8},{10,11... | collective-permute-start | bytes 344072 | tf_op jit(solution)/shard_map/ppermute | solution.py:420
  15.6 1.0 %collective-permute-done.1 = f32[112,256]{1,0:T(8,128)S(1)} collective-permute-done((f32[112,256]{1,0:T(8,128)S(1)}, f32[112,256]{1,0:T(8,128)S(1)}, u32[]{:S(2)}, u32[]{:S(2)}) %collective-permute-start.1) | collective-permute-done | bytes 114720 | tf_op jit(solution)/shard_map/ppermute | solution.py:420
  16.6 4.4 %collective-permute-start.4 = (f32[112,256]{1,0:T(8,128)S(1)}, f32[112,256]{1,0:T(8,128)S(1)}, u32[]{:S(2)}, u32[]{:S(2)}) collective-permute-start(f32[112,256]{1,0:T(8,128)S(1)} %add.35), channel_id=1, source_target_pairs={{0,64},{1,17},{2,66},{3,19},{4,68},{5,21},{6,70},{7,23},{8,72},{9,... | collective-permute-start | bytes 344072 | tf_op jit(solution)/shard_map/ppermute | solution.py:420
  20.9 2.0 %collective-permute-start.3 = (f32[112,256]{1,0:T(8,128)S(1)}, f32[112,256]{1,0:T(8,128)S(1)}, u32[]{:S(2)}, u32[]{:S(2)}) collective-permute-start(f32[112,256]{1,0:T(8,128)S(1)} %add.35), channel_id=1, source_target_pairs={{0,96},{1,9},{2,98},{3,11},{4,100},{5,13},{6,102},{7,15},{8,104},{... | collective-permute-start | bytes 344072 | tf_op jit(solution)/shard_map/ppermute | solution.py:420
  22.9 0.7 %collective-permute-start.2 = (f32[112,256]{1,0:T(8,128)S(1)}, f32[112,256]{1,0:T(8,128)S(1)}, u32[]{:S(2)}, u32[]{:S(2)}) collective-permute-start(f32[112,256]{1,0:T(8,128)S(1)} %add.35), channel_id=1, source_target_pairs={{0,32},{1,25},{2,34},{3,27},{4,36},{5,29},{6,38},{7,31},{8,40},{9,... | collective-permute-start | bytes 344072 | tf_op jit(solution)/shard_map/ppermute | solution.py:420
  23.6 0.0 collective-permute-done.4
  23.6 2.5 %collective-permute-done.3 = f32[112,256]{1,0:T(8,128)S(1)} collective-permute-done((f32[112,256]{1,0:T(8,128)S(1)}, f32[112,256]{1,0:T(8,128)S(1)}, u32[]{:S(2)}, u32[]{:S(2)}) %collective-permute-start.3) | collective-permute-done | bytes 114720 | tf_op jit(solution)/shard_map/ppermute | solution.py:420
  26.1 0.8 %collective-permute-done.2 = f32[112,256]{1,0:T(8,128)S(1)} collective-permute-done((f32[112,256]{1,0:T(8,128)S(1)}, f32[112,256]{1,0:T(8,128)S(1)}, u32[]{:S(2)}, u32[]{:S(2)}) %collective-permute-start.2) | collective-permute-done | bytes 114720 | tf_op jit(solution)/shard_map/ppermute | solution.py:420
  26.9 2.8 %collective-permute-start.7 = (f32[112,256]{1,0:T(8,128)S(1)}, f32[112,256]{1,0:T(8,128)S(1)}, u32[]{:S(2)}, u32[]{:S(2)}) collective-permute-start(f32[112,256]{1,0:T(8,128)S(1)} %add_add_fusion.2), channel_id=1, source_target_pairs={{0,16},{1,5},{2,18},{3,7},{4,20},{5,1},{6,22},{7,3},{8,24},{9,13},... | collective-permute-start | bytes 344072 | tf_op jit(solution)/shard_map/ppermute | solution.py:420
  29.7 0.3 collective-permute-start.6
  30.0 2.4 %collective-permute-start.5 = (f32[112,256]{1,0:T(8,128)S(1)}, f32[112,256]{1,0:T(8,128)S(1)}, u32[]{:S(2)}, u32[]{:S(2)}) collective-permute-start(f32[112,256]{1,0:T(8,128)S(1)} %add_add_fusion.2), channel_id=1, source_target_pairs={{0,8},{1,7},{2,10},{3,1},{4,12},{5,3},{6,14},{7,5},{8,16},{9,15},{... | collective-permute-start | bytes 344072 | tf_op jit(solution)/shard_map/ppermute | solution.py:420
  32.4 0.0 collective-permute-done.7
  32.4 2.2 %collective-permute-done.6 = f32[112,256]{1,0:T(8,128)S(1)} collective-permute-done((f32[112,256]{1,0:T(8,128)S(1)}, f32[112,256]{1,0:T(8,128)S(1)}, u32[]{:S(2)}, u32[]{:S(2)}) %collective-permute-start.6) | collective-permute-done | bytes 114720 | tf_op jit(solution)/shard_map/ppermute | solution.py:420
  34.6 0.0 collective-permute-done.5
  34.6 3.8 %collective-permute-start.10 = (f32[112,256]{1,0:T(8,128)S(1)}, f32[112,256]{1,0:T(8,128)S(1)}, u32[]{:S(2)}, u32[]{:S(2)}) collective-permute-start(f32[112,256]{1,0:T(8,128)S(1)} %add_add_fusion.1), channel_id=1, source_target_pairs={{0,4},{1,65},{2,6},{3,67},{4,0},{5,69},{6,2},{7,71},{8,12},{9,73},... | collective-permute-start | bytes 344072 | tf_op jit(solution)/shard_map/ppermute | solution.py:420
  38.4 0.9 %collective-permute-start.9 = (f32[112,256]{1,0:T(8,128)S(1)}, f32[112,256]{1,0:T(8,128)S(1)}, u32[]{:S(2)}, u32[]{:S(2)}) collective-permute-start(f32[112,256]{1,0:T(8,128)S(1)} %add_add_fusion.1), channel_id=1, source_target_pairs={{0,6},{1,33},{2,0},{3,35},{4,2},{5,37},{6,4},{7,39},{8,14},{9,41},... | collective-permute-start | bytes 344072 | tf_op jit(solution)/shard_map/ppermute | solution.py:420
  39.3 1.8 %collective-permute-start.8 = (f32[112,256]{1,0:T(8,128)S(1)}, f32[112,256]{1,0:T(8,128)S(1)}, u32[]{:S(2)}, u32[]{:S(2)}) collective-permute-start(f32[112,256]{1,0:T(8,128)S(1)} %add_add_fusion.1), channel_id=1, source_target_pairs={{0,2},{1,97},{2,4},{3,99},{4,6},{5,101},{6,0},{7,103},{8,10},{9,10... | collective-permute-start | bytes 344072 | tf_op jit(solution)/shard_map/ppermute | solution.py:420
  41.1 0.0 collective-permute-done.10
  41.1 2.2 %collective-permute-done.9 = f32[112,256]{1,0:T(8,128)S(1)} collective-permute-done((f32[112,256]{1,0:T(8,128)S(1)}, f32[112,256]{1,0:T(8,128)S(1)}, u32[]{:S(2)}, u32[]{:S(2)}) %collective-permute-start.9) | collective-permute-done | bytes 114720 | tf_op jit(solution)/shard_map/ppermute | solution.py:420
  43.3 0.0 collective-permute-done.8
  43.3 6.7 %collective-permute-start.11 = (f32[112,256]{1,0:T(8,128)S(1)}, f32[112,256]{1,0:T(8,128)S(1)}, u32[]{:S(2)}, u32[]{:S(2)}) collective-permute-start(f32[112,256]{1,0:T(8,128)S(1)} %add_add_fusion.mine_ref), channel_id=1, source_target_pairs={{0,1},{1,0},{2,3},{3,2},{4,5},{5,4},{6,7},{7,6},{8,9},{9,8},{10,11... | collective-permute-start | bytes 344072 | tf_op jit(solution)/shard_map/ppermute | solution.py:420
  50.0 1.0 %collective-permute-done.11.other_ref = f32[112,256]{1,0:T(8,128)S(1)} collective-permute-done((f32[112,256]{1,0:T(8,128)S(1)}, f32[112,256]{1,0:T(8,128)S(1)}, u32[]{:S(2)}, u32[]{:S(2)}) %collective-permute-start.11) | collective-permute-done | bytes 114720 | tf_op jit(solution)/shard_map/ppermute | solution.py:420
  51.0 6.8 %solve.1.weights_ref = bf16[768,256]{1,0:T(8,128)(2,1)S(1)} custom-call(s32[1]{0:T(128)} %bitcast.core_ref, f32[112,256]{1,0:T(8,128)S(1)} %add_add_fusion.mine_ref, f32[112,256]{1,0:T(8,128)S(1)} %collective-permute-done.11.other_ref), custom_call_target="tpu_custom_call" | custom-call | tf_op jit(solution)/shard_map/solve/pallas_call | solution.py:363
  57.7 8.4 %filter.1 = f32[32,320,224]{2,1,0:T(8,128)} custom-call(bf16[10240,512]{1,0:T(8,128)(2,1)S(1)} %get-tuple-element.13.halves_ref, f32[4,320,256]{2,1,0:T(8,128)S(1)} %get-tuple-element.14.valid_ref, bf16[768,256]{1,0:T(8,128)(2,1)S(1)} %solve.1.weights_ref), custom_call_target="tpu_custom_call" | custom-call | flops 4026531840 | bytes 10485760 | tf_op jit(solution)/shard_map/filter/pallas_call | solution.py:398
  (5 shorter events, 0.1 us)
Async XLA Ops:
  0.0 0.7 %copy-start = (s32[4,40]{1,0:T(4,128)S(1)}, s32[4,40]{1,0:T(4,128)}, u32[]{:S(2)}) copy-start(s32[4,40]{1,0:T(4,128)} %mask_hbm.3) | copy-start | bytes 1924
  0.7 2.4 %copy-start.1 = (s32[4,40]{1,0:T(4,128)S(1)}, s32[4,40]{1,0:T(4,128)}, u32[]{:S(2)}) copy-start(s32[4,40]{1,0:T(4,128)} %mask_hbm.3) | copy-start | bytes 1924
  1.7 11.8 %collective-permute-start = (f32[320,256]{1,0:T(8,128)S(1)}, f32[320,256]{1,0:T(8,128)S(1)}, u32[]{:S(2)}, u32[]{:S(2)}) collective-permute-start(f32[320,256]{1,0:T(8,128)S(1)} %first_row.1), channel_id=1, source_target_pairs={{8,0},{16,8},{24,16},{32,24},{40,32},{48,40},{56,48},{64,56},{72,6... | collective-permute-start | bytes 983048 | tf_op jit(solution)/shard_map/ppermute | solution.py:443
  14.2 2.3 %collective-permute-start.1 = (f32[112,256]{1,0:T(8,128)S(1)}, f32[112,256]{1,0:T(8,128)S(1)}, u32[]{:S(2)}, u32[]{:S(2)}) collective-permute-start(f32[112,256]{1,0:T(8,128)S(1)} %get-tuple-element.20), channel_id=1, source_target_pairs={{0,1},{1,0},{2,3},{3,2},{4,5},{5,4},{6,7},{7,6},{8,9},{9,8},{10,11... | collective-permute-start | bytes 344072 | tf_op jit(solution)/shard_map/ppermute | solution.py:420
  16.6 7.0 %collective-permute-start.4 = (f32[112,256]{1,0:T(8,128)S(1)}, f32[112,256]{1,0:T(8,128)S(1)}, u32[]{:S(2)}, u32[]{:S(2)}) collective-permute-start(f32[112,256]{1,0:T(8,128)S(1)} %add.35), channel_id=1, source_target_pairs={{0,64},{1,17},{2,66},{3,19},{4,68},{5,21},{6,70},{7,23},{8,72},{9,... | collective-permute-start | bytes 344072 | tf_op jit(solution)/shard_map/ppermute | solution.py:420
  20.9 5.1 %collective-permute-start.3 = (f32[112,256]{1,0:T(8,128)S(1)}, f32[112,256]{1,0:T(8,128)S(1)}, u32[]{:S(2)}, u32[]{:S(2)}) collective-permute-start(f32[112,256]{1,0:T(8,128)S(1)} %add.35), channel_id=1, source_target_pairs={{0,96},{1,9},{2,98},{3,11},{4,100},{5,13},{6,102},{7,15},{8,104},{... | collective-permute-start | bytes 344072 | tf_op jit(solution)/shard_map/ppermute | solution.py:420
  22.9 3.9 %collective-permute-start.2 = (f32[112,256]{1,0:T(8,128)S(1)}, f32[112,256]{1,0:T(8,128)S(1)}, u32[]{:S(2)}, u32[]{:S(2)}) collective-permute-start(f32[112,256]{1,0:T(8,128)S(1)} %add.35), channel_id=1, source_target_pairs={{0,32},{1,25},{2,34},{3,27},{4,36},{5,29},{6,38},{7,31},{8,40},{9,... | collective-permute-start | bytes 344072 | tf_op jit(solution)/shard_map/ppermute | solution.py:420
  26.9 5.5 %collective-permute-start.7 = (f32[112,256]{1,0:T(8,128)S(1)}, f32[112,256]{1,0:T(8,128)S(1)}, u32[]{:S(2)}, u32[]{:S(2)}) collective-permute-start(f32[112,256]{1,0:T(8,128)S(1)} %add_add_fusion.2), channel_id=1, source_target_pairs={{0,16},{1,5},{2,18},{3,7},{4,20},{5,1},{6,22},{7,3},{8,24},{9,13},... | collective-permute-start | bytes 344072 | tf_op jit(solution)/shard_map/ppermute | solution.py:420
  29.7 4.9 %collective-permute-start.6 = (f32[112,256]{1,0:T(8,128)S(1)}, f32[112,256]{1,0:T(8,128)S(1)}, u32[]{:S(2)}, u32[]{:S(2)}) collective-permute-start(f32[112,256]{1,0:T(8,128)S(1)} %add_add_fusion.2), channel_id=1, source_target_pairs={{0,24},{1,3},{2,26},{3,5},{4,28},{5,7},{6,30},{7,1},{8,0},{9,11},{... | collective-permute-start | bytes 344072 | tf_op jit(solution)/shard_map/ppermute | solution.py:420
  30.0 4.5 %collective-permute-start.5 = (f32[112,256]{1,0:T(8,128)S(1)}, f32[112,256]{1,0:T(8,128)S(1)}, u32[]{:S(2)}, u32[]{:S(2)}) collective-permute-start(f32[112,256]{1,0:T(8,128)S(1)} %add_add_fusion.2), channel_id=1, source_target_pairs={{0,8},{1,7},{2,10},{3,1},{4,12},{5,3},{6,14},{7,5},{8,16},{9,15},{... | collective-permute-start | bytes 344072 | tf_op jit(solution)/shard_map/ppermute | solution.py:420
  34.6 6.5 %collective-permute-start.10 = (f32[112,256]{1,0:T(8,128)S(1)}, f32[112,256]{1,0:T(8,128)S(1)}, u32[]{:S(2)}, u32[]{:S(2)}) collective-permute-start(f32[112,256]{1,0:T(8,128)S(1)} %add_add_fusion.1), channel_id=1, source_target_pairs={{0,4},{1,65},{2,6},{3,67},{4,0},{5,69},{6,2},{7,71},{8,12},{9,73},... | collective-permute-start | bytes 344072 | tf_op jit(solution)/shard_map/ppermute | solution.py:420
  38.4 4.9 %collective-permute-start.9 = (f32[112,256]{1,0:T(8,128)S(1)}, f32[112,256]{1,0:T(8,128)S(1)}, u32[]{:S(2)}, u32[]{:S(2)}) collective-permute-start(f32[112,256]{1,0:T(8,128)S(1)} %add_add_fusion.1), channel_id=1, source_target_pairs={{0,6},{1,33},{2,0},{3,35},{4,2},{5,37},{6,4},{7,39},{8,14},{9,41},... | collective-permute-start | bytes 344072 | tf_op jit(solution)/shard_map/ppermute | solution.py:420
  39.3 4.0 %collective-permute-start.8 = (f32[112,256]{1,0:T(8,128)S(1)}, f32[112,256]{1,0:T(8,128)S(1)}, u32[]{:S(2)}, u32[]{:S(2)}) collective-permute-start(f32[112,256]{1,0:T(8,128)S(1)} %add_add_fusion.1), channel_id=1, source_target_pairs={{0,2},{1,97},{2,4},{3,99},{4,6},{5,101},{6,0},{7,103},{8,10},{9,10... | collective-permute-start | bytes 344072 | tf_op jit(solution)/shard_map/ppermute | solution.py:420
  43.3 7.6 %collective-permute-start.11 = (f32[112,256]{1,0:T(8,128)S(1)}, f32[112,256]{1,0:T(8,128)S(1)}, u32[]{:S(2)}, u32[]{:S(2)}) collective-permute-start(f32[112,256]{1,0:T(8,128)S(1)} %add_add_fusion.mine_ref), channel_id=1, source_target_pairs={{0,1},{1,0},{2,3},{3,2},{4,5},{5,4},{6,7},{7,6},{8,9},{9,8},{10,11... | collective-permute-start | bytes 344072 | tf_op jit(solution)/shard_map/ppermute | solution.py:420

commit v2 on v1

--- a/solution.py
+++ b/solution.py
@@ -102,10 +102,11 @@
 
 
 GROUP = 4
+BLOCK = 64
 
 
 def moments_kernel(
-    mask_hbm, cube_hbm, halves_ref, valid_ref, last_ref, pixel_ref, pair_ref, rest_ref, mask, raw, seam, pairs_a, pairs_b, sems
+    mask_hbm, cube_hbm, halves_ref, valid_ref, last_ref, pixel_ref, pair_ref, rest_ref, mask, raw, pairs_a, pairs_b, sems
 ):
     rows, cols, bands = raw.shape
     groups = rows // GROUP
@@ -126,49 +127,64 @@
         buffer[:, W + bands :] = jnp.zeros((count, W - bands), BF16)
     mask_copy.wait()
 
-    def put(value, buffer, r, squares):
+    def put(value, buffer, at, lanes, squares):
+        count = value.shape[0]
         high = value.astype(BF16)
-        rest = value - high.astype(F32)
-        buffer[r * cols : (r + 1) * cols, :bands] = high
-        buffer[r * cols : (r + 1) * cols, W : W + bands] = rest.astype(BF16)
-        return squares + jnp.sum((rest * rest).reshape(cols // 8, 8, bands), 0)
+        low = (value - high.astype(F32)).astype(BF16)
+        buffer[at : at + count, lanes] = high
+        buffer[at : at + count, slice(W + lanes.start, W + lanes.stop)] = low
+        parts = (low * low).reshape(count // 16, 16, -1)
+        total = parts[0]
+        for k in range(1, count // 16):
+            total = total + parts[k]
+        return squares + jnp.sum(total.astype(F32).reshape(2, 8, -1), 0)
+
+    def product(ref, buffer, half):
+        at = slice(half * W, (half + 1) * W)
+        ref[:, at] += dot_t(buffer[:, :W], buffer[:, at])
 
     def products(halves, pairs):
-        pixel_ref[...] += dot_t(halves[:, :W], halves[...])
-        pair_ref[...] += dot_t(pairs[:, :W], pairs[...])
-
-    squares = [jnp.zeros((8, bands), F32)] * 2
-    previous = None
-    pending = None
+        return [(pixel_ref, halves, 0), (pixel_ref, halves, 1), (pair_ref, pairs, 0), (pair_ref, pairs, 1)]
+
+    lane_halves = (slice(0, 128), slice(128, bands))
+    squares = {(k, h): jnp.zeros((8, lanes.stop - lanes.start), F32) for k in range(2) for h, lanes in enumerate(lane_halves)}
+    pending = []
     for g in range(groups):
         pairs = (pairs_a, pairs_b)[g % 2]
         halves = halves_ref.at[pl.ds(g * GROUP * cols, GROUP * cols)]
-        if pending is not None:
-            products(*pending)
         fetch(g).wait()
-        for r in range(GROUP):
-            row = g * GROUP + r
-            valid = valid_ref.at[row // TILE]
-            if row % TILE == 0:
-                fill_validity(mask, row // TILE, valid)
-                if row:
-                    seam[...] = valid_ref[row // TILE - 1] * valid[...]
-            pixel = raw[row] * valid[:, :bands]
-            if row == 0:
-                difference = jnp.zeros_like(pixel)
-            elif row % TILE == 0:
-                difference = (pixel - previous) * seam[:, :bands]
-            else:
-                difference = pixel - previous
-            previous = pixel
-            squares[0] = put(pixel, halves, r, squares[0])
-            squares[1] = put(difference, pairs, r, squares[1])
-        pending = (halves, pairs)
-    products(*pending)
-    last_ref[...] = previous
+        tile_row, within = divmod(g * GROUP, TILE)
+        if within == 0:
+            fill_validity(mask, tile_row, valid_ref.at[tile_row])
+        for c in range(0, cols, BLOCK):
+            if pending:
+                product(*pending.pop(0))
+            block = slice(c, c + BLOCK)
+            valid = valid_ref[tile_row, block, :128]
+            for h, lanes in enumerate(lane_halves):
+                weight = valid[:, : lanes.stop - lanes.start]
+                previous = last_ref[block, lanes] if g else None
+                for r in range(GROUP):
+                    pixel = raw[g * GROUP + r, block, lanes] * weight
+                    if previous is None:
+                        difference = jnp.zeros_like(pixel)
+                    else:
+                        difference = pixel - previous
+                        if within == 0 and r == 0:
+                            difference = difference * (valid_ref[tile_row - 1, block, : weight.shape[1]] * weight)
+                    previous = pixel
+                    squares[0, h] = put(pixel, halves, r * cols + c, lanes, squares[0, h])
+                    squares[1, h] = put(difference, pairs, r * cols + c, lanes, squares[1, h])
+                last_ref[block, lanes] = previous
+        for late in pending:
+            product(*late)
+        pending = products(halves, pairs)
+    for late in pending:
+        product(*late)
     for k in range(2):
-        rest_ref[k, :, :bands] = squares[k]
         rest_ref[k, :, bands:] = jnp.zeros((8, W - bands), F32)
+        for h, lanes in enumerate(lane_halves):
+            rest_ref[k, :, lanes] = squares[k, h]
 
 
 def moments(mask, cube):
@@ -189,7 +205,6 @@
         scratch_shapes=[
             pltpu.SMEM(mask.shape, jnp.int32),
             pltpu.VMEM(cube.shape, F32),
-            pltpu.VMEM((cols, W), F32),
             pltpu.VMEM((GROUP * cols, 2 * W), BF16),
             pltpu.VMEM((GROUP * cols, 2 * W), BF16),
             pltpu.SemaphoreType.DMA((rows // GROUP + 1,)),
@@ -372,35 +387,27 @@
 
 
 def filter_kernel(halves_ref, valid_ref, weights_ref, out_hbm, staged, sems):
-    slots, group, cols, bands = staged.shape
-    groups = out_hbm.shape[0] // group
-
-    def send(g):
-        return pltpu.make_async_copy(staged.at[g % slots], out_hbm.at[pl.ds(g * group, group)], sems.at[g % slots])
-
-    for g in range(groups):
-        if g >= slots:
-            send(g - slots).wait()
-        halves = halves_ref[g * group * cols : (g + 1) * group * cols, :]
+    rows, cols, bands = staged.shape
+    copies = []
+    for r in range(rows):
+        halves = halves_ref[r * cols : (r + 1) * cols, :]
         result = dot(jnp.concatenate([halves, halves[:, :W]], 1), weights_ref[...])
-        valid = valid_ref[g * group // TILE]
-        for r in range(group):
-            staged[g % slots, r] = valid[:, :bands] * result[r * cols : (r + 1) * cols, :bands]
-        send(g).start()
-    for g in range(groups - slots, groups):
-        send(g).wait()
+        staged[r] = valid_ref[r // TILE][:, :bands] * result[:, :bands]
+        copies.append(pltpu.make_async_copy(staged.at[pl.ds(r, 1)], out_hbm.at[pl.ds(r, 1)], sems.at[r]))
+        copies[-1].start()
+    for copy in copies:
+        copy.wait()
 
 
 def apply_filter(halves, valid, weights, shape):
     rows, cols, bands = shape
-    group, slots = 4, 4
     pixels = rows * cols
     return pl.pallas_call(
         filter_kernel,
         out_shape=jax.ShapeDtypeStruct(shape, F32),
         in_specs=[in_vmem()] * 3,
         out_specs=in_hbm(),
-        scratch_shapes=[pltpu.VMEM((slots, group, cols, bands), F32), pltpu.SemaphoreType.DMA((slots,))],
+        scratch_shapes=[pltpu.VMEM(shape, F32), pltpu.SemaphoreType.DMA((rows,))],
         compiler_params=params(24),
         cost_estimate=pl.CostEstimate(flops=3 * 2 * pixels * W * W, bytes_accessed=4 * pixels * W, transcendentals=0),
         name="filter",
@@ -424,17 +431,20 @@
     return permute(x, lambda y, z, chip, core: (y, z, chip, 1 - core))
 
 
+PARTNER = {1: (1, 0, 3, 2), 2: (2, 3, 0, 1), 3: (3, 2, 1, 0)}
+
+
 def ring_sum(x, axes):
-    def moved(by):
+    def exchanged(which):
         def target(y, z, chip, core):
             place = [y, z, chip]
             axis = axes[core]
-            place[axis] = (place[axis] + (by if core == 0 else -by)) % RING
+            place[axis] = PARTNER[which if core == 0 else RING - which][place[axis]]
             return (*place, core)
 
         return permute(x, target)
 
-    return lax.optimization_barrier(x + moved(1) + moved(3) + moved(2))
+    return lax.optimization_barrier(x + exchanged(1) + exchanged(3) + exchanged(2))
 
 
 def per_device(cube, mask):

time: 66.5 us -> 61 us (0.917)
  starting transfers between devices: 28.3 us -> 19 us
  waiting for transfers between devices: 9.86 us -> 16.7 us
  Pallas kernels: 27.1 us -> 24 us
    ppermute x11, starting transfers between devices: 27 us -> 17.7 us  [permute(): return lax.ppermute(x, ('track', 'strip'), pairs)]
    ppermute x11, waiting for transfers between devices: 9.54 us -> 16 us  [permute(): return lax.ppermute(x, ('track', 'strip'), pairs)]
    pallas_call x1, Pallas kernels: 8.43 us -> 5.69 us  [apply_filter(): pl.pallas_call(filter_kernel, out_shape=jax.ShapeDtypeStruct(shape, F32),...]
  transfers between devices with their start and end apart: 12 -> 12, of which waited for: 7 -> 11; matrix products, arithmetic and copies ran while one was open for 0% -> 0% of each run, Pallas kernels for 15% -> 16%
where the time goes in v2:
time: 61 us; the launch traced here: 60.8 us
  Pallas kernels  24 us (39%)
  starting transfers between devices  19 us (31%)
  waiting for transfers between devices  16.7 us (27%)
  local copies, waits for them, and re-layouts  0.68 us (1%)
    ppermute x11, starting transfers between devices, permute(): return lax.ppermute(x, ('track', 'strip'), pairs)  17.7 us
    ppermute x11, waiting for transfers between devices, permute(): return lax.ppermute(x, ('track', 'strip'), pairs)  16 us
    pallas_call x1, Pallas kernels, moments(): pl.pallas_call(moments_kernel, out_shape=[pltpu.VMEM((pixels, 2 * W), BF1...  9.76 us
    pallas_call x1, Pallas kernels, solve(): pl.pallas_call(functools.partial(solve_kernel, bands), out_shape=pltpu.VM...  6.77 us
    pallas_call x1, Pallas kernels, apply_filter(): pl.pallas_call(filter_kernel, out_shape=jax.ShapeDtypeStruct(shape, F32),...  5.69 us
    ppermute x1, starting transfers between devices, per_device(): lax.ppermute(first_row(mask, cube), 'track', [(i, i - 1) for i in range(1...  1.29 us
  transfers between devices with their start and end apart: 12, of which 11 were waited for; matrix products, arithmetic and copies ran while one was open for 0% of the time, Pallas kernels for 16%

profile of v2, /device:TPU:1, one launch (start us, length us, event | category | flops | bytes accessed | tf_op | source)
XLA Modules:
  0.0 60.8 jit_solution(8152721385331645402)
XLA Ops:
  0.0 0.0 copy-start
  0.0 0.7 %copy-done = s32[4,40]{1,0:T(4,128)S(1)} copy-done((s32[4,40]{1,0:T(4,128)S(1)}, s32[4,40]{1,0:T(4,128)}, u32[]{:S(2)}) %copy-start) | copy-done | bytes 664
  0.7 1.0 %first_row.1 = f32[320,256]{1,0:T(8,128)S(1)} custom-call(s32[4,40]{1,0:T(4,128)S(1)} %copy-done, f32[32,320,224]{2,1,0:T(8,128)} %cube_hbm.3), custom_call_target="tpu_custom_call" | custom-call | tf_op jit(solution)/shard_map/first_row/pallas_call | solution.py:89
  1.7 1.3 %collective-permute-start = (f32[320,256]{1,0:T(8,128)S(1)}, f32[320,256]{1,0:T(8,128)S(1)}, u32[]{:S(2)}, u32[]{:S(2)}) collective-permute-start(f32[320,256]{1,0:T(8,128)S(1)} %first_row.1), channel_id=1, source_target_pairs={{8,0},{16,8},{24,16},{32,24},{40,32},{48,40},{56,48},{64,56},{72,6... | collective-permute-start | bytes 983048 | tf_op jit(solution)/shard_map/ppermute | solution.py:453
  3.0 0.0 copy-done.1
  3.0 9.8 %moments.1 = (bf16[10240,512]{1,0:T(8,128)(2,1)S(1)}, f32[4,320,256]{2,1,0:T(8,128)S(1)}, f32[320,224]{1,0:T(8,128)S(1)}, f32[256,512]{1,0:T(8,128)S(1)}, f32[25...) custom-call(s32[4,40]{1,0:T(4,128)S(1)} %copy-done.1, f32[32,320,224]{2,1,0:T(8,128)} %cube_hbm.3), custom_call_target="tpu_custom_call" | custom-call | flops 5368709120 | bytes 10485760 | tf_op jit(solution)/shard_map/moments/pallas_call | solution.py:193
  12.8 0.7 %collective-permute-done.below_ref = f32[320,256]{1,0:T(8,128)S(1)} collective-permute-done((f32[320,256]{1,0:T(8,128)S(1)}, f32[320,256]{1,0:T(8,128)S(1)}, u32[]{:S(2)}, u32[]{:S(2)}) %collective-permute-start) | collective-permute-done | bytes 327712 | tf_op jit(solution)/shard_map/ppermute | solution.py:453
  13.5 0.7 %pack.1 = (f32[112,256]{1,0:T(8,128)S(1)}, f32[112,256]{1,0:T(8,128)S(1)}) custom-call(s32[1]{0:T(128)} %bitcast.core_ref, f32[4,320,256]{2,1,0:T(8,128)S(1)} %get-tuple-element.14.valid_ref, f32[320,224]{1,0:T(8,128)S(1)} %get-tuple-element.15.last_ref, f32[320,256]{1,0:T(8,128)S(1)} %collective-permute-done.below_ref, ...), custom_call_target="tpu_custom_call" | custom-call | tf_op jit(solution)/shard_map/pack/pallas_call | solution.py:267
  14.2 1.3 %collective-permute-start.1 = (f32[112,256]{1,0:T(8,128)S(1)}, f32[112,256]{1,0:T(8,128)S(1)}, u32[]{:S(2)}, u32[]{:S(2)}) collective-permute-start(f32[112,256]{1,0:T(8,128)S(1)} %get-tuple-element.20), channel_id=1, source_target_pairs={{0,1},{1,0},{2,3},{3,2},{4,5},{5,4},{6,7},{7,6},{8,9},{9,8},{10,11... | collective-permute-start | bytes 344072 | tf_op jit(solution)/shard_map/ppermute | solution.py:427
  15.6 1.0 %collective-permute-done.1 = f32[112,256]{1,0:T(8,128)S(1)} collective-permute-done((f32[112,256]{1,0:T(8,128)S(1)}, f32[112,256]{1,0:T(8,128)S(1)}, u32[]{:S(2)}, u32[]{:S(2)}) %collective-permute-start.1) | collective-permute-done | bytes 114720 | tf_op jit(solution)/shard_map/ppermute | solution.py:427
  16.6 4.0 %collective-permute-start.4 = (f32[112,256]{1,0:T(8,128)S(1)}, f32[112,256]{1,0:T(8,128)S(1)}, u32[]{:S(2)}, u32[]{:S(2)}) collective-permute-start(f32[112,256]{1,0:T(8,128)S(1)} %add.35), channel_id=1, source_target_pairs={{0,64},{1,17},{2,66},{3,19},{4,68},{5,21},{6,70},{7,23},{8,72},{9,... | collective-permute-start | bytes 344072 | tf_op jit(solution)/shard_map/ppermute | solution.py:427
  20.5 2.4 %collective-permute-start.3 = (f32[112,256]{1,0:T(8,128)S(1)}, f32[112,256]{1,0:T(8,128)S(1)}, u32[]{:S(2)}, u32[]{:S(2)}) collective-permute-start(f32[112,256]{1,0:T(8,128)S(1)} %add.35), channel_id=1, source_target_pairs={{0,96},{1,9},{2,98},{3,11},{4,100},{5,13},{6,102},{7,15},{8,104},{... | collective-permute-start | bytes 344072 | tf_op jit(solution)/shard_map/ppermute | solution.py:427
  22.9 0.0 collective-permute-start.2
  22.9 0.0 collective-permute-done.4
  22.9 3.7 %collective-permute-done.3 = f32[112,256]{1,0:T(8,128)S(1)} collective-permute-done((f32[112,256]{1,0:T(8,128)S(1)}, f32[112,256]{1,0:T(8,128)S(1)}, u32[]{:S(2)}, u32[]{:S(2)}) %collective-permute-start.3) | collective-permute-done | bytes 114720 | tf_op jit(solution)/shard_map/ppermute | solution.py:427
  26.6 1.2 %collective-permute-done.2 = f32[112,256]{1,0:T(8,128)S(1)} collective-permute-done((f32[112,256]{1,0:T(8,128)S(1)}, f32[112,256]{1,0:T(8,128)S(1)}, u32[]{:S(2)}, u32[]{:S(2)}) %collective-permute-start.2) | collective-permute-done | bytes 114720 | tf_op jit(solution)/shard_map/ppermute | solution.py:427
  27.8 2.8 %collective-permute-start.7 = (f32[112,256]{1,0:T(8,128)S(1)}, f32[112,256]{1,0:T(8,128)S(1)}, u32[]{:S(2)}, u32[]{:S(2)}) collective-permute-start(f32[112,256]{1,0:T(8,128)S(1)} %add_add_fusion.2), channel_id=1, source_target_pairs={{0,16},{1,5},{2,18},{3,7},{4,20},{5,1},{6,22},{7,3},{8,24},{9,13},... | collective-permute-start | bytes 344072 | tf_op jit(solution)/shard_map/ppermute | solution.py:427
  30.6 0.3 collective-permute-start.6
  30.9 0.5 collective-permute-start.5
  31.5 1.5 %collective-permute-done.7 = f32[112,256]{1,0:T(8,128)S(1)} collective-permute-done((f32[112,256]{1,0:T(8,128)S(1)}, f32[112,256]{1,0:T(8,128)S(1)}, u32[]{:S(2)}, u32[]{:S(2)}) %collective-permute-start.7) | collective-permute-done | bytes 114720 | tf_op jit(solution)/shard_map/ppermute | solution.py:427
  33.0 1.3 %collective-permute-done.6 = f32[112,256]{1,0:T(8,128)S(1)} collective-permute-done((f32[112,256]{1,0:T(8,128)S(1)}, f32[112,256]{1,0:T(8,128)S(1)}, u32[]{:S(2)}, u32[]{:S(2)}) %collective-permute-start.6) | collective-permute-done | bytes 114720 | tf_op jit(solution)/shard_map/ppermute | solution.py:427
  34.3 1.7 %collective-permute-done.5 = f32[112,256]{1,0:T(8,128)S(1)} collective-permute-done((f32[112,256]{1,0:T(8,128)S(1)}, f32[112,256]{1,0:T(8,128)S(1)}, u32[]{:S(2)}, u32[]{:S(2)}) %collective-permute-start.5) | collective-permute-done | bytes 114720 | tf_op jit(solution)/shard_map/ppermute | solution.py:427
  36.1 3.1 %collective-permute-start.10 = (f32[112,256]{1,0:T(8,128)S(1)}, f32[112,256]{1,0:T(8,128)S(1)}, u32[]{:S(2)}, u32[]{:S(2)}) collective-permute-start(f32[112,256]{1,0:T(8,128)S(1)} %add_add_fusion.1), channel_id=1, source_target_pairs={{0,4},{1,65},{2,6},{3,67},{4,0},{5,69},{6,2},{7,71},{8,12},{9,73},... | collective-permute-start | bytes 344072 | tf_op jit(solution)/shard_map/ppermute | solution.py:427
  39.2 0.4 collective-permute-start.9
  39.7 0.2 collective-permute-start.8
  39.8 1.7 %collective-permute-done.10 = f32[112,256]{1,0:T(8,128)S(1)} collective-permute-done((f32[112,256]{1,0:T(8,128)S(1)}, f32[112,256]{1,0:T(8,128)S(1)}, u32[]{:S(2)}, u32[]{:S(2)}) %collective-permute-start.10) | collective-permute-done | bytes 114720 | tf_op jit(solution)/shard_map/ppermute | solution.py:427
  41.5 1.8 %collective-permute-done.9 = f32[112,256]{1,0:T(8,128)S(1)} collective-permute-done((f32[112,256]{1,0:T(8,128)S(1)}, f32[112,256]{1,0:T(8,128)S(1)}, u32[]{:S(2)}, u32[]{:S(2)}) %collective-permute-start.9) | collective-permute-done | bytes 114720 | tf_op jit(solution)/shard_map/ppermute | solution.py:427
  43.4 1.2 %collective-permute-done.8 = f32[112,256]{1,0:T(8,128)S(1)} collective-permute-done((f32[112,256]{1,0:T(8,128)S(1)}, f32[112,256]{1,0:T(8,128)S(1)}, u32[]{:S(2)}, u32[]{:S(2)}) %collective-permute-start.8) | collective-permute-done | bytes 114720 | tf_op jit(solution)/shard_map/ppermute | solution.py:427
  44.5 2.7 %collective-permute-start.11 = (f32[112,256]{1,0:T(8,128)S(1)}, f32[112,256]{1,0:T(8,128)S(1)}, u32[]{:S(2)}, u32[]{:S(2)}) collective-permute-start(f32[112,256]{1,0:T(8,128)S(1)} %add_add_fusion.mine_ref), channel_id=1, source_target_pairs={{0,1},{1,0},{2,3},{3,2},{4,5},{5,4},{6,7},{7,6},{8,9},{9,8},{10,11... | collective-permute-start | bytes 344072 | tf_op jit(solution)/shard_map/ppermute | solution.py:427
  47.2 1.0 %collective-permute-done.11.other_ref = f32[112,256]{1,0:T(8,128)S(1)} collective-permute-done((f32[112,256]{1,0:T(8,128)S(1)}, f32[112,256]{1,0:T(8,128)S(1)}, u32[]{:S(2)}, u32[]{:S(2)}) %collective-permute-start.11) | collective-permute-done | bytes 114720 | tf_op jit(solution)/shard_map/ppermute | solution.py:427
  48.2 6.8 %solve.1.weights_ref = bf16[768,256]{1,0:T(8,128)(2,1)S(1)} custom-call(s32[1]{0:T(128)} %bitcast.core_ref, f32[112,256]{1,0:T(8,128)S(1)} %add_add_fusion.mine_ref, f32[112,256]{1,0:T(8,128)S(1)} %collective-permute-done.11.other_ref), custom_call_target="tpu_custom_call" | custom-call | tf_op jit(solution)/shard_map/solve/pallas_call | solution.py:378
  54.9 5.7 %filter.1 = f32[32,320,224]{2,1,0:T(8,128)} custom-call(bf16[10240,512]{1,0:T(8,128)(2,1)S(1)} %get-tuple-element.13.halves_ref, f32[4,320,256]{2,1,0:T(8,128)S(1)} %get-tuple-element.14.valid_ref, bf16[768,256]{1,0:T(8,128)(2,1)S(1)} %solve.1.weights_ref), custom_call_target="tpu_custom_call" | custom-call | flops 4026531840 | bytes 10485760 | tf_op jit(solution)/shard_map/filter/pallas_call | solution.py:405
  (5 shorter events, 0.1 us)
Async XLA Ops:
  0.0 0.7 %copy-start = (s32[4,40]{1,0:T(4,128)S(1)}, s32[4,40]{1,0:T(4,128)}, u32[]{:S(2)}) copy-start(s32[4,40]{1,0:T(4,128)} %mask_hbm.3) | copy-start | bytes 1924
  0.7 2.4 %copy-start.1 = (s32[4,40]{1,0:T(4,128)S(1)}, s32[4,40]{1,0:T(4,128)}, u32[]{:S(2)}) copy-start(s32[4,40]{1,0:T(4,128)} %mask_hbm.3) | copy-start | bytes 1924
  1.7 11.8 %collective-permute-start = (f32[320,256]{1,0:T(8,128)S(1)}, f32[320,256]{1,0:T(8,128)S(1)}, u32[]{:S(2)}, u32[]{:S(2)}) collective-permute-start(f32[320,256]{1,0:T(8,128)S(1)} %first_row.1), channel_id=1, source_target_pairs={{8,0},{16,8},{24,16},{32,24},{40,32},{48,40},{56,48},{64,56},{72,6... | collective-permute-start | bytes 983048 | tf_op jit(solution)/shard_map/ppermute | solution.py:453
  14.2 2.3 %collective-permute-start.1 = (f32[112,256]{1,0:T(8,128)S(1)}, f32[112,256]{1,0:T(8,128)S(1)}, u32[]{:S(2)}, u32[]{:S(2)}) collective-permute-start(f32[112,256]{1,0:T(8,128)S(1)} %get-tuple-element.20), channel_id=1, source_target_pairs={{0,1},{1,0},{2,3},{3,2},{4,5},{5,4},{6,7},{7,6},{8,9},{9,8},{10,11... | collective-permute-start | bytes 344072 | tf_op jit(solution)/shard_map/ppermute | solution.py:427
  16.6 6.3 %collective-permute-start.4 = (f32[112,256]{1,0:T(8,128)S(1)}, f32[112,256]{1,0:T(8,128)S(1)}, u32[]{:S(2)}, u32[]{:S(2)}) collective-permute-start(f32[112,256]{1,0:T(8,128)S(1)} %add.35), channel_id=1, source_target_pairs={{0,64},{1,17},{2,66},{3,19},{4,68},{5,21},{6,70},{7,23},{8,72},{9,... | collective-permute-start | bytes 344072 | tf_op jit(solution)/shard_map/ppermute | solution.py:427
  20.5 6.1 %collective-permute-start.3 = (f32[112,256]{1,0:T(8,128)S(1)}, f32[112,256]{1,0:T(8,128)S(1)}, u32[]{:S(2)}, u32[]{:S(2)}) collective-permute-start(f32[112,256]{1,0:T(8,128)S(1)} %add.35), channel_id=1, source_target_pairs={{0,96},{1,9},{2,98},{3,11},{4,100},{5,13},{6,102},{7,15},{8,104},{... | collective-permute-start | bytes 344072 | tf_op jit(solution)/shard_map/ppermute | solution.py:427
  22.9 4.9 %collective-permute-start.2 = (f32[112,256]{1,0:T(8,128)S(1)}, f32[112,256]{1,0:T(8,128)S(1)}, u32[]{:S(2)}, u32[]{:S(2)}) collective-permute-start(f32[112,256]{1,0:T(8,128)S(1)} %add.35), channel_id=1, source_target_pairs={{0,32},{1,25},{2,34},{3,27},{4,36},{5,29},{6,38},{7,31},{8,40},{9,... | collective-permute-start | bytes 344072 | tf_op jit(solution)/shard_map/ppermute | solution.py:427
  27.8 5.2 %collective-permute-start.7 = (f32[112,256]{1,0:T(8,128)S(1)}, f32[112,256]{1,0:T(8,128)S(1)}, u32[]{:S(2)}, u32[]{:S(2)}) collective-permute-start(f32[112,256]{1,0:T(8,128)S(1)} %add_add_fusion.2), channel_id=1, source_target_pairs={{0,16},{1,5},{2,18},{3,7},{4,20},{5,1},{6,22},{7,3},{8,24},{9,13},... | collective-permute-start | bytes 344072 | tf_op jit(solution)/shard_map/ppermute | solution.py:427
  30.6 3.7 %collective-permute-start.6 = (f32[112,256]{1,0:T(8,128)S(1)}, f32[112,256]{1,0:T(8,128)S(1)}, u32[]{:S(2)}, u32[]{:S(2)}) collective-permute-start(f32[112,256]{1,0:T(8,128)S(1)} %add_add_fusion.2), channel_id=1, source_target_pairs={{0,24},{1,3},{2,26},{3,1},{4,28},{5,7},{6,30},{7,5},{8,16},{9,11},... | collective-permute-start | bytes 344072 | tf_op jit(solution)/shard_map/ppermute | solution.py:427
  30.9 5.1 %collective-permute-start.5 = (f32[112,256]{1,0:T(8,128)S(1)}, f32[112,256]{1,0:T(8,128)S(1)}, u32[]{:S(2)}, u32[]{:S(2)}) collective-permute-start(f32[112,256]{1,0:T(8,128)S(1)} %add_add_fusion.2), channel_id=1, source_target_pairs={{0,8},{1,7},{2,10},{3,5},{4,12},{5,3},{6,14},{7,1},{8,0},{9,15},{1... | collective-permute-start | bytes 344072 | tf_op jit(solution)/shard_map/ppermute | solution.py:427
  36.1 5.4 %collective-permute-start.10 = (f32[112,256]{1,0:T(8,128)S(1)}, f32[112,256]{1,0:T(8,128)S(1)}, u32[]{:S(2)}, u32[]{:S(2)}) collective-permute-start(f32[112,256]{1,0:T(8,128)S(1)} %add_add_fusion.1), channel_id=1, source_target_pairs={{0,4},{1,65},{2,6},{3,67},{4,0},{5,69},{6,2},{7,71},{8,12},{9,73},... | collective-permute-start | bytes 344072 | tf_op jit(solution)/shard_map/ppermute | solution.py:427
  39.2 4.1 %collective-permute-start.9 = (f32[112,256]{1,0:T(8,128)S(1)}, f32[112,256]{1,0:T(8,128)S(1)}, u32[]{:S(2)}, u32[]{:S(2)}) collective-permute-start(f32[112,256]{1,0:T(8,128)S(1)} %add_add_fusion.1), channel_id=1, source_target_pairs={{0,6},{1,33},{2,4},{3,35},{4,2},{5,37},{6,0},{7,39},{8,14},{9,41},... | collective-permute-start | bytes 344072 | tf_op jit(solution)/shard_map/ppermute | solution.py:427
  39.7 4.9 %collective-permute-start.8 = (f32[112,256]{1,0:T(8,128)S(1)}, f32[112,256]{1,0:T(8,128)S(1)}, u32[]{:S(2)}, u32[]{:S(2)}) collective-permute-start(f32[112,256]{1,0:T(8,128)S(1)} %add_add_fusion.1), channel_id=1, source_target_pairs={{0,2},{1,97},{2,0},{3,99},{4,6},{5,101},{6,4},{7,103},{8,10},{9,10... | collective-permute-start | bytes 344072 | tf_op jit(solution)/shard_map/ppermute | solution.py:427
  44.5 3.6 %collective-permute-start.11 = (f32[112,256]{1,0:T(8,128)S(1)}, f32[112,256]{1,0:T(8,128)S(1)}, u32[]{:S(2)}, u32[]{:S(2)}) collective-permute-start(f32[112,256]{1,0:T(8,128)S(1)} %add_add_fusion.mine_ref), channel_id=1, source_target_pairs={{0,1},{1,0},{2,3},{3,2},{4,5},{5,4},{6,7},{7,6},{8,9},{9,8},{10,11... | collective-permute-start | bytes 344072 | tf_op jit(solution)/shard_map/ppermute | solution.py:427

commit v3 on v2

--- a/solution.py
+++ b/solution.py
@@ -279,6 +279,61 @@
     return jnp.sum(x * x)
 
 
+QUICK_STEPS = 7
+
+
+def careful(matrix, target, identity, row, column, bands, left, right):
+    start = 1.0 / jnp.max(jnp.sum(jnp.abs(matrix), 1, keepdims=True))
+    left[:W, :] = start * identity
+    left[W:, :] = identity - start * matrix
+
+    def more(carry):
+        count, size = carry
+        return (count < 24) & (size > 4e-6)
+
+    def squaring(carry):
+        count, _ = carry
+        new = dot3(left[...], left[W:, :])
+        left[:W, :] = left[:W, :] + new[:W]
+        left[W:, :] = new[W:]
+        return count + 1, square_sum(new[W:])
+
+    lax.while_loop(more, squaring, (0, jnp.float32(1e9)))
+    right[...] = dot3(left[:W, :], target)
+
+    def refining(carry):
+        count, _ = carry
+        residual = target - dot6(matrix, right[...])
+        change = dot3(left[:W, :], residual)
+        gain = right[...] + change
+        right[...] = gain
+        return count + 1, square_sum(change) / square_sum(gain)
+
+    def rough(carry):
+        count, size = carry
+        return (count < 8) & jnp.logical_not(size <= 1e-6)
+
+    _, size = lax.while_loop(rough, refining, (0, jnp.float32(1e9)))
+
+    @pl.when(jnp.logical_not(size <= 1e-6))
+    def _():
+        left[:W, :] = matrix
+        right[...] = target
+
+        def eliminate(k, _):
+            here = row[:, 0:1] == k
+            pivot_left = left[pl.ds(k, 1), :]
+            pivot_right = right[pl.ds(k, 1), :]
+            values = jnp.sum(jnp.where(column == k, left[:W, :], 0.0), 1, keepdims=True)
+            pivot = jnp.sum(jnp.where(here, values, 0.0))
+            factor = jnp.where(here, (values - 1.0) / pivot, values / pivot)
+            left[:W, :] = left[:W, :] - factor * pivot_left
+            right[...] = right[...] - factor * pivot_right
+            return 0
+
+        lax.fori_loop(0, bands, eliminate, 0)
+
+
 def solve_kernel(bands, core_ref, mine_ref, other_ref, weights_ref, left, right):
     core = core_ref[0]
     packed = jnp.concatenate([mine_ref[...], other_ref[...]], 0)
@@ -315,55 +370,29 @@
     matrix = jnp.where(inside, combined * scale_column * scale_row, identity)
     target = noise * scale_column * scale_row
 
-    start = 1.0 / jnp.max(jnp.sum(jnp.abs(matrix), 1, keepdims=True))
-    left[:W, :] = start * identity
-    left[W:, :] = identity - start * matrix
-
-    def more(carry):
-        count, size = carry
-        return (count < 24) & (size > 4e-6)
-
-    def squaring(carry):
-        count, _ = carry
-        new = dot3(left[...], left[W:, :])
-        left[:W, :] = left[:W, :] + new[:W]
-        left[W:, :] = new[W:]
-        return count + 1, square_sum(new[W:])
-
-    lax.while_loop(more, squaring, (0, jnp.float32(1e9)))
-    right[...] = dot3(left[:W, :], target)
-
-    def refining(carry):
-        count, _ = carry
-        residual = target - dot6(matrix, right[...])
-        change = dot3(left[:W, :], residual)
-        gain = right[...] + change
-        right[...] = gain
-        return count + 1, square_sum(change) / square_sum(gain)
-
-    def rough(carry):
-        count, size = carry
-        return (count < 8) & jnp.logical_not(size <= 1e-6)
-
-    _, size = lax.while_loop(rough, refining, (0, jnp.float32(1e9)))
-
-    @pl.when(jnp.logical_not(size <= 1e-6))
+    coarse = matrix.astype(BF16)
+    square = dot(coarse, coarse)
+    shrink = lax.rsqrt(jnp.max(jnp.sum(jnp.abs(square), 1, keepdims=True), 0, keepdims=True))
+    near = 2.0 * shrink * matrix - shrink * shrink * square
+    inverse = 2.0 * shrink * identity - shrink * shrink * matrix
+
+    def double(near, inverse):
+        step = dot(near.astype(BF16), jnp.concatenate([near.astype(BF16), inverse.astype(BF16)], 1))
+        return 2.0 * near - step[:, :W], 2.0 * inverse - step[:, W:]
+
+    for _ in range(QUICK_STEPS):
+        near, inverse = double(near, inverse)
+    off = identity - dot3(matrix, inverse)
+    inverse = inverse + dot(inverse.astype(BF16), off.astype(BF16))
+    first = dot3(inverse, target)
+    change = dot(inverse.astype(BF16), (target - dot3(matrix, first)).astype(BF16))
+    right[...] = first + change
+    off_size = square_sum(off)
+    done = square_sum(change) * off_size * off_size <= 1e-8 * square_sum(first)
+
+    @pl.when(jnp.logical_not(done & (off_size < 0.25)))
     def _():
-        left[:W, :] = matrix
-        right[...] = target
-
-        def eliminate(k, _):
-            here = row[:, 0:1] == k
-            pivot_left = left[pl.ds(k, 1), :]
-            pivot_right = right[pl.ds(k, 1), :]
-            values = jnp.sum(jnp.where(column == k, left[:W, :], 0.0), 1, keepdims=True)
-            pivot = jnp.sum(jnp.where(here, values, 0.0))
-            factor = jnp.where(here, (values - 1.0) / pivot, values / pivot)
-            left[:W, :] = left[:W, :] - factor * pivot_left
-            right[...] = right[...] - factor * pivot_right
-            return 0
-
-        lax.fori_loop(0, bands, eliminate, 0)
+        careful(matrix, target, identity, row, column, bands, left, right)
 
     gain = right[...] * scale_column * (1.0 / scale_row)
     shift = jnp.sum(jnp.where(row < bands, mean, 0.0) * gain, 0, keepdims=True)

time: 61 us -> 57.9 us (0.949)
  Pallas kernels: 24 us -> 21 us
    pallas_call x1, Pallas kernels: 6.77 us -> 3.75 us  [solve(): pl.pallas_call(functools.partial(solve_kernel, bands), out_shape=pltpu.VM...]
  transfers between devices with their start and end apart: 12 -> 12, of which waited for: 11 -> 11; matrix products, arithmetic and copies ran while one was open for 0% -> 0% of each run, Pallas kernels for 16% -> 17%
where the time goes in v3:
time: 57.9 us; the launch traced here: 57.8 us
  Pallas kernels  21 us (36%)
  starting transfers between devices  19 us (33%)
  waiting for transfers between devices  16.7 us (29%)
  local copies, waits for them, and re-layouts  0.68 us (1%)
    ppermute x11, starting transfers between devices, permute(): return lax.ppermute(x, ('track', 'strip'), pairs)  17.7 us
    ppermute x11, waiting for transfers between devices, permute(): return lax.ppermute(x, ('track', 'strip'), pairs)  16 us
    pallas_call x1, Pallas kernels, moments(): pl.pallas_call(moments_kernel, out_shape=[pltpu.VMEM((pixels, 2 * W), BF1...  9.76 us
    pallas_call x1, Pallas kernels, apply_filter(): pl.pallas_call(filter_kernel, out_shape=jax.ShapeDtypeStruct(shape, F32),...  5.7 us
    pallas_call x1, Pallas kernels, solve(): pl.pallas_call(functools.partial(solve_kernel, bands), out_shape=pltpu.VM...  3.75 us
    ppermute x1, starting transfers between devices, per_device(): lax.ppermute(first_row(mask, cube), 'track', [(i, i - 1) for i in range(1...  1.29 us
  transfers between devices with their start and end apart: 12, of which 11 were waited for; matrix products, arithmetic and copies ran while one was open for 0% of the time, Pallas kernels for 17%

profile of v3, /device:TPU:1, one launch (start us, length us, event | category | flops | bytes accessed | tf_op | source)
XLA Modules:
  0.0 57.8 jit_solution(3132829667331306015)
XLA Ops:
  0.0 0.0 copy-start
  0.0 0.7 %copy-done = s32[4,40]{1,0:T(4,128)S(1)} copy-done((s32[4,40]{1,0:T(4,128)S(1)}, s32[4,40]{1,0:T(4,128)}, u32[]{:S(2)}) %copy-start) | copy-done | bytes 664
  0.7 1.0 %first_row.1 = f32[320,256]{1,0:T(8,128)S(1)} custom-call(s32[4,40]{1,0:T(4,128)S(1)} %copy-done, f32[32,320,224]{2,1,0:T(8,128)} %cube_hbm.3), custom_call_target="tpu_custom_call" | custom-call | tf_op jit(solution)/shard_map/first_row/pallas_call | solution.py:89
  1.7 1.3 %collective-permute-start = (f32[320,256]{1,0:T(8,128)S(1)}, f32[320,256]{1,0:T(8,128)S(1)}, u32[]{:S(2)}, u32[]{:S(2)}) collective-permute-start(f32[320,256]{1,0:T(8,128)S(1)} %first_row.1), channel_id=1, source_target_pairs={{8,0},{16,8},{24,16},{32,24},{40,32},{48,40},{56,48},{64,56},{72,6... | collective-permute-start | bytes 983048 | tf_op jit(solution)/shard_map/ppermute | solution.py:482
  3.0 0.0 copy-done.1
  3.0 9.8 %moments.1 = (bf16[10240,512]{1,0:T(8,128)(2,1)S(1)}, f32[4,320,256]{2,1,0:T(8,128)S(1)}, f32[320,224]{1,0:T(8,128)S(1)}, f32[256,512]{1,0:T(8,128)S(1)}, f32[25...) custom-call(s32[4,40]{1,0:T(4,128)S(1)} %copy-done.1, f32[32,320,224]{2,1,0:T(8,128)} %cube_hbm.3), custom_call_target="tpu_custom_call" | custom-call | flops 5368709120 | bytes 10485760 | tf_op jit(solution)/shard_map/moments/pallas_call | solution.py:193
  12.8 0.7 %collective-permute-done.below_ref = f32[320,256]{1,0:T(8,128)S(1)} collective-permute-done((f32[320,256]{1,0:T(8,128)S(1)}, f32[320,256]{1,0:T(8,128)S(1)}, u32[]{:S(2)}, u32[]{:S(2)}) %collective-permute-start) | collective-permute-done | bytes 327712 | tf_op jit(solution)/shard_map/ppermute | solution.py:482
  13.5 0.7 %pack.1 = (f32[112,256]{1,0:T(8,128)S(1)}, f32[112,256]{1,0:T(8,128)S(1)}) custom-call(s32[1]{0:T(128)} %bitcast.core_ref, f32[4,320,256]{2,1,0:T(8,128)S(1)} %get-tuple-element.14.valid_ref, f32[320,224]{1,0:T(8,128)S(1)} %get-tuple-element.15.last_ref, f32[320,256]{1,0:T(8,128)S(1)} %collective-permute-done.below_ref, ...), custom_call_target="tpu_custom_call" | custom-call | tf_op jit(solution)/shard_map/pack/pallas_call | solution.py:267
  14.2 1.3 %collective-permute-start.1 = (f32[112,256]{1,0:T(8,128)S(1)}, f32[112,256]{1,0:T(8,128)S(1)}, u32[]{:S(2)}, u32[]{:S(2)}) collective-permute-start(f32[112,256]{1,0:T(8,128)S(1)} %get-tuple-element.20), channel_id=1, source_target_pairs={{0,1},{1,0},{2,3},{3,2},{4,5},{5,4},{6,7},{7,6},{8,9},{9,8},{10,11... | collective-permute-start | bytes 344072 | tf_op jit(solution)/shard_map/ppermute | solution.py:456
  15.6 1.0 %collective-permute-done.1 = f32[112,256]{1,0:T(8,128)S(1)} collective-permute-done((f32[112,256]{1,0:T(8,128)S(1)}, f32[112,256]{1,0:T(8,128)S(1)}, u32[]{:S(2)}, u32[]{:S(2)}) %collective-permute-start.1) | collective-permute-done | bytes 114720 | tf_op jit(solution)/shard_map/ppermute | solution.py:456
  16.6 4.0 %collective-permute-start.4 = (f32[112,256]{1,0:T(8,128)S(1)}, f32[112,256]{1,0:T(8,128)S(1)}, u32[]{:S(2)}, u32[]{:S(2)}) collective-permute-start(f32[112,256]{1,0:T(8,128)S(1)} %add.35), channel_id=1, source_target_pairs={{0,64},{1,17},{2,66},{3,19},{4,68},{5,21},{6,70},{7,23},{8,72},{9,... | collective-permute-start | bytes 344072 | tf_op jit(solution)/shard_map/ppermute | solution.py:456
  20.5 2.4 %collective-permute-start.3 = (f32[112,256]{1,0:T(8,128)S(1)}, f32[112,256]{1,0:T(8,128)S(1)}, u32[]{:S(2)}, u32[]{:S(2)}) collective-permute-start(f32[112,256]{1,0:T(8,128)S(1)} %add.35), channel_id=1, source_target_pairs={{0,96},{1,9},{2,98},{3,11},{4,100},{5,13},{6,102},{7,15},{8,104},{... | collective-permute-start | bytes 344072 | tf_op jit(solution)/shard_map/ppermute | solution.py:456
  22.9 0.0 collective-permute-start.2
  22.9 0.0 collective-permute-done.4
  22.9 3.7 %collective-permute-done.3 = f32[112,256]{1,0:T(8,128)S(1)} collective-permute-done((f32[112,256]{1,0:T(8,128)S(1)}, f32[112,256]{1,0:T(8,128)S(1)}, u32[]{:S(2)}, u32[]{:S(2)}) %collective-permute-start.3) | collective-permute-done | bytes 114720 | tf_op jit(solution)/shard_map/ppermute | solution.py:456
  26.6 1.2 %collective-permute-done.2 = f32[112,256]{1,0:T(8,128)S(1)} collective-permute-done((f32[112,256]{1,0:T(8,128)S(1)}, f32[112,256]{1,0:T(8,128)S(1)}, u32[]{:S(2)}, u32[]{:S(2)}) %collective-permute-start.2) | collective-permute-done | bytes 114720 | tf_op jit(solution)/shard_map/ppermute | solution.py:456
  27.8 2.8 %collective-permute-start.7 = (f32[112,256]{1,0:T(8,128)S(1)}, f32[112,256]{1,0:T(8,128)S(1)}, u32[]{:S(2)}, u32[]{:S(2)}) collective-permute-start(f32[112,256]{1,0:T(8,128)S(1)} %add_add_fusion.2), channel_id=1, source_target_pairs={{0,16},{1,5},{2,18},{3,7},{4,20},{5,1},{6,22},{7,3},{8,24},{9,13},... | collective-permute-start | bytes 344072 | tf_op jit(solution)/shard_map/ppermute | solution.py:456
  30.6 0.3 collective-permute-start.6
  30.9 0.5 collective-permute-start.5
  31.5 1.5 %collective-permute-done.7 = f32[112,256]{1,0:T(8,128)S(1)} collective-permute-done((f32[112,256]{1,0:T(8,128)S(1)}, f32[112,256]{1,0:T(8,128)S(1)}, u32[]{:S(2)}, u32[]{:S(2)}) %collective-permute-start.7) | collective-permute-done | bytes 114720 | tf_op jit(solution)/shard_map/ppermute | solution.py:456
  33.0 1.3 %collective-permute-done.6 = f32[112,256]{1,0:T(8,128)S(1)} collective-permute-done((f32[112,256]{1,0:T(8,128)S(1)}, f32[112,256]{1,0:T(8,128)S(1)}, u32[]{:S(2)}, u32[]{:S(2)}) %collective-permute-start.6) | collective-permute-done | bytes 114720 | tf_op jit(solution)/shard_map/ppermute | solution.py:456
  34.3 1.7 %collective-permute-done.5 = f32[112,256]{1,0:T(8,128)S(1)} collective-permute-done((f32[112,256]{1,0:T(8,128)S(1)}, f32[112,256]{1,0:T(8,128)S(1)}, u32[]{:S(2)}, u32[]{:S(2)}) %collective-permute-start.5) | collective-permute-done | bytes 114720 | tf_op jit(solution)/shard_map/ppermute | solution.py:456
  36.1 3.1 %collective-permute-start.10 = (f32[112,256]{1,0:T(8,128)S(1)}, f32[112,256]{1,0:T(8,128)S(1)}, u32[]{:S(2)}, u32[]{:S(2)}) collective-permute-start(f32[112,256]{1,0:T(8,128)S(1)} %add_add_fusion.1), channel_id=1, source_target_pairs={{0,4},{1,65},{2,6},{3,67},{4,0},{5,69},{6,2},{7,71},{8,12},{9,73},... | collective-permute-start | bytes 344072 | tf_op jit(solution)/shard_map/ppermute | solution.py:456
  39.2 0.4 collective-permute-start.9
  39.7 0.2 collective-permute-start.8
  39.8 1.7 %collective-permute-done.10 = f32[112,256]{1,0:T(8,128)S(1)} collective-permute-done((f32[112,256]{1,0:T(8,128)S(1)}, f32[112,256]{1,0:T(8,128)S(1)}, u32[]{:S(2)}, u32[]{:S(2)}) %collective-permute-start.10) | collective-permute-done | bytes 114720 | tf_op jit(solution)/shard_map/ppermute | solution.py:456
  41.5 1.8 %collective-permute-done.9 = f32[112,256]{1,0:T(8,128)S(1)} collective-permute-done((f32[112,256]{1,0:T(8,128)S(1)}, f32[112,256]{1,0:T(8,128)S(1)}, u32[]{:S(2)}, u32[]{:S(2)}) %collective-permute-start.9) | collective-permute-done | bytes 114720 | tf_op jit(solution)/shard_map/ppermute | solution.py:456
  43.4 1.2 %collective-permute-done.8 = f32[112,256]{1,0:T(8,128)S(1)} collective-permute-done((f32[112,256]{1,0:T(8,128)S(1)}, f32[112,256]{1,0:T(8,128)S(1)}, u32[]{:S(2)}, u32[]{:S(2)}) %collective-permute-start.8) | collective-permute-done | bytes 114720 | tf_op jit(solution)/shard_map/ppermute | solution.py:456
  44.5 2.7 %collective-permute-start.11 = (f32[112,256]{1,0:T(8,128)S(1)}, f32[112,256]{1,0:T(8,128)S(1)}, u32[]{:S(2)}, u32[]{:S(2)}) collective-permute-start(f32[112,256]{1,0:T(8,128)S(1)} %add_add_fusion.mine_ref), channel_id=1, source_target_pairs={{0,1},{1,0},{2,3},{3,2},{4,5},{5,4},{6,7},{7,6},{8,9},{9,8},{10,11... | collective-permute-start | bytes 344072 | tf_op jit(solution)/shard_map/ppermute | solution.py:456
  47.2 1.0 %collective-permute-done.11.other_ref = f32[112,256]{1,0:T(8,128)S(1)} collective-permute-done((f32[112,256]{1,0:T(8,128)S(1)}, f32[112,256]{1,0:T(8,128)S(1)}, u32[]{:S(2)}, u32[]{:S(2)}) %collective-permute-start.11) | collective-permute-done | bytes 114720 | tf_op jit(solution)/shard_map/ppermute | solution.py:456
  48.2 3.7 %solve.1.weights_ref = bf16[768,256]{1,0:T(8,128)(2,1)S(1)} custom-call(s32[1]{0:T(128)} %bitcast.core_ref, f32[112,256]{1,0:T(8,128)S(1)} %add_add_fusion.mine_ref, f32[112,256]{1,0:T(8,128)S(1)} %collective-permute-done.11.other_ref), custom_call_target="tpu_custom_call" | custom-call | tf_op jit(solution)/shard_map/solve/pallas_call | solution.py:407
  51.9 5.7 %filter.1 = f32[32,320,224]{2,1,0:T(8,128)} custom-call(bf16[10240,512]{1,0:T(8,128)(2,1)S(1)} %get-tuple-element.13.halves_ref, f32[4,320,256]{2,1,0:T(8,128)S(1)} %get-tuple-element.14.valid_ref, bf16[768,256]{1,0:T(8,128)(2,1)S(1)} %solve.1.weights_ref), custom_call_target="tpu_custom_call" | custom-call | flops 4026531840 | bytes 10485760 | tf_op jit(solution)/shard_map/filter/pallas_call | solution.py:434
  (5 shorter events, 0.1 us)
Async XLA Ops:
  0.0 0.7 %copy-start = (s32[4,40]{1,0:T(4,128)S(1)}, s32[4,40]{1,0:T(4,128)}, u32[]{:S(2)}) copy-start(s32[4,40]{1,0:T(4,128)} %mask_hbm.3) | copy-start | bytes 1924
  0.7 2.4 %copy-start.1 = (s32[4,40]{1,0:T(4,128)S(1)}, s32[4,40]{1,0:T(4,128)}, u32[]{:S(2)}) copy-start(s32[4,40]{1,0:T(4,128)} %mask_hbm.3) | copy-start | bytes 1924
  1.7 11.8 %collective-permute-start = (f32[320,256]{1,0:T(8,128)S(1)}, f32[320,256]{1,0:T(8,128)S(1)}, u32[]{:S(2)}, u32[]{:S(2)}) collective-permute-start(f32[320,256]{1,0:T(8,128)S(1)} %first_row.1), channel_id=1, source_target_pairs={{8,0},{16,8},{24,16},{32,24},{40,32},{48,40},{56,48},{64,56},{72,6... | collective-permute-start | bytes 983048 | tf_op jit(solution)/shard_map/ppermute | solution.py:482
  14.2 2.3 %collective-permute-start.1 = (f32[112,256]{1,0:T(8,128)S(1)}, f32[112,256]{1,0:T(8,128)S(1)}, u32[]{:S(2)}, u32[]{:S(2)}) collective-permute-start(f32[112,256]{1,0:T(8,128)S(1)} %get-tuple-element.20), channel_id=1, source_target_pairs={{0,1},{1,0},{2,3},{3,2},{4,5},{5,4},{6,7},{7,6},{8,9},{9,8},{10,11... | collective-permute-start | bytes 344072 | tf_op jit(solution)/shard_map/ppermute | solution.py:456
  16.6 6.3 %collective-permute-start.4 = (f32[112,256]{1,0:T(8,128)S(1)}, f32[112,256]{1,0:T(8,128)S(1)}, u32[]{:S(2)}, u32[]{:S(2)}) collective-permute-start(f32[112,256]{1,0:T(8,128)S(1)} %add.35), channel_id=1, source_target_pairs={{0,64},{1,17},{2,66},{3,19},{4,68},{5,21},{6,70},{7,23},{8,72},{9,... | collective-permute-start | bytes 344072 | tf_op jit(solution)/shard_map/ppermute | solution.py:456
  20.5 6.1 %collective-permute-start.3 = (f32[112,256]{1,0:T(8,128)S(1)}, f32[112,256]{1,0:T(8,128)S(1)}, u32[]{:S(2)}, u32[]{:S(2)}) collective-permute-start(f32[112,256]{1,0:T(8,128)S(1)} %add.35), channel_id=1, source_target_pairs={{0,96},{1,9},{2,98},{3,11},{4,100},{5,13},{6,102},{7,15},{8,104},{... | collective-permute-start | bytes 344072 | tf_op jit(solution)/shard_map/ppermute | solution.py:456
  22.9 4.9 %collective-permute-start.2 = (f32[112,256]{1,0:T(8,128)S(1)}, f32[112,256]{1,0:T(8,128)S(1)}, u32[]{:S(2)}, u32[]{:S(2)}) collective-permute-start(f32[112,256]{1,0:T(8,128)S(1)} %add.35), channel_id=1, source_target_pairs={{0,32},{1,25},{2,34},{3,27},{4,36},{5,29},{6,38},{7,31},{8,40},{9,... | collective-permute-start | bytes 344072 | tf_op jit(solution)/shard_map/ppermute | solution.py:456
  27.8 5.2 %collective-permute-start.7 = (f32[112,256]{1,0:T(8,128)S(1)}, f32[112,256]{1,0:T(8,128)S(1)}, u32[]{:S(2)}, u32[]{:S(2)}) collective-permute-start(f32[112,256]{1,0:T(8,128)S(1)} %add_add_fusion.2), channel_id=1, source_target_pairs={{0,16},{1,5},{2,18},{3,7},{4,20},{5,1},{6,22},{7,3},{8,24},{9,13},... | collective-permute-start | bytes 344072 | tf_op jit(solution)/shard_map/ppermute | solution.py:456
  30.6 3.7 %collective-permute-start.6 = (f32[112,256]{1,0:T(8,128)S(1)}, f32[112,256]{1,0:T(8,128)S(1)}, u32[]{:S(2)}, u32[]{:S(2)}) collective-permute-start(f32[112,256]{1,0:T(8,128)S(1)} %add_add_fusion.2), channel_id=1, source_target_pairs={{0,24},{1,3},{2,26},{3,1},{4,28},{5,7},{6,30},{7,5},{8,16},{9,11},... | collective-permute-start | bytes 344072 | tf_op jit(solution)/shard_map/ppermute | solution.py:456
  30.9 5.1 %collective-permute-start.5 = (f32[112,256]{1,0:T(8,128)S(1)}, f32[112,256]{1,0:T(8,128)S(1)}, u32[]{:S(2)}, u32[]{:S(2)}) collective-permute-start(f32[112,256]{1,0:T(8,128)S(1)} %add_add_fusion.2), channel_id=1, source_target_pairs={{0,8},{1,7},{2,10},{3,5},{4,12},{5,3},{6,14},{7,1},{8,0},{9,15},{1... | collective-permute-start | bytes 344072 | tf_op jit(solution)/shard_map/ppermute | solution.py:456
  36.1 5.4 %collective-permute-start.10 = (f32[112,256]{1,0:T(8,128)S(1)}, f32[112,256]{1,0:T(8,128)S(1)}, u32[]{:S(2)}, u32[]{:S(2)}) collective-permute-start(f32[112,256]{1,0:T(8,128)S(1)} %add_add_fusion.1), channel_id=1, source_target_pairs={{0,4},{1,65},{2,6},{3,67},{4,0},{5,69},{6,2},{7,71},{8,12},{9,73},... | collective-permute-start | bytes 344072 | tf_op jit(solution)/shard_map/ppermute | solution.py:456
  39.2 4.1 %collective-permute-start.9 = (f32[112,256]{1,0:T(8,128)S(1)}, f32[112,256]{1,0:T(8,128)S(1)}, u32[]{:S(2)}, u32[]{:S(2)}) collective-permute-start(f32[112,256]{1,0:T(8,128)S(1)} %add_add_fusion.1), channel_id=1, source_target_pairs={{0,6},{1,33},{2,4},{3,35},{4,2},{5,37},{6,0},{7,39},{8,14},{9,41},... | collective-permute-start | bytes 344072 | tf_op jit(solution)/shard_map/ppermute | solution.py:456
  39.7 4.9 %collective-permute-start.8 = (f32[112,256]{1,0:T(8,128)S(1)}, f32[112,256]{1,0:T(8,128)S(1)}, u32[]{:S(2)}, u32[]{:S(2)}) collective-permute-start(f32[112,256]{1,0:T(8,128)S(1)} %add_add_fusion.1), channel_id=1, source_target_pairs={{0,2},{1,97},{2,0},{3,99},{4,6},{5,101},{6,4},{7,103},{8,10},{9,10... | collective-permute-start | bytes 344072 | tf_op jit(solution)/shard_map/ppermute | solution.py:456
  44.5 3.6 %collective-permute-start.11 = (f32[112,256]{1,0:T(8,128)S(1)}, f32[112,256]{1,0:T(8,128)S(1)}, u32[]{:S(2)}, u32[]{:S(2)}) collective-permute-start(f32[112,256]{1,0:T(8,128)S(1)} %add_add_fusion.mine_ref), channel_id=1, source_target_pairs={{0,1},{1,0},{2,3},{3,2},{4,5},{5,4},{6,7},{7,6},{8,9},{9,8},{10,11... | collective-permute-start | bytes 344072 | tf_op jit(solution)/shard_map/ppermute | solution.py:456

commit v4 on v3

--- a/solution.py
+++ b/solution.py
@@ -70,35 +70,36 @@
         out_ref[c * TILE : (c + 1) * TILE, :] = jnp.full((TILE, out_ref.shape[1]), value, F32)
 
 
-def first_row_kernel(mask_hbm, cube_hbm, out_ref, mask, row, sems):
-    bands = row.shape[2]
-    copies = [
-        pltpu.make_async_copy(mask_hbm, mask, sems.at[0]),
-        pltpu.make_async_copy(cube_hbm.at[pl.ds(0, 1)], row, sems.at[1]),
-    ]
-    for copy in copies:
-        copy.start()
-    for copy in copies:
-        copy.wait()
-    fill_validity(mask, 0, out_ref)
-    out_ref[:, :bands] = row[0]
+def fetch_row_kernel(cube_hbm, row_ref, sem):
+    copy = pltpu.make_async_copy(cube_hbm.at[pl.ds(0, 1)], row_ref, sem)
+    copy.start()
+    copy.wait()
+
+
+def join_row_kernel(mask_ref, row_ref, out_ref):
+    fill_validity(mask_ref, 0, out_ref)
+    out_ref[:, : row_ref.shape[2]] = row_ref[0]
 
 
 def first_row(mask, cube):
     _, cols, bands = cube.shape
+    row = pl.pallas_call(
+        fetch_row_kernel,
+        out_shape=pltpu.VMEM((1, cols, bands), F32),
+        in_specs=[in_hbm()],
+        out_specs=in_vmem(),
+        scratch_shapes=[pltpu.SemaphoreType.DMA],
+        compiler_params=params(50),
+        name="fetch_row",
+    )(cube)
     return pl.pallas_call(
-        first_row_kernel,
+        join_row_kernel,
         out_shape=pltpu.VMEM((cols, W), F32),
-        in_specs=[in_hbm(), in_hbm()],
+        in_specs=[pl.BlockSpec(memory_space=pltpu.SMEM), in_vmem()],
         out_specs=in_vmem(),
-        scratch_shapes=[
-            pltpu.SMEM(mask.shape, jnp.int32),
-            pltpu.VMEM((1, cols, bands), F32),
-            pltpu.SemaphoreType.DMA((2,)),
-        ],
-        compiler_params=params(46),
-        name="first_row",
-    )(mask, cube)
+        compiler_params=params(12),
+        name="join_row",
+    )(mask, row)
 
 
 GROUP = 4
@@ -139,12 +140,8 @@
             total = total + parts[k]
         return squares + jnp.sum(total.astype(F32).reshape(2, 8, -1), 0)
 
-    def product(ref, buffer, half):
-        at = slice(half * W, (half + 1) * W)
-        ref[:, at] += dot_t(buffer[:, :W], buffer[:, at])
-
-    def products(halves, pairs):
-        return [(pixel_ref, halves, 0), (pixel_ref, halves, 1), (pair_ref, pairs, 0), (pair_ref, pairs, 1)]
+    def product(ref, buffer):
+        ref[...] += dot_t(buffer[:, :W], buffer[...])
 
     lane_halves = (slice(0, 128), slice(128, bands))
     squares = {(k, h): jnp.zeros((8, lanes.stop - lanes.start), F32) for k in range(2) for h, lanes in enumerate(lane_halves)}
@@ -157,7 +154,7 @@
         if within == 0:
             fill_validity(mask, tile_row, valid_ref.at[tile_row])
         for c in range(0, cols, BLOCK):
-            if pending:
+            if pending and c // BLOCK % 2 == 0:
                 product(*pending.pop(0))
             block = slice(c, c + BLOCK)
             valid = valid_ref[tile_row, block, :128]
@@ -178,7 +175,7 @@
                 last_ref[block, lanes] = previous
         for late in pending:
             product(*late)
-        pending = products(halves, pairs)
+        pending = [(pixel_ref, halves), (pair_ref, pairs)]
     for late in pending:
         product(*late)
     for k in range(2):

time: 57.9 us -> 57.3 us (0.990)
  local copies, waits for them, and re-layouts: 0.68 us -> 0.01 us
    unnamed x4 -> x2, local copies, waits for them, and re-layouts: 0.68 us -> 0.01 us
    ppermute x1, waiting for transfers between devices: 0.7 us -> 1.37 us  [per_device(): lax.ppermute(first_row(mask, cube), 'track', [(i, i - 1) for i in range(1...]
    pallas_call x1, Pallas kernels: 9.76 us -> 9.1 us  [moments(): pl.pallas_call(moments_kernel, out_shape=[pltpu.VMEM((pixels, 2 * W), BF1...]
    pallas_call x1 -> x2, Pallas kernels: 1.04 us -> 1.59 us  [the longest x1 0.99 us: first_row(): pl.pallas_call(fetch_row_kernel, out_shape=pltpu.VMEM((1, cols, bands), F...]
  transfers between devices with their start and end apart: 12 -> 12, of which waited for: 11 -> 11; matrix products, arithmetic and copies ran while one was open for 0% -> 0% of each run, Pallas kernels for 17% -> 16%
where the time goes in v4:
time: 57.3 us; the launch traced here: 57.2 us
  Pallas kernels  20.9 us (36%)
  starting transfers between devices  19 us (33%)
  waiting for transfers between devices  17 us (30%)
    ppermute x11, starting transfers between devices, permute(): return lax.ppermute(x, ('track', 'strip'), pairs)  17.7 us
    ppermute x11, waiting for transfers between devices, permute(): return lax.ppermute(x, ('track', 'strip'), pairs)  15.6 us
    pallas_call x1, Pallas kernels, moments(): pl.pallas_call(moments_kernel, out_shape=[pltpu.VMEM((pixels, 2 * W), BF1...  9.1 us
    pallas_call x1, Pallas kernels, apply_filter(): pl.pallas_call(filter_kernel, out_shape=jax.ShapeDtypeStruct(shape, F32),...  5.7 us
    pallas_call x1, Pallas kernels, solve(): pl.pallas_call(functools.partial(solve_kernel, bands), out_shape=pltpu.VM...  3.75 us
    ppermute x1, waiting for transfers between devices, per_device(): lax.ppermute(first_row(mask, cube), 'track', [(i, i - 1) for i in range(1...  1.37 us
    ppermute x1, starting transfers between devices, per_device(): lax.ppermute(first_row(mask, cube), 'track', [(i, i - 1) for i in range(1...  1.29 us
  transfers between devices with their start and end apart: 12, of which 11 were waited for; matrix products, arithmetic and copies ran while one was open for 0% of the time, Pallas kernels for 16%

profile of v4, /device:TPU:1, one launch (start us, length us, event | category | flops | bytes accessed | tf_op | source)
XLA Modules:
  0.0 57.2 jit_solution(14599896712719307968)
XLA Ops:
  0.0 0.0 copy-start
  0.0 1.0 %fetch_row.1.row_ref = f32[1,320,224]{2,1,0:T(8,128)S(1)} custom-call(f32[32,320,224]{2,1,0:T(8,128)} %cube_hbm.3), custom_call_target="tpu_custom_call" | custom-call | tf_op jit(solution)/shard_map/fetch_row/pallas_call | solution.py:86
  1.0 0.0 copy-done
  1.0 0.6 %join_row.1 = f32[320,256]{1,0:T(8,128)S(1)} custom-call(s32[4,40]{1,0:T(4,128)S(1)} %copy-done, f32[1,320,224]{2,1,0:T(8,128)S(1)} %fetch_row.1.row_ref), custom_call_target="tpu_custom_call" | custom-call | tf_op jit(solution)/shard_map/join_row/pallas_call | solution.py:95
  1.6 1.3 %collective-permute-start = (f32[320,256]{1,0:T(8,128)S(1)}, f32[320,256]{1,0:T(8,128)S(1)}, u32[]{:S(2)}, u32[]{:S(2)}) collective-permute-start(f32[320,256]{1,0:T(8,128)S(1)} %join_row.1), channel_id=1, source_target_pairs={{8,0},{16,8},{24,16},{32,24},{40,32},{48,40},{56,48},{64,56},{72,6... | collective-permute-start | bytes 983048 | tf_op jit(solution)/shard_map/ppermute | solution.py:479
  2.9 9.1 %moments.1 = (bf16[10240,512]{1,0:T(8,128)(2,1)S(1)}, f32[4,320,256]{2,1,0:T(8,128)S(1)}, f32[320,224]{1,0:T(8,128)S(1)}, f32[256,512]{1,0:T(8,128)S(1)}, f32[25...) custom-call(s32[4,40]{1,0:T(4,128)S(1)} %copy-done, f32[32,320,224]{2,1,0:T(8,128)} %cube_hbm.3), custom_call_target="tpu_custom_call" | custom-call | flops 5368709120 | bytes 10485760 | tf_op jit(solution)/shard_map/moments/pallas_call | solution.py:190
  12.0 1.4 %collective-permute-done.below_ref = f32[320,256]{1,0:T(8,128)S(1)} collective-permute-done((f32[320,256]{1,0:T(8,128)S(1)}, f32[320,256]{1,0:T(8,128)S(1)}, u32[]{:S(2)}, u32[]{:S(2)}) %collective-permute-start) | collective-permute-done | bytes 327712 | tf_op jit(solution)/shard_map/ppermute | solution.py:479
  13.4 0.7 %pack.1 = (f32[112,256]{1,0:T(8,128)S(1)}, f32[112,256]{1,0:T(8,128)S(1)}) custom-call(s32[1]{0:T(128)} %bitcast.core_ref, f32[4,320,256]{2,1,0:T(8,128)S(1)} %get-tuple-element.14.valid_ref, f32[320,224]{1,0:T(8,128)S(1)} %get-tuple-element.15.last_ref, f32[320,256]{1,0:T(8,128)S(1)} %collective-permute-done.below_ref, ...), custom_call_target="tpu_custom_call" | custom-call | tf_op jit(solution)/shard_map/pack/pallas_call | solution.py:264
  14.1 1.3 %collective-permute-start.1 = (f32[112,256]{1,0:T(8,128)S(1)}, f32[112,256]{1,0:T(8,128)S(1)}, u32[]{:S(2)}, u32[]{:S(2)}) collective-permute-start(f32[112,256]{1,0:T(8,128)S(1)} %get-tuple-element.20), channel_id=1, source_target_pairs={{0,1},{1,0},{2,3},{3,2},{4,5},{5,4},{6,7},{7,6},{8,9},{9,8},{10,11... | collective-permute-start | bytes 344072 | tf_op jit(solution)/shard_map/ppermute | solution.py:453
  15.5 1.0 %collective-permute-done.1 = f32[112,256]{1,0:T(8,128)S(1)} collective-permute-done((f32[112,256]{1,0:T(8,128)S(1)}, f32[112,256]{1,0:T(8,128)S(1)}, u32[]{:S(2)}, u32[]{:S(2)}) %collective-permute-start.1) | collective-permute-done | bytes 114720 | tf_op jit(solution)/shard_map/ppermute | solution.py:453
  16.5 3.5 %collective-permute-start.4 = (f32[112,256]{1,0:T(8,128)S(1)}, f32[112,256]{1,0:T(8,128)S(1)}, u32[]{:S(2)}, u32[]{:S(2)}) collective-permute-start(f32[112,256]{1,0:T(8,128)S(1)} %add.35), channel_id=1, source_target_pairs={{0,64},{1,17},{2,66},{3,19},{4,68},{5,21},{6,70},{7,23},{8,72},{9,... | collective-permute-start | bytes 344072 | tf_op jit(solution)/shard_map/ppermute | solution.py:453
  19.9 2.8 %collective-permute-start.3 = (f32[112,256]{1,0:T(8,128)S(1)}, f32[112,256]{1,0:T(8,128)S(1)}, u32[]{:S(2)}, u32[]{:S(2)}) collective-permute-start(f32[112,256]{1,0:T(8,128)S(1)} %add.35), channel_id=1, source_target_pairs={{0,96},{1,9},{2,98},{3,11},{4,100},{5,13},{6,102},{7,15},{8,104},{... | collective-permute-start | bytes 344072 | tf_op jit(solution)/shard_map/ppermute | solution.py:453
  22.8 0.0 collective-permute-start.2
  22.8 0.0 collective-permute-done.4
  22.8 3.4 %collective-permute-done.3 = f32[112,256]{1,0:T(8,128)S(1)} collective-permute-done((f32[112,256]{1,0:T(8,128)S(1)}, f32[112,256]{1,0:T(8,128)S(1)}, u32[]{:S(2)}, u32[]{:S(2)}) %collective-permute-start.3) | collective-permute-done | bytes 114720 | tf_op jit(solution)/shard_map/ppermute | solution.py:453
  26.2 1.7 %collective-permute-done.2 = f32[112,256]{1,0:T(8,128)S(1)} collective-permute-done((f32[112,256]{1,0:T(8,128)S(1)}, f32[112,256]{1,0:T(8,128)S(1)}, u32[]{:S(2)}, u32[]{:S(2)}) %collective-permute-start.2) | collective-permute-done | bytes 114720 | tf_op jit(solution)/shard_map/ppermute | solution.py:453
  28.0 2.8 %collective-permute-start.7 = (f32[112,256]{1,0:T(8,128)S(1)}, f32[112,256]{1,0:T(8,128)S(1)}, u32[]{:S(2)}, u32[]{:S(2)}) collective-permute-start(f32[112,256]{1,0:T(8,128)S(1)} %add_add_fusion.2), channel_id=1, source_target_pairs={{0,16},{1,5},{2,18},{3,7},{4,20},{5,1},{6,22},{7,3},{8,24},{9,13},... | collective-permute-start | bytes 344072 | tf_op jit(solution)/shard_map/ppermute | solution.py:453
  30.8 0.3 collective-permute-start.6
  31.1 0.6 collective-permute-start.5
  31.7 1.5 %collective-permute-done.7 = f32[112,256]{1,0:T(8,128)S(1)} collective-permute-done((f32[112,256]{1,0:T(8,128)S(1)}, f32[112,256]{1,0:T(8,128)S(1)}, u32[]{:S(2)}, u32[]{:S(2)}) %collective-permute-start.7) | collective-permute-done | bytes 114720 | tf_op jit(solution)/shard_map/ppermute | solution.py:453
  33.2 1.6 %collective-permute-done.6 = f32[112,256]{1,0:T(8,128)S(1)} collective-permute-done((f32[112,256]{1,0:T(8,128)S(1)}, f32[112,256]{1,0:T(8,128)S(1)}, u32[]{:S(2)}, u32[]{:S(2)}) %collective-permute-start.6) | collective-permute-done | bytes 114720 | tf_op jit(solution)/shard_map/ppermute | solution.py:453
  34.8 1.4 %collective-permute-done.5 = f32[112,256]{1,0:T(8,128)S(1)} collective-permute-done((f32[112,256]{1,0:T(8,128)S(1)}, f32[112,256]{1,0:T(8,128)S(1)}, u32[]{:S(2)}, u32[]{:S(2)}) %collective-permute-start.5) | collective-permute-done | bytes 114720 | tf_op jit(solution)/shard_map/ppermute | solution.py:453
  36.3 2.4 %collective-permute-start.10 = (f32[112,256]{1,0:T(8,128)S(1)}, f32[112,256]{1,0:T(8,128)S(1)}, u32[]{:S(2)}, u32[]{:S(2)}) collective-permute-start(f32[112,256]{1,0:T(8,128)S(1)} %add_add_fusion.1), channel_id=1, source_target_pairs={{0,4},{1,65},{2,6},{3,67},{4,0},{5,69},{6,2},{7,71},{8,12},{9,73},... | collective-permute-start | bytes 344072 | tf_op jit(solution)/shard_map/ppermute | solution.py:453
  38.7 0.0 collective-permute-start.9
  38.7 0.9 %collective-permute-start.8 = (f32[112,256]{1,0:T(8,128)S(1)}, f32[112,256]{1,0:T(8,128)S(1)}, u32[]{:S(2)}, u32[]{:S(2)}) collective-permute-start(f32[112,256]{1,0:T(8,128)S(1)} %add_add_fusion.1), channel_id=1, source_target_pairs={{0,2},{1,97},{2,0},{3,99},{4,6},{5,101},{6,4},{7,103},{8,10},{9,10... | collective-permute-start | bytes 344072 | tf_op jit(solution)/shard_map/ppermute | solution.py:453
  39.6 1.9 %collective-permute-done.10 = f32[112,256]{1,0:T(8,128)S(1)} collective-permute-done((f32[112,256]{1,0:T(8,128)S(1)}, f32[112,256]{1,0:T(8,128)S(1)}, u32[]{:S(2)}, u32[]{:S(2)}) %collective-permute-start.10) | collective-permute-done | bytes 114720 | tf_op jit(solution)/shard_map/ppermute | solution.py:453
  41.5 1.1 %collective-permute-done.9 = f32[112,256]{1,0:T(8,128)S(1)} collective-permute-done((f32[112,256]{1,0:T(8,128)S(1)}, f32[112,256]{1,0:T(8,128)S(1)}, u32[]{:S(2)}, u32[]{:S(2)}) %collective-permute-start.9) | collective-permute-done | bytes 114720 | tf_op jit(solution)/shard_map/ppermute | solution.py:453
  42.6 0.9 %collective-permute-done.8 = f32[112,256]{1,0:T(8,128)S(1)} collective-permute-done((f32[112,256]{1,0:T(8,128)S(1)}, f32[112,256]{1,0:T(8,128)S(1)}, u32[]{:S(2)}, u32[]{:S(2)}) %collective-permute-start.8) | collective-permute-done | bytes 114720 | tf_op jit(solution)/shard_map/ppermute | solution.py:453
  43.6 3.0 %collective-permute-start.11 = (f32[112,256]{1,0:T(8,128)S(1)}, f32[112,256]{1,0:T(8,128)S(1)}, u32[]{:S(2)}, u32[]{:S(2)}) collective-permute-start(f32[112,256]{1,0:T(8,128)S(1)} %add_add_fusion.mine_ref), channel_id=1, source_target_pairs={{0,1},{1,0},{2,3},{3,2},{4,5},{5,4},{6,7},{7,6},{8,9},{9,8},{10,11... | collective-permute-start | bytes 344072 | tf_op jit(solution)/shard_map/ppermute | solution.py:453
  46.6 1.0 %collective-permute-done.11.other_ref = f32[112,256]{1,0:T(8,128)S(1)} collective-permute-done((f32[112,256]{1,0:T(8,128)S(1)}, f32[112,256]{1,0:T(8,128)S(1)}, u32[]{:S(2)}, u32[]{:S(2)}) %collective-permute-start.11) | collective-permute-done | bytes 114720 | tf_op jit(solution)/shard_map/ppermute | solution.py:453
  47.5 3.8 %solve.1.weights_ref = bf16[768,256]{1,0:T(8,128)(2,1)S(1)} custom-call(s32[1]{0:T(128)} %bitcast.core_ref, f32[112,256]{1,0:T(8,128)S(1)} %add_add_fusion.mine_ref, f32[112,256]{1,0:T(8,128)S(1)} %collective-permute-done.11.other_ref), custom_call_target="tpu_custom_call" | custom-call | tf_op jit(solution)/shard_map/solve/pallas_call | solution.py:404
  51.3 5.7 %filter.1 = f32[32,320,224]{2,1,0:T(8,128)} custom-call(bf16[10240,512]{1,0:T(8,128)(2,1)S(1)} %get-tuple-element.13.halves_ref, f32[4,320,256]{2,1,0:T(8,128)S(1)} %get-tuple-element.14.valid_ref, bf16[768,256]{1,0:T(8,128)(2,1)S(1)} %solve.1.weights_ref), custom_call_target="tpu_custom_call" | custom-call | flops 4026531840 | bytes 10485760 | tf_op jit(solution)/shard_map/filter/pallas_call | solution.py:431
  (4 shorter events, 0.1 us)
Async XLA Ops:
  0.0 1.0 %copy-start = (s32[4,40]{1,0:T(4,128)S(1)}, s32[4,40]{1,0:T(4,128)}, u32[]{:S(2)}) copy-start(s32[4,40]{1,0:T(4,128)} %mask_ref.1) | copy-start | bytes 1924
  1.6 11.8 %collective-permute-start = (f32[320,256]{1,0:T(8,128)S(1)}, f32[320,256]{1,0:T(8,128)S(1)}, u32[]{:S(2)}, u32[]{:S(2)}) collective-permute-start(f32[320,256]{1,0:T(8,128)S(1)} %join_row.1), channel_id=1, source_target_pairs={{8,0},{16,8},{24,16},{32,24},{40,32},{48,40},{56,48},{64,56},{72,6... | collective-permute-start | bytes 983048 | tf_op jit(solution)/shard_map/ppermute | solution.py:479
  14.1 2.3 %collective-permute-start.1 = (f32[112,256]{1,0:T(8,128)S(1)}, f32[112,256]{1,0:T(8,128)S(1)}, u32[]{:S(2)}, u32[]{:S(2)}) collective-permute-start(f32[112,256]{1,0:T(8,128)S(1)} %get-tuple-element.20), channel_id=1, source_target_pairs={{0,1},{1,0},{2,3},{3,2},{4,5},{5,4},{6,7},{7,6},{8,9},{9,8},{10,11... | collective-permute-start | bytes 344072 | tf_op jit(solution)/shard_map/ppermute | solution.py:453
  16.5 6.3 %collective-permute-start.4 = (f32[112,256]{1,0:T(8,128)S(1)}, f32[112,256]{1,0:T(8,128)S(1)}, u32[]{:S(2)}, u32[]{:S(2)}) collective-permute-start(f32[112,256]{1,0:T(8,128)S(1)} %add.35), channel_id=1, source_target_pairs={{0,64},{1,17},{2,66},{3,19},{4,68},{5,21},{6,70},{7,23},{8,72},{9,... | collective-permute-start | bytes 344072 | tf_op jit(solution)/shard_map/ppermute | solution.py:453
  19.9 6.3 %collective-permute-start.3 = (f32[112,256]{1,0:T(8,128)S(1)}, f32[112,256]{1,0:T(8,128)S(1)}, u32[]{:S(2)}, u32[]{:S(2)}) collective-permute-start(f32[112,256]{1,0:T(8,128)S(1)} %add.35), channel_id=1, source_target_pairs={{0,96},{1,9},{2,98},{3,11},{4,100},{5,13},{6,102},{7,15},{8,104},{... | collective-permute-start | bytes 344072 | tf_op jit(solution)/shard_map/ppermute | solution.py:453
  22.8 5.1 %collective-permute-start.2 = (f32[112,256]{1,0:T(8,128)S(1)}, f32[112,256]{1,0:T(8,128)S(1)}, u32[]{:S(2)}, u32[]{:S(2)}) collective-permute-start(f32[112,256]{1,0:T(8,128)S(1)} %add.35), channel_id=1, source_target_pairs={{0,32},{1,25},{2,34},{3,27},{4,36},{5,29},{6,38},{7,31},{8,40},{9,... | collective-permute-start | bytes 344072 | tf_op jit(solution)/shard_map/ppermute | solution.py:453
  28.0 5.2 %collective-permute-start.7 = (f32[112,256]{1,0:T(8,128)S(1)}, f32[112,256]{1,0:T(8,128)S(1)}, u32[]{:S(2)}, u32[]{:S(2)}) collective-permute-start(f32[112,256]{1,0:T(8,128)S(1)} %add_add_fusion.2), channel_id=1, source_target_pairs={{0,16},{1,5},{2,18},{3,7},{4,20},{5,1},{6,22},{7,3},{8,24},{9,13},... | collective-permute-start | bytes 344072 | tf_op jit(solution)/shard_map/ppermute | solution.py:453
  30.8 4.0 %collective-permute-start.6 = (f32[112,256]{1,0:T(8,128)S(1)}, f32[112,256]{1,0:T(8,128)S(1)}, u32[]{:S(2)}, u32[]{:S(2)}) collective-permute-start(f32[112,256]{1,0:T(8,128)S(1)} %add_add_fusion.2), channel_id=1, source_target_pairs={{0,24},{1,3},{2,26},{3,1},{4,28},{5,7},{6,30},{7,5},{8,16},{9,11},... | collective-permute-start | bytes 344072 | tf_op jit(solution)/shard_map/ppermute | solution.py:453
  31.1 5.1 %collective-permute-start.5 = (f32[112,256]{1,0:T(8,128)S(1)}, f32[112,256]{1,0:T(8,128)S(1)}, u32[]{:S(2)}, u32[]{:S(2)}) collective-permute-start(f32[112,256]{1,0:T(8,128)S(1)} %add_add_fusion.2), channel_id=1, source_target_pairs={{0,8},{1,7},{2,10},{3,5},{4,12},{5,3},{6,14},{7,1},{8,0},{9,15},{1... | collective-permute-start | bytes 344072 | tf_op jit(solution)/shard_map/ppermute | solution.py:453
  36.3 5.2 %collective-permute-start.10 = (f32[112,256]{1,0:T(8,128)S(1)}, f32[112,256]{1,0:T(8,128)S(1)}, u32[]{:S(2)}, u32[]{:S(2)}) collective-permute-start(f32[112,256]{1,0:T(8,128)S(1)} %add_add_fusion.1), channel_id=1, source_target_pairs={{0,4},{1,65},{2,6},{3,67},{4,0},{5,69},{6,2},{7,71},{8,12},{9,73},... | collective-permute-start | bytes 344072 | tf_op jit(solution)/shard_map/ppermute | solution.py:453
  38.7 3.9 %collective-permute-start.9 = (f32[112,256]{1,0:T(8,128)S(1)}, f32[112,256]{1,0:T(8,128)S(1)}, u32[]{:S(2)}, u32[]{:S(2)}) collective-permute-start(f32[112,256]{1,0:T(8,128)S(1)} %add_add_fusion.1), channel_id=1, source_target_pairs={{0,6},{1,33},{2,4},{3,35},{4,2},{5,37},{6,0},{7,39},{8,14},{9,41},... | collective-permute-start | bytes 344072 | tf_op jit(solution)/shard_map/ppermute | solution.py:453
  38.7 4.9 %collective-permute-start.8 = (f32[112,256]{1,0:T(8,128)S(1)}, f32[112,256]{1,0:T(8,128)S(1)}, u32[]{:S(2)}, u32[]{:S(2)}) collective-permute-start(f32[112,256]{1,0:T(8,128)S(1)} %add_add_fusion.1), channel_id=1, source_target_pairs={{0,2},{1,97},{2,0},{3,99},{4,6},{5,101},{6,4},{7,103},{8,10},{9,10... | collective-permute-start | bytes 344072 | tf_op jit(solution)/shard_map/ppermute | solution.py:453
  43.6 4.0 %collective-permute-start.11 = (f32[112,256]{1,0:T(8,128)S(1)}, f32[112,256]{1,0:T(8,128)S(1)}, u32[]{:S(2)}, u32[]{:S(2)}) collective-permute-start(f32[112,256]{1,0:T(8,128)S(1)} %add_add_fusion.mine_ref), channel_id=1, source_target_pairs={{0,1},{1,0},{2,3},{3,2},{4,5},{5,4},{6,7},{7,6},{8,9},{9,8},{10,11... | collective-permute-start | bytes 344072 | tf_op jit(solution)/shard_map/ppermute | solution.py:453

commit v5 on v4

--- a/solution.py
+++ b/solution.py
@@ -102,30 +102,42 @@
     )(mask, row)
 
 
-GROUP = 4
+CUTS = ((0, 128), (128, 192))
 BLOCK = 64
+PIXEL_ONE, PAIR_ONE = 0, 1
+
+
+def one_in(lane, count, width):
+    return jnp.where(lax.broadcasted_iota(jnp.int32, (count, width), 1) == lane, 1.0, 0.0).astype(BF16)
 
 
 def moments_kernel(
-    mask_hbm, cube_hbm, halves_ref, valid_ref, last_ref, pixel_ref, pair_ref, rest_ref, mask, raw, pairs_a, pairs_b, sems
+    mask_hbm, cube_hbm, halves_ref, valid_ref, last_ref, sums_ref, steps_ref, seams_ref, rest_ref, mask, raw, between_a, between_b, sems
 ):
     rows, cols, bands = raw.shape
-    groups = rows // GROUP
+    groups = [(t, c0, width) for t in range(rows // TILE) for c0, width in CUTS]
 
     def fetch(g):
-        at = pl.ds(g * GROUP, GROUP)
+        t, c0, width = groups[g]
+        at = (pl.ds(t * TILE, TILE), pl.ds(c0, width))
         return pltpu.make_async_copy(cube_hbm.at[at], raw.at[at], sems.at[g])
 
-    mask_copy = pltpu.make_async_copy(mask_hbm, mask, sems.at[groups])
+    mask_copy = pltpu.make_async_copy(mask_hbm, mask, sems.at[len(groups)])
     mask_copy.start()
-    for g in range(groups):
+    for g in range(len(groups)):
         fetch(g).start()
-    pixel_ref[...] = jnp.zeros_like(pixel_ref)
-    pair_ref[...] = jnp.zeros_like(pair_ref)
-    for buffer in (halves_ref, pairs_a, pairs_b):
-        count = buffer.shape[0]
-        buffer[:, bands:W] = jnp.ones((count, W - bands), BF16)
-        buffer[:, W + bands :] = jnp.zeros((count, W - bands), BF16)
+    for ref in (sums_ref, steps_ref, seams_ref):
+        ref[...] = jnp.zeros_like(ref)
+    spare = W - bands
+    for t, c0, width in groups:
+        start = (t * cols + c0) * TILE
+        for i in range(TILE):
+            at = slice(start + i * width, start + (i + 1) * width)
+            halves_ref[at, bands:W] = one_in(i % 2, width, spare)
+            halves_ref[at, W + bands :] = jnp.zeros((width, spare), BF16)
+    for buffer in (between_a, between_b):
+        buffer[:, bands:W] = one_in(PAIR_ONE, buffer.shape[0], spare)
+        buffer[:, W + bands :] = jnp.zeros((buffer.shape[0], spare), BF16)
     mask_copy.wait()
 
     def put(value, buffer, at, lanes, squares):
@@ -140,45 +152,57 @@
             total = total + parts[k]
         return squares + jnp.sum(total.astype(F32).reshape(2, 8, -1), 0)
 
-    def product(ref, buffer):
-        ref[...] += dot_t(buffer[:, :W], buffer[...])
+    def product(ref, buffer, places, width):
+        value = jnp.concatenate([buffer[at : at + width, :] for at in places], 0)
+        ref[...] += dot_t(value[:, :W], value)
 
     lane_halves = (slice(0, 128), slice(128, bands))
-    squares = {(k, h): jnp.zeros((8, lanes.stop - lanes.start), F32) for k in range(2) for h, lanes in enumerate(lane_halves)}
+    squares = {(k, h): jnp.zeros((8, lanes.stop - lanes.start), F32) for k in range(3) for h, lanes in enumerate(lane_halves)}
     pending = []
-    for g in range(groups):
-        pairs = (pairs_a, pairs_b)[g % 2]
-        halves = halves_ref.at[pl.ds(g * GROUP * cols, GROUP * cols)]
+    for g, (t, c0, width) in enumerate(groups):
+        between = (between_a, between_b)[g % 2]
+        start = (t * cols + c0) * TILE
         fetch(g).wait()
-        tile_row, within = divmod(g * GROUP, TILE)
-        if within == 0:
-            fill_validity(mask, tile_row, valid_ref.at[tile_row])
-        for c in range(0, cols, BLOCK):
-            if pending and c // BLOCK % 2 == 0:
-                product(*pending.pop(0))
-            block = slice(c, c + BLOCK)
-            valid = valid_ref[tile_row, block, :128]
+        if c0 == 0:
+            fill_validity(mask, t, valid_ref.at[t])
+        gap = 1 if width == 128 else 2
+        slot = 0
+        for c in range(0, width, BLOCK):
+            block = slice(c0 + c, c0 + c + BLOCK)
+            valid = valid_ref[t, block, :128]
             for h, lanes in enumerate(lane_halves):
+                if pending and slot % gap == 0:
+                    product(*pending.pop(0))
+                slot += 1
                 weight = valid[:, : lanes.stop - lanes.start]
-                previous = last_ref[block, lanes] if g else None
-                for r in range(GROUP):
-                    pixel = raw[g * GROUP + r, block, lanes] * weight
+                previous = last_ref[block, lanes] if t else None
+                for i in range(TILE // 2):
+                    row = t * TILE + 2 * i
+                    first = raw[row, block, lanes] * weight
+                    second = raw[row + 1, block, lanes] * weight
                     if previous is None:
-                        difference = jnp.zeros_like(pixel)
+                        gone = jnp.zeros_like(first)
                     else:
-                        difference = pixel - previous
-                        if within == 0 and r == 0:
-                            difference = difference * (valid_ref[tile_row - 1, block, : weight.shape[1]] * weight)
-                    previous = pixel
-                    squares[0, h] = put(pixel, halves, r * cols + c, lanes, squares[0, h])
-                    squares[1, h] = put(difference, pairs, r * cols + c, lanes, squares[1, h])
+                        gone = first - previous
+                        if i == 0:
+                            gone = gone * (valid_ref[t - 1, block, : weight.shape[1]] * weight)
+                    previous = second
+                    at = start + 2 * i * width + c
+                    squares[0, h] = put(first + second, halves_ref, at, lanes, squares[0, h])
+                    squares[1, h] = put(second - first, halves_ref, at + width, lanes, squares[1, h])
+                    squares[2, h] = put(gone, between, i * width + c, lanes, squares[2, h])
                 last_ref[block, lanes] = previous
         for late in pending:
             product(*late)
-        pending = [(pixel_ref, halves), (pair_ref, pairs)]
+        pairs = range(TILE // 2)
+        pending = [
+            (sums_ref, halves_ref, [start + 2 * i * width for i in pairs], width),
+            (steps_ref, halves_ref, [start + (2 * i + 1) * width for i in pairs], width),
+            (seams_ref, between, [i * width for i in pairs], width),
+        ]
     for late in pending:
         product(*late)
-    for k in range(2):
+    for k in range(3):
         rest_ref[k, :, bands:] = jnp.zeros((8, W - bands), F32)
         for h, lanes in enumerate(lane_halves):
             rest_ref[k, :, lanes] = squares[k, h]
@@ -187,6 +211,7 @@
 def moments(mask, cube):
     rows, cols, bands = cube.shape
     pixels = rows * cols
+    widest = max(width for _, width in CUTS) * TILE // 2
     return pl.pallas_call(
         moments_kernel,
         out_shape=[
@@ -195,19 +220,20 @@
             pltpu.VMEM((cols, bands), F32),
             pltpu.VMEM((W, 2 * W), F32),
             pltpu.VMEM((W, 2 * W), F32),
-            pltpu.VMEM((2, 8, W), F32),
+            pltpu.VMEM((W, 2 * W), F32),
+            pltpu.VMEM((3, 8, W), F32),
         ],
         in_specs=[in_hbm(), in_hbm()],
-        out_specs=[in_vmem()] * 6,
+        out_specs=[in_vmem()] * 7,
         scratch_shapes=[
             pltpu.SMEM(mask.shape, jnp.int32),
             pltpu.VMEM(cube.shape, F32),
-            pltpu.VMEM((GROUP * cols, 2 * W), BF16),
-            pltpu.VMEM((GROUP * cols, 2 * W), BF16),
-            pltpu.SemaphoreType.DMA((rows // GROUP + 1,)),
+            pltpu.VMEM((widest, 2 * W), BF16),
+            pltpu.VMEM((widest, 2 * W), BF16),
+            pltpu.SemaphoreType.DMA((rows // TILE * len(CUTS) + 1,)),
         ],
         compiler_params=params(40),
-        cost_estimate=pl.CostEstimate(flops=4 * 2 * pixels * W * W, bytes_accessed=4 * pixels * W, transcendentals=0),
+        cost_estimate=pl.CostEstimate(flops=3 * 2 * pixels * W * W, bytes_accessed=4 * pixels * W, transcendentals=0),
         name="moments",
     )(mask, cube)
 
@@ -217,7 +243,7 @@
 
 
 def pack_kernel(
-    core_ref, valid_ref, last_ref, below_ref, pixel_ref, pair_ref, rest_ref, mine_ref, other_ref, packed, buffer
+    core_ref, valid_ref, last_ref, below_ref, sums_ref, steps_ref, seams_ref, rest_ref, mine_ref, other_ref, packed, buffer
 ):
     bands = last_ref.shape[1]
     half = bands // 2
@@ -228,28 +254,31 @@
     difference = (below_ref[:, :bands] - last_ref[...]) * weight[:, :bands]
     high, low = split(difference)
     rest = difference - high.astype(F32)
-    buffer[:, bands:W] = jnp.ones((buffer.shape[0], W - bands), BF16)
+    buffer[:, bands:W] = one_in(PAIR_ONE, buffer.shape[0], W - bands)
     buffer[:, W + bands :] = jnp.zeros((buffer.shape[0], W - bands), BF16)
     buffer[:, :bands] = high
     buffer[:, W : W + bands] = low
-    pairs = pair_ref[...] + dot_t(buffer[:, :W], buffer[...])
-    squares = jnp.sum(rest * rest, 0, keepdims=True)
+    steps = steps_ref[...]
+    seams = seams_ref[...] + dot_t(buffer[:, :W], buffer[...])
+    rests = [jnp.sum(rest_ref[k, :, :bands], 0, keepdims=True) for k in range(3)]
+    rests[2] = rests[2] + jnp.sum(rest * rest, 0, keepdims=True)
 
     def whole(parts, squares):
         mixed = parts[:, W:]
         squares = jnp.concatenate([squares, jnp.zeros((1, W - bands), F32)], 1)
         return parts[:, :W] + mixed + mixed.T + jnp.where(on_diagonal, squares, 0.0)
 
-    pixel = whole(pixel_ref[...], jnp.sum(rest_ref[0, :, :bands], 0, keepdims=True))
-    pair = whole(pairs, squares + jnp.sum(rest_ref[1, :, :bands], 0, keepdims=True))
+    pixel = whole(0.5 * (sums_ref[...] + steps), 0.5 * (rests[0] + rests[1]))
+    pixel = jnp.where(column == bands + PIXEL_ONE, 2.0 * pixel, pixel)
+    pair = whole(steps + seams, rests[1] + rests[2])
     valid = valid_ref[:, :, :128]
     inner = jnp.sum(valid, 0)
-    seams = jnp.sum(valid[1:] * valid[:-1], 0)
+    crossing = jnp.sum(valid[1:] * valid[:-1], 0)
     pixel_count = TILE * jnp.sum(inner, 0, keepdims=True)
-    pair_count = jnp.sum((TILE - 1) * inner + seams + weight[:, :128], 0, keepdims=True)
+    pair_count = jnp.sum((TILE - 1) * inner + crossing + weight[:, :128], 0, keepdims=True)
     out = jnp.where(column <= row, pair, 0.0)
     out = jnp.where((column > row) & (column <= bands + 1), pltpu.roll(pixel, 1, 1), out)
-    out = jnp.where(column == bands + 2, pltpu.roll(pair, 2, 1), out)
+    out = jnp.where(column == bands + 2, pltpu.roll(pair, 2 - PAIR_ONE, 1), out)
     counts = jnp.where(row == 0, pixel_count[:, :1], 0.0)
     counts = jnp.where(row == 1, pair_count[:, :1], counts)
     packed[...] = jnp.where(column == bands + 3, counts, out)
@@ -258,18 +287,18 @@
     other_ref[...] = packed[pl.ds(pl.multiple_of((1 - core) * half, 8), half), :]
 
 
-def pack(core, valid, last, below, pixel, pair, rest):
+def pack(core, valid, last, below, sums, steps, seams, rest):
     cols, bands = last.shape
     half = pltpu.VMEM((bands // 2, W), F32)
     return pl.pallas_call(
         pack_kernel,
         out_shape=[half, half],
-        in_specs=[pl.BlockSpec(memory_space=pltpu.SMEM)] + [in_vmem()] * 6,
+        in_specs=[pl.BlockSpec(memory_space=pltpu.SMEM)] + [in_vmem()] * 7,
         out_specs=[in_vmem()] * 2,
         scratch_shapes=[pltpu.VMEM((W, W), F32), pltpu.VMEM((cols, 2 * W), BF16)],
         compiler_params=params(12),
         name="pack",
-    )(core, valid, last, below, pixel, pair, rest)
+    )(core, valid, last, below, sums, steps, seams, rest)
 
 
 def square_sum(x):
@@ -393,7 +422,7 @@
 
     gain = right[...] * scale_column * (1.0 / scale_row)
     shift = jnp.sum(jnp.where(row < bands, mean, 0.0) * gain, 0, keepdims=True)
-    weights = jnp.where(row == bands, shift, jnp.where(inside, identity - gain, 0.0))
+    weights = jnp.where(row == bands + PIXEL_ONE, shift, jnp.where(inside, 0.5 * (identity - gain), 0.0))
     high, low = split(weights)
     weights_ref[:W, :] = high
     weights_ref[W : 2 * W, :] = high
@@ -415,12 +444,20 @@
 def filter_kernel(halves_ref, valid_ref, weights_ref, out_hbm, staged, sems):
     rows, cols, bands = staged.shape
     copies = []
-    for r in range(rows):
-        halves = halves_ref[r * cols : (r + 1) * cols, :]
-        result = dot(jnp.concatenate([halves, halves[:, :W]], 1), weights_ref[...])
-        staged[r] = valid_ref[r // TILE][:, :bands] * result[:, :bands]
-        copies.append(pltpu.make_async_copy(staged.at[pl.ds(r, 1)], out_hbm.at[pl.ds(r, 1)], sems.at[r]))
-        copies[-1].start()
+    for t in range(rows // TILE):
+        for c0, width in CUTS:
+            at = (t * cols + c0) * TILE
+            valid = valid_ref.at[t, c0 : c0 + width, :bands]
+            for i in range(TILE // 2):
+                halves = halves_ref[at + 2 * i * width : at + 2 * (i + 1) * width, :]
+                result = dot(jnp.concatenate([halves, halves[:, :W]], 1), weights_ref[...])
+                half_sum, half_step = result[:width, :bands], result[width:, :bands]
+                row = t * TILE + 2 * i
+                staged[row, c0 : c0 + width] = valid[...] * (half_sum - half_step)
+                staged[row + 1, c0 : c0 + width] = valid[...] * (half_sum + half_step)
+                part = (pl.ds(row, 2), pl.ds(c0, width))
+                copies.append(pltpu.make_async_copy(staged.at[part], out_hbm.at[part], sems.at[len(copies)]))
+                copies[-1].start()
     for copy in copies:
         copy.wait()
 
@@ -433,7 +470,7 @@
         out_shape=jax.ShapeDtypeStruct(shape, F32),
         in_specs=[in_vmem()] * 3,
         out_specs=in_hbm(),
-        scratch_shapes=[pltpu.VMEM(shape, F32), pltpu.SemaphoreType.DMA((rows,))],
+        scratch_shapes=[pltpu.VMEM(shape, F32), pltpu.SemaphoreType.DMA((rows // 2 * len(CUTS),))],
         compiler_params=params(24),
         cost_estimate=pl.CostEstimate(flops=3 * 2 * pixels * W * W, bytes_accessed=4 * pixels * W, transcendentals=0),
         name="filter",
@@ -478,8 +515,8 @@
     size = lax.axis_size("track")
     below = lax.ppermute(first_row(mask, cube), "track", [(i, i - 1) for i in range(1, size)])
     core = (lax.axis_index("strip") % 2).astype(jnp.int32)[None]
-    halves, valid, last, pixel, pair, rest = moments(mask, cube)
-    mine, other = pack(core, valid, last, below, pixel, pair, rest)
+    halves, valid, last, sums, steps, seams, rest = moments(mask, cube)
+    mine, other = pack(core, valid, last, below, sums, steps, seams, rest)
     total = mine + other_core(other)
     for axes in ((0, 1), (1, 2), (2, 0)):
         total = ring_sum(total, axes)

time: 57.3 us -> 57.4 us (level)
  Pallas kernels: 20.9 us -> 20 us
  waiting for transfers between devices: 17 us -> 17.9 us
    ppermute x1, waiting for transfers between devices: 1.37 us -> 2.42 us  [per_device(): lax.ppermute(first_row(mask, cube), 'track', [(i, i - 1) for i in range(1...]
    pallas_call x1, Pallas kernels: 9.1 us -> 8.05 us  [moments(): pl.pallas_call(moments_kernel, out_shape=[pltpu.VMEM((pixels, 2 * W), BF1...]
  transfers between devices with their start and end apart: 12 -> 12, of which waited for: 11 -> 11; matrix products, arithmetic and copies ran while one was open for 0% -> 0% of each run, Pallas kernels for 16% -> 14%
where the time goes in v5:
time: 57.4 us; the launch traced here: 57.3 us
  Pallas kernels  20 us (35%)
  starting transfers between devices  19 us (33%)
  waiting for transfers between devices  17.9 us (31%)
    ppermute x11, starting transfers between devices, permute(): return lax.ppermute(x, ('track', 'strip'), pairs)  17.8 us
    ppermute x11, waiting for transfers between devices, permute(): return lax.ppermute(x, ('track', 'strip'), pairs)  15.4 us
    pallas_call x1, Pallas kernels, moments(): pl.pallas_call(moments_kernel, out_shape=[pltpu.VMEM((pixels, 2 * W), BF1...  8.05 us
    pallas_call x1, Pallas kernels, apply_filter(): pl.pallas_call(filter_kernel, out_shape=jax.ShapeDtypeStruct(shape, F32),...  5.86 us
    pallas_call x1, Pallas kernels, solve(): pl.pallas_call(functools.partial(solve_kernel, bands), out_shape=pltpu.VM...  3.76 us
    ppermute x1, waiting for transfers between devices, per_device(): lax.ppermute(first_row(mask, cube), 'track', [(i, i - 1) for i in range(1...  2.42 us
    ppermute x1, starting transfers between devices, per_device(): lax.ppermute(first_row(mask, cube), 'track', [(i, i - 1) for i in range(1...  1.29 us
  transfers between devices with their start and end apart: 12, of which 11 were waited for; matrix products, arithmetic and copies ran while one was open for 0% of the time, Pallas kernels for 14%

profile of v5, /device:TPU:1, one launch (start us, length us, event | category | flops | bytes accessed | tf_op | source)
XLA Modules:
  0.0 57.3 jit_solution(17934888918020853858)
XLA Ops:
  0.0 0.0 copy-start
  0.0 1.0 %fetch_row.1.row_ref = f32[1,320,224]{2,1,0:T(8,128)S(1)} custom-call(f32[32,320,224]{2,1,0:T(8,128)} %cube_hbm.3), custom_call_target="tpu_custom_call" | custom-call | tf_op jit(solution)/shard_map/fetch_row/pallas_call | solution.py:86
  1.0 0.0 copy-done
  1.0 0.6 %join_row.1 = f32[320,256]{1,0:T(8,128)S(1)} custom-call(s32[4,40]{1,0:T(4,128)S(1)} %copy-done, f32[1,320,224]{2,1,0:T(8,128)S(1)} %fetch_row.1.row_ref), custom_call_target="tpu_custom_call" | custom-call | tf_op jit(solution)/shard_map/join_row/pallas_call | solution.py:95
  1.6 1.3 %collective-permute-start = (f32[320,256]{1,0:T(8,128)S(1)}, f32[320,256]{1,0:T(8,128)S(1)}, u32[]{:S(2)}, u32[]{:S(2)}) collective-permute-start(f32[320,256]{1,0:T(8,128)S(1)} %join_row.1), channel_id=1, source_target_pairs={{8,0},{16,8},{24,16},{32,24},{40,32},{48,40},{56,48},{64,56},{72,6... | collective-permute-start | bytes 983048 | tf_op jit(solution)/shard_map/ppermute | solution.py:516
  2.9 8.1 %moments.1 = (bf16[10240,512]{1,0:T(8,128)(2,1)S(1)}, f32[4,320,256]{2,1,0:T(8,128)S(1)}, f32[320,224]{1,0:T(8,128)S(1)}, f32[256,512]{1,0:T(8,128)S(1)}, f32[25...) custom-call(s32[4,40]{1,0:T(4,128)S(1)} %copy-done, f32[32,320,224]{2,1,0:T(8,128)} %cube_hbm.3), custom_call_target="tpu_custom_call" | custom-call | flops 4026531840 | bytes 10485760 | tf_op jit(solution)/shard_map/moments/pallas_call | solution.py:215
  11.0 2.4 %collective-permute-done.below_ref = f32[320,256]{1,0:T(8,128)S(1)} collective-permute-done((f32[320,256]{1,0:T(8,128)S(1)}, f32[320,256]{1,0:T(8,128)S(1)}, u32[]{:S(2)}, u32[]{:S(2)}) %collective-permute-start) | collective-permute-done | bytes 327712 | tf_op jit(solution)/shard_map/ppermute | solution.py:516
  13.4 0.7 %pack.1 = (f32[112,256]{1,0:T(8,128)S(1)}, f32[112,256]{1,0:T(8,128)S(1)}) custom-call(s32[1]{0:T(128)} %bitcast.core_ref, f32[4,320,256]{2,1,0:T(8,128)S(1)} %get-tuple-element.15.valid_ref, f32[320,224]{1,0:T(8,128)S(1)} %get-tuple-element.16.last_ref, f32[320,256]{1,0:T(8,128)S(1)} %collective-permute-done.below_ref, ...), custom_call_target="tpu_custom_call" | custom-call | tf_op jit(solution)/shard_map/pack/pallas_call | solution.py:293
  14.2 1.3 %collective-permute-start.1 = (f32[112,256]{1,0:T(8,128)S(1)}, f32[112,256]{1,0:T(8,128)S(1)}, u32[]{:S(2)}, u32[]{:S(2)}) collective-permute-start(f32[112,256]{1,0:T(8,128)S(1)} %get-tuple-element.22), channel_id=1, source_target_pairs={{0,1},{1,0},{2,3},{3,2},{4,5},{5,4},{6,7},{7,6},{8,9},{9,8},{10,11... | collective-permute-start | bytes 344072 | tf_op jit(solution)/shard_map/ppermute | solution.py:490
  15.5 1.0 %collective-permute-done.1 = f32[112,256]{1,0:T(8,128)S(1)} collective-permute-done((f32[112,256]{1,0:T(8,128)S(1)}, f32[112,256]{1,0:T(8,128)S(1)}, u32[]{:S(2)}, u32[]{:S(2)}) %collective-permute-start.1) | collective-permute-done | bytes 114720 | tf_op jit(solution)/shard_map/ppermute | solution.py:490
  16.5 3.5 %collective-permute-start.4 = (f32[112,256]{1,0:T(8,128)S(1)}, f32[112,256]{1,0:T(8,128)S(1)}, u32[]{:S(2)}, u32[]{:S(2)}) collective-permute-start(f32[112,256]{1,0:T(8,128)S(1)} %add.35), channel_id=1, source_target_pairs={{0,64},{1,17},{2,66},{3,19},{4,68},{5,21},{6,70},{7,23},{8,72},{9,... | collective-permute-start | bytes 344072 | tf_op jit(solution)/shard_map/ppermute | solution.py:490
  20.0 2.8 %collective-permute-start.3 = (f32[112,256]{1,0:T(8,128)S(1)}, f32[112,256]{1,0:T(8,128)S(1)}, u32[]{:S(2)}, u32[]{:S(2)}) collective-permute-start(f32[112,256]{1,0:T(8,128)S(1)} %add.35), channel_id=1, source_target_pairs={{0,96},{1,9},{2,98},{3,11},{4,100},{5,13},{6,102},{7,15},{8,104},{... | collective-permute-start | bytes 344072 | tf_op jit(solution)/shard_map/ppermute | solution.py:490
  22.8 0.0 collective-permute-start.2
  22.8 0.0 collective-permute-done.4
  22.8 3.4 %collective-permute-done.3 = f32[112,256]{1,0:T(8,128)S(1)} collective-permute-done((f32[112,256]{1,0:T(8,128)S(1)}, f32[112,256]{1,0:T(8,128)S(1)}, u32[]{:S(2)}, u32[]{:S(2)}) %collective-permute-start.3) | collective-permute-done | bytes 114720 | tf_op jit(solution)/shard_map/ppermute | solution.py:490
  26.2 1.7 %collective-permute-done.2 = f32[112,256]{1,0:T(8,128)S(1)} collective-permute-done((f32[112,256]{1,0:T(8,128)S(1)}, f32[112,256]{1,0:T(8,128)S(1)}, u32[]{:S(2)}, u32[]{:S(2)}) %collective-permute-start.2) | collective-permute-done | bytes 114720 | tf_op jit(solution)/shard_map/ppermute | solution.py:490
  28.0 2.8 %collective-permute-start.7 = (f32[112,256]{1,0:T(8,128)S(1)}, f32[112,256]{1,0:T(8,128)S(1)}, u32[]{:S(2)}, u32[]{:S(2)}) collective-permute-start(f32[112,256]{1,0:T(8,128)S(1)} %add_add_fusion.2), channel_id=1, source_target_pairs={{0,16},{1,5},{2,18},{3,7},{4,20},{5,1},{6,22},{7,3},{8,24},{9,13},... | collective-permute-start | bytes 344072 | tf_op jit(solution)/shard_map/ppermute | solution.py:490
  30.8 0.3 collective-permute-start.6
  31.1 0.6 collective-permute-start.5
  31.7 1.8 %collective-permute-done.7 = f32[112,256]{1,0:T(8,128)S(1)} collective-permute-done((f32[112,256]{1,0:T(8,128)S(1)}, f32[112,256]{1,0:T(8,128)S(1)}, u32[]{:S(2)}, u32[]{:S(2)}) %collective-permute-start.7) | collective-permute-done | bytes 114720 | tf_op jit(solution)/shard_map/ppermute | solution.py:490
  33.5 1.3 %collective-permute-done.6 = f32[112,256]{1,0:T(8,128)S(1)} collective-permute-done((f32[112,256]{1,0:T(8,128)S(1)}, f32[112,256]{1,0:T(8,128)S(1)}, u32[]{:S(2)}, u32[]{:S(2)}) %collective-permute-start.6) | collective-permute-done | bytes 114720 | tf_op jit(solution)/shard_map/ppermute | solution.py:490
  34.8 1.2 %collective-permute-done.5 = f32[112,256]{1,0:T(8,128)S(1)} collective-permute-done((f32[112,256]{1,0:T(8,128)S(1)}, f32[112,256]{1,0:T(8,128)S(1)}, u32[]{:S(2)}, u32[]{:S(2)}) %collective-permute-start.5) | collective-permute-done | bytes 114720 | tf_op jit(solution)/shard_map/ppermute | solution.py:490
  36.0 2.7 %collective-permute-start.10 = (f32[112,256]{1,0:T(8,128)S(1)}, f32[112,256]{1,0:T(8,128)S(1)}, u32[]{:S(2)}, u32[]{:S(2)}) collective-permute-start(f32[112,256]{1,0:T(8,128)S(1)} %add_add_fusion.1), channel_id=1, source_target_pairs={{0,4},{1,65},{2,6},{3,67},{4,0},{5,69},{6,2},{7,71},{8,12},{9,73},... | collective-permute-start | bytes 344072 | tf_op jit(solution)/shard_map/ppermute | solution.py:490
  38.7 0.0 collective-permute-start.9
  38.7 0.8 %collective-permute-start.8 = (f32[112,256]{1,0:T(8,128)S(1)}, f32[112,256]{1,0:T(8,128)S(1)}, u32[]{:S(2)}, u32[]{:S(2)}) collective-permute-start(f32[112,256]{1,0:T(8,128)S(1)} %add_add_fusion.1), channel_id=1, source_target_pairs={{0,2},{1,97},{2,0},{3,99},{4,6},{5,101},{6,4},{7,103},{8,10},{9,10... | collective-permute-start | bytes 344072 | tf_op jit(solution)/shard_map/ppermute | solution.py:490
  39.5 1.7 %collective-permute-done.10 = f32[112,256]{1,0:T(8,128)S(1)} collective-permute-done((f32[112,256]{1,0:T(8,128)S(1)}, f32[112,256]{1,0:T(8,128)S(1)}, u32[]{:S(2)}, u32[]{:S(2)}) %collective-permute-start.10) | collective-permute-done | bytes 114720 | tf_op jit(solution)/shard_map/ppermute | solution.py:490
  41.2 1.4 %collective-permute-done.9 = f32[112,256]{1,0:T(8,128)S(1)} collective-permute-done((f32[112,256]{1,0:T(8,128)S(1)}, f32[112,256]{1,0:T(8,128)S(1)}, u32[]{:S(2)}, u32[]{:S(2)}) %collective-permute-start.9) | collective-permute-done | bytes 114720 | tf_op jit(solution)/shard_map/ppermute | solution.py:490
  42.7 0.9 %collective-permute-done.8 = f32[112,256]{1,0:T(8,128)S(1)} collective-permute-done((f32[112,256]{1,0:T(8,128)S(1)}, f32[112,256]{1,0:T(8,128)S(1)}, u32[]{:S(2)}, u32[]{:S(2)}) %collective-permute-start.8) | collective-permute-done | bytes 114720 | tf_op jit(solution)/shard_map/ppermute | solution.py:490
  43.6 2.9 %collective-permute-start.11 = (f32[112,256]{1,0:T(8,128)S(1)}, f32[112,256]{1,0:T(8,128)S(1)}, u32[]{:S(2)}, u32[]{:S(2)}) collective-permute-start(f32[112,256]{1,0:T(8,128)S(1)} %add_add_fusion.mine_ref), channel_id=1, source_target_pairs={{0,1},{1,0},{2,3},{3,2},{4,5},{5,4},{6,7},{7,6},{8,9},{9,8},{10,11... | collective-permute-start | bytes 344072 | tf_op jit(solution)/shard_map/ppermute | solution.py:490
  46.5 1.0 %collective-permute-done.11.other_ref = f32[112,256]{1,0:T(8,128)S(1)} collective-permute-done((f32[112,256]{1,0:T(8,128)S(1)}, f32[112,256]{1,0:T(8,128)S(1)}, u32[]{:S(2)}, u32[]{:S(2)}) %collective-permute-start.11) | collective-permute-done | bytes 114720 | tf_op jit(solution)/shard_map/ppermute | solution.py:490
  47.5 3.8 %solve.1.weights_ref = bf16[768,256]{1,0:T(8,128)(2,1)S(1)} custom-call(s32[1]{0:T(128)} %bitcast.core_ref, f32[112,256]{1,0:T(8,128)S(1)} %add_add_fusion.mine_ref, f32[112,256]{1,0:T(8,128)S(1)} %collective-permute-done.11.other_ref), custom_call_target="tpu_custom_call" | custom-call | tf_op jit(solution)/shard_map/solve/pallas_call | solution.py:433
  51.3 5.9 %filter.1 = f32[32,320,224]{2,1,0:T(8,128)} custom-call(bf16[10240,512]{1,0:T(8,128)(2,1)S(1)} %get-tuple-element.14.halves_ref, f32[4,320,256]{2,1,0:T(8,128)S(1)} %get-tuple-element.15.valid_ref, bf16[768,256]{1,0:T(8,128)(2,1)S(1)} %solve.1.weights_ref), custom_call_target="tpu_custom_call" | custom-call | flops 4026531840 | bytes 10485760 | tf_op jit(solution)/shard_map/filter/pallas_call | solution.py:468
  (4 shorter events, 0.1 us)
Async XLA Ops:
  0.0 1.0 %copy-start = (s32[4,40]{1,0:T(4,128)S(1)}, s32[4,40]{1,0:T(4,128)}, u32[]{:S(2)}) copy-start(s32[4,40]{1,0:T(4,128)} %mask_ref.1) | copy-start | bytes 1924
  1.6 11.8 %collective-permute-start = (f32[320,256]{1,0:T(8,128)S(1)}, f32[320,256]{1,0:T(8,128)S(1)}, u32[]{:S(2)}, u32[]{:S(2)}) collective-permute-start(f32[320,256]{1,0:T(8,128)S(1)} %join_row.1), channel_id=1, source_target_pairs={{8,0},{16,8},{24,16},{32,24},{40,32},{48,40},{56,48},{64,56},{72,6... | collective-permute-start | bytes 983048 | tf_op jit(solution)/shard_map/ppermute | solution.py:516
  14.2 2.3 %collective-permute-start.1 = (f32[112,256]{1,0:T(8,128)S(1)}, f32[112,256]{1,0:T(8,128)S(1)}, u32[]{:S(2)}, u32[]{:S(2)}) collective-permute-start(f32[112,256]{1,0:T(8,128)S(1)} %get-tuple-element.22), channel_id=1, source_target_pairs={{0,1},{1,0},{2,3},{3,2},{4,5},{5,4},{6,7},{7,6},{8,9},{9,8},{10,11... | collective-permute-start | bytes 344072 | tf_op jit(solution)/shard_map/ppermute | solution.py:490
  16.5 6.3 %collective-permute-start.4 = (f32[112,256]{1,0:T(8,128)S(1)}, f32[112,256]{1,0:T(8,128)S(1)}, u32[]{:S(2)}, u32[]{:S(2)}) collective-permute-start(f32[112,256]{1,0:T(8,128)S(1)} %add.35), channel_id=1, source_target_pairs={{0,64},{1,17},{2,66},{3,19},{4,68},{5,21},{6,70},{7,23},{8,72},{9,... | collective-permute-start | bytes 344072 | tf_op jit(solution)/shard_map/ppermute | solution.py:490
  20.0 6.3 %collective-permute-start.3 = (f32[112,256]{1,0:T(8,128)S(1)}, f32[112,256]{1,0:T(8,128)S(1)}, u32[]{:S(2)}, u32[]{:S(2)}) collective-permute-start(f32[112,256]{1,0:T(8,128)S(1)} %add.35), channel_id=1, source_target_pairs={{0,96},{1,9},{2,98},{3,11},{4,100},{5,13},{6,102},{7,15},{8,104},{... | collective-permute-start | bytes 344072 | tf_op jit(solution)/shard_map/ppermute | solution.py:490
  22.8 5.1 %collective-permute-start.2 = (f32[112,256]{1,0:T(8,128)S(1)}, f32[112,256]{1,0:T(8,128)S(1)}, u32[]{:S(2)}, u32[]{:S(2)}) collective-permute-start(f32[112,256]{1,0:T(8,128)S(1)} %add.35), channel_id=1, source_target_pairs={{0,32},{1,25},{2,34},{3,27},{4,36},{5,29},{6,38},{7,31},{8,40},{9,... | collective-permute-start | bytes 344072 | tf_op jit(solution)/shard_map/ppermute | solution.py:490
  28.0 5.5 %collective-permute-start.7 = (f32[112,256]{1,0:T(8,128)S(1)}, f32[112,256]{1,0:T(8,128)S(1)}, u32[]{:S(2)}, u32[]{:S(2)}) collective-permute-start(f32[112,256]{1,0:T(8,128)S(1)} %add_add_fusion.2), channel_id=1, source_target_pairs={{0,16},{1,5},{2,18},{3,7},{4,20},{5,1},{6,22},{7,3},{8,24},{9,13},... | collective-permute-start | bytes 344072 | tf_op jit(solution)/shard_map/ppermute | solution.py:490
  30.8 4.0 %collective-permute-start.6 = (f32[112,256]{1,0:T(8,128)S(1)}, f32[112,256]{1,0:T(8,128)S(1)}, u32[]{:S(2)}, u32[]{:S(2)}) collective-permute-start(f32[112,256]{1,0:T(8,128)S(1)} %add_add_fusion.2), channel_id=1, source_target_pairs={{0,24},{1,3},{2,26},{3,1},{4,28},{5,7},{6,30},{7,5},{8,16},{9,11},... | collective-permute-start | bytes 344072 | tf_op jit(solution)/shard_map/ppermute | solution.py:490
  31.1 4.9 %collective-permute-start.5 = (f32[112,256]{1,0:T(8,128)S(1)}, f32[112,256]{1,0:T(8,128)S(1)}, u32[]{:S(2)}, u32[]{:S(2)}) collective-permute-start(f32[112,256]{1,0:T(8,128)S(1)} %add_add_fusion.2), channel_id=1, source_target_pairs={{0,8},{1,7},{2,10},{3,5},{4,12},{5,3},{6,14},{7,1},{8,0},{9,15},{1... | collective-permute-start | bytes 344072 | tf_op jit(solution)/shard_map/ppermute | solution.py:490
  36.0 5.2 %collective-permute-start.10 = (f32[112,256]{1,0:T(8,128)S(1)}, f32[112,256]{1,0:T(8,128)S(1)}, u32[]{:S(2)}, u32[]{:S(2)}) collective-permute-start(f32[112,256]{1,0:T(8,128)S(1)} %add_add_fusion.1), channel_id=1, source_target_pairs={{0,4},{1,65},{2,6},{3,67},{4,0},{5,69},{6,2},{7,71},{8,12},{9,73},... | collective-permute-start | bytes 344072 | tf_op jit(solution)/shard_map/ppermute | solution.py:490
  38.7 3.9 %collective-permute-start.9 = (f32[112,256]{1,0:T(8,128)S(1)}, f32[112,256]{1,0:T(8,128)S(1)}, u32[]{:S(2)}, u32[]{:S(2)}) collective-permute-start(f32[112,256]{1,0:T(8,128)S(1)} %add_add_fusion.1), channel_id=1, source_target_pairs={{0,6},{1,33},{2,4},{3,35},{4,2},{5,37},{6,0},{7,39},{8,14},{9,41},... | collective-permute-start | bytes 344072 | tf_op jit(solution)/shard_map/ppermute | solution.py:490
  38.7 4.9 %collective-permute-start.8 = (f32[112,256]{1,0:T(8,128)S(1)}, f32[112,256]{1,0:T(8,128)S(1)}, u32[]{:S(2)}, u32[]{:S(2)}) collective-permute-start(f32[112,256]{1,0:T(8,128)S(1)} %add_add_fusion.1), channel_id=1, source_target_pairs={{0,2},{1,97},{2,0},{3,99},{4,6},{5,101},{6,4},{7,103},{8,10},{9,10... | collective-permute-start | bytes 344072 | tf_op jit(solution)/shard_map/ppermute | solution.py:490
  43.6 3.9 %collective-permute-start.11 = (f32[112,256]{1,0:T(8,128)S(1)}, f32[112,256]{1,0:T(8,128)S(1)}, u32[]{:S(2)}, u32[]{:S(2)}) collective-permute-start(f32[112,256]{1,0:T(8,128)S(1)} %add_add_fusion.mine_ref), channel_id=1, source_target_pairs={{0,1},{1,0},{2,3},{3,2},{4,5},{5,4},{6,7},{7,6},{8,9},{9,8},{10,11... | collective-permute-start | bytes 344072 | tf_op jit(solution)/shard_map/ppermute | solution.py:490

commit v6 on v5

--- a/solution.py
+++ b/solution.py
@@ -71,17 +71,17 @@
 
 
 def fetch_row_kernel(cube_hbm, row_ref, sem):
-    copy = pltpu.make_async_copy(cube_hbm.at[pl.ds(0, 1)], row_ref, sem)
+    copy = pltpu.make_async_copy(cube_hbm.at[pl.ds(cube_hbm.shape[0] - 1, 1)], row_ref, sem)
     copy.start()
     copy.wait()
 
 
 def join_row_kernel(mask_ref, row_ref, out_ref):
-    fill_validity(mask_ref, 0, out_ref)
+    fill_validity(mask_ref, mask_ref.shape[0] - 1, out_ref)
     out_ref[:, : row_ref.shape[2]] = row_ref[0]
 
 
-def first_row(mask, cube):
+def final_row(mask, cube):
     _, cols, bands = cube.shape
     row = pl.pallas_call(
         fetch_row_kernel,
@@ -112,7 +112,7 @@
 
 
 def moments_kernel(
-    mask_hbm, cube_hbm, halves_ref, valid_ref, last_ref, sums_ref, steps_ref, seams_ref, rest_ref, mask, raw, between_a, between_b, sems
+    mask_hbm, cube_hbm, halves_ref, valid_ref, first_ref, sums_ref, steps_ref, seams_ref, rest_ref, mask, raw, last, between_a, between_b, sems
 ):
     rows, cols, bands = raw.shape
     groups = [(t, c0, width) for t in range(rows // TILE) for c0, width in CUTS]
@@ -175,12 +175,13 @@
                     product(*pending.pop(0))
                 slot += 1
                 weight = valid[:, : lanes.stop - lanes.start]
-                previous = last_ref[block, lanes] if t else None
+                previous = last[block, lanes] if t else None
                 for i in range(TILE // 2):
                     row = t * TILE + 2 * i
                     first = raw[row, block, lanes] * weight
                     second = raw[row + 1, block, lanes] * weight
                     if previous is None:
+                        first_ref[block, lanes] = first
                         gone = jnp.zeros_like(first)
                     else:
                         gone = first - previous
@@ -191,7 +192,7 @@
                     squares[0, h] = put(first + second, halves_ref, at, lanes, squares[0, h])
                     squares[1, h] = put(second - first, halves_ref, at + width, lanes, squares[1, h])
                     squares[2, h] = put(gone, between, i * width + c, lanes, squares[2, h])
-                last_ref[block, lanes] = previous
+                last[block, lanes] = previous
         for late in pending:
             product(*late)
         pairs = range(TILE // 2)
@@ -228,6 +229,7 @@
         scratch_shapes=[
             pltpu.SMEM(mask.shape, jnp.int32),
             pltpu.VMEM(cube.shape, F32),
+            pltpu.VMEM((cols, bands), F32),
             pltpu.VMEM((widest, 2 * W), BF16),
             pltpu.VMEM((widest, 2 * W), BF16),
             pltpu.SemaphoreType.DMA((rows // TILE * len(CUTS) + 1,)),
@@ -243,15 +245,15 @@
 
 
 def pack_kernel(
-    core_ref, valid_ref, last_ref, below_ref, sums_ref, steps_ref, seams_ref, rest_ref, mine_ref, other_ref, packed, buffer
+    core_ref, valid_ref, first_ref, above_ref, sums_ref, steps_ref, seams_ref, rest_ref, mine_ref, other_ref, packed, buffer
 ):
-    bands = last_ref.shape[1]
+    bands = first_ref.shape[1]
     half = bands // 2
     row, column = indices((W, W))
     on_diagonal = row == column
-    last_valid = valid_ref[valid_ref.shape[0] - 1]
-    weight = last_valid * jnp.broadcast_to(below_ref[:, bands : bands + 1], last_valid.shape)
-    difference = (below_ref[:, :bands] - last_ref[...]) * weight[:, :bands]
+    first_valid = valid_ref[0]
+    weight = first_valid * jnp.broadcast_to(above_ref[:, bands : bands + 1], first_valid.shape)
+    difference = (first_ref[...] - above_ref[:, :bands]) * weight[:, :bands]
     high, low = split(difference)
     rest = difference - high.astype(F32)
     buffer[:, bands:W] = one_in(PAIR_ONE, buffer.shape[0], W - bands)
@@ -287,8 +289,8 @@
     other_ref[...] = packed[pl.ds(pl.multiple_of((1 - core) * half, 8), half), :]
 
 
-def pack(core, valid, last, below, sums, steps, seams, rest):
-    cols, bands = last.shape
+def pack(core, valid, first, above, sums, steps, seams, rest):
+    cols, bands = first.shape
     half = pltpu.VMEM((bands // 2, W), F32)
     return pl.pallas_call(
         pack_kernel,
@@ -298,7 +300,7 @@
         scratch_shapes=[pltpu.VMEM((W, W), F32), pltpu.VMEM((cols, 2 * W), BF16)],
         compiler_params=params(12),
         name="pack",
-    )(core, valid, last, below, sums, steps, seams, rest)
+    )(core, valid, first, above, sums, steps, seams, rest)
 
 
 def square_sum(x):
@@ -513,10 +515,10 @@
 def per_device(cube, mask):
     bands = cube.shape[2]
     size = lax.axis_size("track")
-    below = lax.ppermute(first_row(mask, cube), "track", [(i, i - 1) for i in range(1, size)])
+    above = lax.ppermute(final_row(mask, cube), "track", [(i, i + 1) for i in range(size - 1)])
     core = (lax.axis_index("strip") % 2).astype(jnp.int32)[None]
-    halves, valid, last, sums, steps, seams, rest = moments(mask, cube)
-    mine, other = pack(core, valid, last, below, sums, steps, seams, rest)
+    halves, valid, first, sums, steps, seams, rest = moments(mask, cube)
+    mine, other = pack(core, valid, first, above, sums, steps, seams, rest)
     total = mine + other_core(other)
     for axes in ((0, 1), (1, 2), (2, 0)):
         total = ring_sum(total, axes)

time: 57.4 us -> 56.6 us (0.986)
  waiting for transfers between devices: 17.9 us -> 15.9 us
  starting transfers between devices: 19 us -> 20.2 us
    ppermute x1, starting transfers between devices: 1.29 us -> 4.39 us  [per_device(): lax.ppermute(final_row(mask, cube), 'track', [(i, i + 1) for i in range(s...]
    ppermute x1, waiting for transfers between devices: 2.42 us -> 0.01 us  [per_device(): lax.ppermute(final_row(mask, cube), 'track', [(i, i + 1) for i in range(s...]
    ppermute x11, starting transfers between devices: 17.8 us -> 15.8 us  [permute(): return lax.ppermute(x, ('track', 'strip'), pairs)]
where the time goes in v6:
time: 56.6 us; the launch traced here: 56.4 us
  starting transfers between devices  20.2 us (36%)
  Pallas kernels  20 us (35%)
  waiting for transfers between devices  15.9 us (28%)
    ppermute x11, waiting for transfers between devices, permute(): return lax.ppermute(x, ('track', 'strip'), pairs)  15.9 us
    ppermute x11, starting transfers between devices, permute(): return lax.ppermute(x, ('track', 'strip'), pairs)  15.8 us
    pallas_call x1, Pallas kernels, moments(): pl.pallas_call(moments_kernel, out_shape=[pltpu.VMEM((pixels, 2 * W), BF1...  8.08 us
    pallas_call x1, Pallas kernels, apply_filter(): pl.pallas_call(filter_kernel, out_shape=jax.ShapeDtypeStruct(shape, F32),...  5.86 us
    ppermute x1, starting transfers between devices, per_device(): lax.ppermute(final_row(mask, cube), 'track', [(i, i + 1) for i in range(s...  4.39 us
    pallas_call x1, Pallas kernels, solve(): pl.pallas_call(functools.partial(solve_kernel, bands), out_shape=pltpu.VM...  3.76 us
  transfers between devices with their start and end apart: 12, of which 11 were waited for; matrix products, arithmetic and copies ran while one was open for 0% of the time, Pallas kernels for 14%

profile of v6, /device:TPU:1, one launch (start us, length us, event | category | flops | bytes accessed | tf_op | source)
XLA Modules:
  0.0 56.4 jit_solution(16795988667687612982)
XLA Ops:
  0.0 0.0 copy-start
  0.0 1.0 %fetch_row.1.row_ref = f32[1,320,224]{2,1,0:T(8,128)S(1)} custom-call(f32[32,320,224]{2,1,0:T(8,128)} %cube_hbm.3), custom_call_target="tpu_custom_call" | custom-call | tf_op jit(solution)/shard_map/fetch_row/pallas_call | solution.py:86
  1.0 0.0 copy-done
  1.0 0.6 %join_row.1 = f32[320,256]{1,0:T(8,128)S(1)} custom-call(s32[4,40]{1,0:T(4,128)S(1)} %copy-done, f32[1,320,224]{2,1,0:T(8,128)S(1)} %fetch_row.1.row_ref), custom_call_target="tpu_custom_call" | custom-call | tf_op jit(solution)/shard_map/join_row/pallas_call | solution.py:95
  1.6 4.4 %collective-permute-start = (f32[320,256]{1,0:T(8,128)S(1)}, f32[320,256]{1,0:T(8,128)S(1)}, u32[]{:S(2)}, u32[]{:S(2)}) collective-permute-start(f32[320,256]{1,0:T(8,128)S(1)} %join_row.1), channel_id=1, source_target_pairs={{0,8},{8,16},{16,24},{24,32},{32,40},{40,48},{48,56},{56,64},{64,7... | collective-permute-start | bytes 983048 | tf_op jit(solution)/shard_map/ppermute | solution.py:518
  6.0 8.1 %moments.1 = (bf16[10240,512]{1,0:T(8,128)(2,1)S(1)}, f32[4,320,256]{2,1,0:T(8,128)S(1)}, f32[320,224]{1,0:T(8,128)S(1)}, f32[256,512]{1,0:T(8,128)S(1)}, f32[25...) custom-call(s32[4,40]{1,0:T(4,128)S(1)} %copy-done, f32[32,320,224]{2,1,0:T(8,128)} %cube_hbm.3), custom_call_target="tpu_custom_call" | custom-call | flops 4026531840 | bytes 10485760 | tf_op jit(solution)/shard_map/moments/pallas_call | solution.py:216
  14.1 0.0 collective-permute-done.above_ref
  14.1 0.8 %pack.1 = (f32[112,256]{1,0:T(8,128)S(1)}, f32[112,256]{1,0:T(8,128)S(1)}) custom-call(s32[1]{0:T(128)} %bitcast.core_ref, f32[4,320,256]{2,1,0:T(8,128)S(1)} %get-tuple-element.15.valid_ref, f32[320,224]{1,0:T(8,128)S(1)} %get-tuple-element.16.first_ref, f32[320,256]{1,0:T(8,128)S(1)} %collective-permute-done.above_ref, ...), custom_call_target="tpu_custom_call" | custom-call | tf_op jit(solution)/shard_map/pack/pallas_call | solution.py:295
  14.9 1.0 %collective-permute-start.1 = (f32[112,256]{1,0:T(8,128)S(1)}, f32[112,256]{1,0:T(8,128)S(1)}, u32[]{:S(2)}, u32[]{:S(2)}) collective-permute-start(f32[112,256]{1,0:T(8,128)S(1)} %get-tuple-element.22), channel_id=1, source_target_pairs={{0,1},{1,0},{2,3},{3,2},{4,5},{5,4},{6,7},{7,6},{8,9},{9,8},{10,11... | collective-permute-start | bytes 344072 | tf_op jit(solution)/shard_map/ppermute | solution.py:492
  15.9 1.0 %collective-permute-done.1 = f32[112,256]{1,0:T(8,128)S(1)} collective-permute-done((f32[112,256]{1,0:T(8,128)S(1)}, f32[112,256]{1,0:T(8,128)S(1)}, u32[]{:S(2)}, u32[]{:S(2)}) %collective-permute-start.1) | collective-permute-done | bytes 114720 | tf_op jit(solution)/shard_map/ppermute | solution.py:492
  16.9 3.4 %collective-permute-start.4 = (f32[112,256]{1,0:T(8,128)S(1)}, f32[112,256]{1,0:T(8,128)S(1)}, u32[]{:S(2)}, u32[]{:S(2)}) collective-permute-start(f32[112,256]{1,0:T(8,128)S(1)} %add.35), channel_id=1, source_target_pairs={{0,64},{1,17},{2,66},{3,19},{4,68},{5,21},{6,70},{7,23},{8,72},{9,... | collective-permute-start | bytes 344072 | tf_op jit(solution)/shard_map/ppermute | solution.py:492
  20.3 0.4 collective-permute-start.3
  20.7 0.3 collective-permute-start.2
  21.0 1.5 %collective-permute-done.4 = f32[112,256]{1,0:T(8,128)S(1)} collective-permute-done((f32[112,256]{1,0:T(8,128)S(1)}, f32[112,256]{1,0:T(8,128)S(1)}, u32[]{:S(2)}, u32[]{:S(2)}) %collective-permute-start.4) | collective-permute-done | bytes 114720 | tf_op jit(solution)/shard_map/ppermute | solution.py:492
  22.5 2.0 %collective-permute-done.3 = f32[112,256]{1,0:T(8,128)S(1)} collective-permute-done((f32[112,256]{1,0:T(8,128)S(1)}, f32[112,256]{1,0:T(8,128)S(1)}, u32[]{:S(2)}, u32[]{:S(2)}) %collective-permute-start.3) | collective-permute-done | bytes 114720 | tf_op jit(solution)/shard_map/ppermute | solution.py:492
  24.4 1.2 %collective-permute-done.2 = f32[112,256]{1,0:T(8,128)S(1)} collective-permute-done((f32[112,256]{1,0:T(8,128)S(1)}, f32[112,256]{1,0:T(8,128)S(1)}, u32[]{:S(2)}, u32[]{:S(2)}) %collective-permute-start.2) | collective-permute-done | bytes 114720 | tf_op jit(solution)/shard_map/ppermute | solution.py:492
  25.6 2.8 %collective-permute-start.7 = (f32[112,256]{1,0:T(8,128)S(1)}, f32[112,256]{1,0:T(8,128)S(1)}, u32[]{:S(2)}, u32[]{:S(2)}) collective-permute-start(f32[112,256]{1,0:T(8,128)S(1)} %add_add_fusion.2), channel_id=1, source_target_pairs={{0,16},{1,5},{2,18},{3,7},{4,20},{5,1},{6,22},{7,3},{8,24},{9,13},... | collective-permute-start | bytes 344072 | tf_op jit(solution)/shard_map/ppermute | solution.py:492
  28.4 0.3 collective-permute-start.6
  28.7 0.6 collective-permute-start.5
  29.3 1.5 %collective-permute-done.7 = f32[112,256]{1,0:T(8,128)S(1)} collective-permute-done((f32[112,256]{1,0:T(8,128)S(1)}, f32[112,256]{1,0:T(8,128)S(1)}, u32[]{:S(2)}, u32[]{:S(2)}) %collective-permute-start.7) | collective-permute-done | bytes 114720 | tf_op jit(solution)/shard_map/ppermute | solution.py:492
  30.8 1.3 %collective-permute-done.6 = f32[112,256]{1,0:T(8,128)S(1)} collective-permute-done((f32[112,256]{1,0:T(8,128)S(1)}, f32[112,256]{1,0:T(8,128)S(1)}, u32[]{:S(2)}, u32[]{:S(2)}) %collective-permute-start.6) | collective-permute-done | bytes 114720 | tf_op jit(solution)/shard_map/ppermute | solution.py:492
  32.1 1.7 %collective-permute-done.5 = f32[112,256]{1,0:T(8,128)S(1)} collective-permute-done((f32[112,256]{1,0:T(8,128)S(1)}, f32[112,256]{1,0:T(8,128)S(1)}, u32[]{:S(2)}, u32[]{:S(2)}) %collective-permute-start.5) | collective-permute-done | bytes 114720 | tf_op jit(solution)/shard_map/ppermute | solution.py:492
  33.9 3.0 %collective-permute-start.10 = (f32[112,256]{1,0:T(8,128)S(1)}, f32[112,256]{1,0:T(8,128)S(1)}, u32[]{:S(2)}, u32[]{:S(2)}) collective-permute-start(f32[112,256]{1,0:T(8,128)S(1)} %add_add_fusion.1), channel_id=1, source_target_pairs={{0,4},{1,65},{2,6},{3,67},{4,0},{5,69},{6,2},{7,71},{8,12},{9,73},... | collective-permute-start | bytes 344072 | tf_op jit(solution)/shard_map/ppermute | solution.py:492
  36.9 0.7 %collective-permute-start.9 = (f32[112,256]{1,0:T(8,128)S(1)}, f32[112,256]{1,0:T(8,128)S(1)}, u32[]{:S(2)}, u32[]{:S(2)}) collective-permute-start(f32[112,256]{1,0:T(8,128)S(1)} %add_add_fusion.1), channel_id=1, source_target_pairs={{0,6},{1,33},{2,4},{3,35},{4,2},{5,37},{6,0},{7,39},{8,14},{9,41},... | collective-permute-start | bytes 344072 | tf_op jit(solution)/shard_map/ppermute | solution.py:492
  37.6 0.1 collective-permute-start.8
  37.7 1.5 %collective-permute-done.10 = f32[112,256]{1,0:T(8,128)S(1)} collective-permute-done((f32[112,256]{1,0:T(8,128)S(1)}, f32[112,256]{1,0:T(8,128)S(1)}, u32[]{:S(2)}, u32[]{:S(2)}) %collective-permute-start.10) | collective-permute-done | bytes 114720 | tf_op jit(solution)/shard_map/ppermute | solution.py:492
  39.1 2.2 %collective-permute-done.9 = f32[112,256]{1,0:T(8,128)S(1)} collective-permute-done((f32[112,256]{1,0:T(8,128)S(1)}, f32[112,256]{1,0:T(8,128)S(1)}, u32[]{:S(2)}, u32[]{:S(2)}) %collective-permute-start.9) | collective-permute-done | bytes 114720 | tf_op jit(solution)/shard_map/ppermute | solution.py:492
  41.3 1.2 %collective-permute-done.8 = f32[112,256]{1,0:T(8,128)S(1)} collective-permute-done((f32[112,256]{1,0:T(8,128)S(1)}, f32[112,256]{1,0:T(8,128)S(1)}, u32[]{:S(2)}, u32[]{:S(2)}) %collective-permute-start.8) | collective-permute-done | bytes 114720 | tf_op jit(solution)/shard_map/ppermute | solution.py:492
  42.5 3.2 %collective-permute-start.11 = (f32[112,256]{1,0:T(8,128)S(1)}, f32[112,256]{1,0:T(8,128)S(1)}, u32[]{:S(2)}, u32[]{:S(2)}) collective-permute-start(f32[112,256]{1,0:T(8,128)S(1)} %add_add_fusion.mine_ref), channel_id=1, source_target_pairs={{0,1},{1,0},{2,3},{3,2},{4,5},{5,4},{6,7},{7,6},{8,9},{9,8},{10,11... | collective-permute-start | bytes 344072 | tf_op jit(solution)/shard_map/ppermute | solution.py:492
  45.7 1.0 %collective-permute-done.11.other_ref = f32[112,256]{1,0:T(8,128)S(1)} collective-permute-done((f32[112,256]{1,0:T(8,128)S(1)}, f32[112,256]{1,0:T(8,128)S(1)}, u32[]{:S(2)}, u32[]{:S(2)}) %collective-permute-start.11) | collective-permute-done | bytes 114720 | tf_op jit(solution)/shard_map/ppermute | solution.py:492
  46.6 3.8 %solve.1.weights_ref = bf16[768,256]{1,0:T(8,128)(2,1)S(1)} custom-call(s32[1]{0:T(128)} %bitcast.core_ref, f32[112,256]{1,0:T(8,128)S(1)} %add_add_fusion.mine_ref, f32[112,256]{1,0:T(8,128)S(1)} %collective-permute-done.11.other_ref), custom_call_target="tpu_custom_call" | custom-call | tf_op jit(solution)/shard_map/solve/pallas_call | solution.py:435
  50.4 5.9 %filter.1 = f32[32,320,224]{2,1,0:T(8,128)} custom-call(bf16[10240,512]{1,0:T(8,128)(2,1)S(1)} %get-tuple-element.14.halves_ref, f32[4,320,256]{2,1,0:T(8,128)S(1)} %get-tuple-element.15.valid_ref, bf16[768,256]{1,0:T(8,128)(2,1)S(1)} %solve.1.weights_ref), custom_call_target="tpu_custom_call" | custom-call | flops 4026531840 | bytes 10485760 | tf_op jit(solution)/shard_map/filter/pallas_call | solution.py:470
  (4 shorter events, 0.1 us)
Async XLA Ops:
  0.0 1.0 %copy-start = (s32[4,40]{1,0:T(4,128)S(1)}, s32[4,40]{1,0:T(4,128)}, u32[]{:S(2)}) copy-start(s32[4,40]{1,0:T(4,128)} %mask_ref.1) | copy-start | bytes 1924
  1.6 12.5 %collective-permute-start = (f32[320,256]{1,0:T(8,128)S(1)}, f32[320,256]{1,0:T(8,128)S(1)}, u32[]{:S(2)}, u32[]{:S(2)}) collective-permute-start(f32[320,256]{1,0:T(8,128)S(1)} %join_row.1), channel_id=1, source_target_pairs={{0,8},{8,16},{16,24},{24,32},{32,40},{40,48},{48,56},{56,64},{64,7... | collective-permute-start | bytes 983048 | tf_op jit(solution)/shard_map/ppermute | solution.py:518
  14.9 2.0 %collective-permute-start.1 = (f32[112,256]{1,0:T(8,128)S(1)}, f32[112,256]{1,0:T(8,128)S(1)}, u32[]{:S(2)}, u32[]{:S(2)}) collective-permute-start(f32[112,256]{1,0:T(8,128)S(1)} %get-tuple-element.22), channel_id=1, source_target_pairs={{0,1},{1,0},{2,3},{3,2},{4,5},{5,4},{6,7},{7,6},{8,9},{9,8},{10,11... | collective-permute-start | bytes 344072 | tf_op jit(solution)/shard_map/ppermute | solution.py:492
  16.9 5.5 %collective-permute-start.4 = (f32[112,256]{1,0:T(8,128)S(1)}, f32[112,256]{1,0:T(8,128)S(1)}, u32[]{:S(2)}, u32[]{:S(2)}) collective-permute-start(f32[112,256]{1,0:T(8,128)S(1)} %add.35), channel_id=1, source_target_pairs={{0,64},{1,17},{2,66},{3,19},{4,68},{5,21},{6,70},{7,23},{8,72},{9,... | collective-permute-start | bytes 344072 | tf_op jit(solution)/shard_map/ppermute | solution.py:492
  20.3 4.1 %collective-permute-start.3 = (f32[112,256]{1,0:T(8,128)S(1)}, f32[112,256]{1,0:T(8,128)S(1)}, u32[]{:S(2)}, u32[]{:S(2)}) collective-permute-start(f32[112,256]{1,0:T(8,128)S(1)} %add.35), channel_id=1, source_target_pairs={{0,96},{1,9},{2,98},{3,11},{4,100},{5,13},{6,102},{7,15},{8,104},{... | collective-permute-start | bytes 344072 | tf_op jit(solution)/shard_map/ppermute | solution.py:492
  20.7 4.9 %collective-permute-start.2 = (f32[112,256]{1,0:T(8,128)S(1)}, f32[112,256]{1,0:T(8,128)S(1)}, u32[]{:S(2)}, u32[]{:S(2)}) collective-permute-start(f32[112,256]{1,0:T(8,128)S(1)} %add.35), channel_id=1, source_target_pairs={{0,32},{1,25},{2,34},{3,27},{4,36},{5,29},{6,38},{7,31},{8,40},{9,... | collective-permute-start | bytes 344072 | tf_op jit(solution)/shard_map/ppermute | solution.py:492
  25.6 5.2 %collective-permute-start.7 = (f32[112,256]{1,0:T(8,128)S(1)}, f32[112,256]{1,0:T(8,128)S(1)}, u32[]{:S(2)}, u32[]{:S(2)}) collective-permute-start(f32[112,256]{1,0:T(8,128)S(1)} %add_add_fusion.2), channel_id=1, source_target_pairs={{0,16},{1,5},{2,18},{3,7},{4,20},{5,1},{6,22},{7,3},{8,24},{9,13},... | collective-permute-start | bytes 344072 | tf_op jit(solution)/shard_map/ppermute | solution.py:492
  28.4 3.7 %collective-permute-start.6 = (f32[112,256]{1,0:T(8,128)S(1)}, f32[112,256]{1,0:T(8,128)S(1)}, u32[]{:S(2)}, u32[]{:S(2)}) collective-permute-start(f32[112,256]{1,0:T(8,128)S(1)} %add_add_fusion.2), channel_id=1, source_target_pairs={{0,24},{1,3},{2,26},{3,1},{4,28},{5,7},{6,30},{7,5},{8,16},{9,11},... | collective-permute-start | bytes 344072 | tf_op jit(solution)/shard_map/ppermute | solution.py:492
  28.7 5.1 %collective-permute-start.5 = (f32[112,256]{1,0:T(8,128)S(1)}, f32[112,256]{1,0:T(8,128)S(1)}, u32[]{:S(2)}, u32[]{:S(2)}) collective-permute-start(f32[112,256]{1,0:T(8,128)S(1)} %add_add_fusion.2), channel_id=1, source_target_pairs={{0,8},{1,7},{2,10},{3,5},{4,12},{5,3},{6,14},{7,1},{8,0},{9,15},{1... | collective-permute-start | bytes 344072 | tf_op jit(solution)/shard_map/ppermute | solution.py:492
  33.9 5.2 %collective-permute-start.10 = (f32[112,256]{1,0:T(8,128)S(1)}, f32[112,256]{1,0:T(8,128)S(1)}, u32[]{:S(2)}, u32[]{:S(2)}) collective-permute-start(f32[112,256]{1,0:T(8,128)S(1)} %add_add_fusion.1), channel_id=1, source_target_pairs={{0,4},{1,65},{2,6},{3,67},{4,0},{5,69},{6,2},{7,71},{8,12},{9,73},... | collective-permute-start | bytes 344072 | tf_op jit(solution)/shard_map/ppermute | solution.py:492
  36.9 4.4 %collective-permute-start.9 = (f32[112,256]{1,0:T(8,128)S(1)}, f32[112,256]{1,0:T(8,128)S(1)}, u32[]{:S(2)}, u32[]{:S(2)}) collective-permute-start(f32[112,256]{1,0:T(8,128)S(1)} %add_add_fusion.1), channel_id=1, source_target_pairs={{0,6},{1,33},{2,4},{3,35},{4,2},{5,37},{6,0},{7,39},{8,14},{9,41},... | collective-permute-start | bytes 344072 | tf_op jit(solution)/shard_map/ppermute | solution.py:492
  37.6 4.9 %collective-permute-start.8 = (f32[112,256]{1,0:T(8,128)S(1)}, f32[112,256]{1,0:T(8,128)S(1)}, u32[]{:S(2)}, u32[]{:S(2)}) collective-permute-start(f32[112,256]{1,0:T(8,128)S(1)} %add_add_fusion.1), channel_id=1, source_target_pairs={{0,2},{1,97},{2,0},{3,99},{4,6},{5,101},{6,4},{7,103},{8,10},{9,10... | collective-permute-start | bytes 344072 | tf_op jit(solution)/shard_map/ppermute | solution.py:492
  42.5 4.2 %collective-permute-start.11 = (f32[112,256]{1,0:T(8,128)S(1)}, f32[112,256]{1,0:T(8,128)S(1)}, u32[]{:S(2)}, u32[]{:S(2)}) collective-permute-start(f32[112,256]{1,0:T(8,128)S(1)} %add_add_fusion.mine_ref), channel_id=1, source_target_pairs={{0,1},{1,0},{2,3},{3,2},{4,5},{5,4},{6,7},{7,6},{8,9},{9,8},{10,11... | collective-permute-start | bytes 344072 | tf_op jit(solution)/shard_map/ppermute | solution.py:492

commit v7 on v6

--- a/solution.py
+++ b/solution.py
@@ -70,33 +70,38 @@
         out_ref[c * TILE : (c + 1) * TILE, :] = jnp.full((TILE, out_ref.shape[1]), value, F32)
 
 
-def fetch_row_kernel(cube_hbm, row_ref, sem):
-    copy = pltpu.make_async_copy(cube_hbm.at[pl.ds(cube_hbm.shape[0] - 1, 1)], row_ref, sem)
+def fetch_row_kernel(cube_hbm, out_ref, sem):
+    rows, cols, _ = cube_hbm.shape
+    copy = pltpu.make_async_copy(cube_hbm.at[rows - 1], out_ref.at[pl.ds(0, cols)], sem)
     copy.start()
     copy.wait()
 
 
 def join_row_kernel(mask_ref, row_ref, out_ref):
-    fill_validity(mask_ref, mask_ref.shape[0] - 1, out_ref)
-    out_ref[:, : row_ref.shape[2]] = row_ref[0]
+    rows, tiles = mask_ref.shape
+    spare = out_ref.shape[0] - tiles * TILE
+    flags = mask_ref[rows - 1 : rows, :].astype(F32)
+    out_ref[tiles * TILE :, :tiles] = jnp.broadcast_to(flags, (spare, tiles))
 
 
 def final_row(mask, cube):
     _, cols, bands = cube.shape
+    out = pltpu.VMEM((cols + 8, bands), F32)
     row = pl.pallas_call(
         fetch_row_kernel,
-        out_shape=pltpu.VMEM((1, cols, bands), F32),
+        out_shape=out,
         in_specs=[in_hbm()],
         out_specs=in_vmem(),
         scratch_shapes=[pltpu.SemaphoreType.DMA],
-        compiler_params=params(50),
+        compiler_params=params(54),
         name="fetch_row",
     )(cube)
     return pl.pallas_call(
         join_row_kernel,
-        out_shape=pltpu.VMEM((cols, W), F32),
-        in_specs=[pl.BlockSpec(memory_space=pltpu.SMEM), in_vmem()],
+        out_shape=out,
+        in_specs=[in_vmem(), in_vmem()],
         out_specs=in_vmem(),
+        input_output_aliases={1: 0},
         compiler_params=params(12),
         name="join_row",
     )(mask, row)
@@ -245,15 +250,19 @@
 
 
 def pack_kernel(
-    core_ref, valid_ref, first_ref, above_ref, sums_ref, steps_ref, seams_ref, rest_ref, mine_ref, other_ref, packed, buffer
+    core_ref, track_ref, valid_ref, first_ref, above_ref, sums_ref, steps_ref, seams_ref, rest_ref, mine_ref, other_ref, packed, buffer
 ):
     bands = first_ref.shape[1]
     half = bands // 2
     row, column = indices((W, W))
     on_diagonal = row == column
     first_valid = valid_ref[0]
-    weight = first_valid * jnp.broadcast_to(above_ref[:, bands : bands + 1], first_valid.shape)
-    difference = (first_ref[...] - above_ref[:, :bands]) * weight[:, :bands]
+    cols = first_valid.shape[0]
+    pixel_row, tile = indices((cols, 128))
+    flags = jnp.where(tile == lax.shift_right_logical(pixel_row, 3), above_ref[cols : cols + 1, :128], 0.0)
+    flags = jnp.where(track_ref[0] > 0, jnp.sum(flags, 1, keepdims=True), 0.0)
+    weight = first_valid * jnp.broadcast_to(flags, first_valid.shape)
+    difference = (first_ref[...] - above_ref[:cols, :]) * weight[:, :bands]
     high, low = split(difference)
     rest = difference - high.astype(F32)
     buffer[:, bands:W] = one_in(PAIR_ONE, buffer.shape[0], W - bands)
@@ -289,18 +298,18 @@
     other_ref[...] = packed[pl.ds(pl.multiple_of((1 - core) * half, 8), half), :]
 
 
-def pack(core, valid, first, above, sums, steps, seams, rest):
+def pack(core, track, valid, first, above, sums, steps, seams, rest):
     cols, bands = first.shape
     half = pltpu.VMEM((bands // 2, W), F32)
     return pl.pallas_call(
         pack_kernel,
         out_shape=[half, half],
-        in_specs=[pl.BlockSpec(memory_space=pltpu.SMEM)] + [in_vmem()] * 7,
+        in_specs=[pl.BlockSpec(memory_space=pltpu.SMEM)] * 2 + [in_vmem()] * 7,
         out_specs=[in_vmem()] * 2,
         scratch_shapes=[pltpu.VMEM((W, W), F32), pltpu.VMEM((cols, 2 * W), BF16)],
         compiler_params=params(12),
         name="pack",
-    )(core, valid, first, above, sums, steps, seams, rest)
+    )(core, track, valid, first, above, sums, steps, seams, rest)
 
 
 def square_sum(x):
@@ -515,10 +524,11 @@
 def per_device(cube, mask):
     bands = cube.shape[2]
     size = lax.axis_size("track")
-    above = lax.ppermute(final_row(mask, cube), "track", [(i, i + 1) for i in range(size - 1)])
+    above = lax.ppermute(final_row(mask, cube), "track", [(i, (i + 1) % size) for i in range(size)])
     core = (lax.axis_index("strip") % 2).astype(jnp.int32)[None]
+    track = lax.axis_index("track").astype(jnp.int32)[None]
     halves, valid, first, sums, steps, seams, rest = moments(mask, cube)
-    mine, other = pack(core, valid, first, above, sums, steps, seams, rest)
+    mine, other = pack(core, track, valid, first, above, sums, steps, seams, rest)
     total = mine + other_core(other)
     for axes in ((0, 1), (1, 2), (2, 0)):
         total = ring_sum(total, axes)

time: 56.6 us -> 54.7 us (0.966)
  starting transfers between devices: 20.2 us -> 17.6 us
  waiting for transfers between devices: 15.9 us -> 17.2 us
  Pallas kernels: 20 us -> 19.4 us
    ppermute x1, waiting for transfers between devices: 0.01 us -> 4.1 us  [per_device(): lax.ppermute(final_row(mask, cube), 'track', [(i, (i + 1) % size) for i i...]
    ppermute x11, waiting for transfers between devices: 15.9 us -> 13.1 us  [permute(): return lax.ppermute(x, ('track', 'strip'), pairs)]
    ppermute x1, starting transfers between devices: 4.39 us -> 2.54 us  [per_device(): lax.ppermute(final_row(mask, cube), 'track', [(i, (i + 1) % size) for i i...]
    ppermute x11, starting transfers between devices: 15.8 us -> 15 us  [permute(): return lax.ppermute(x, ('track', 'strip'), pairs)]
    pallas_call x2, Pallas kernels: 1.59 us -> 1 us  [the longest x1 0.99 us: final_row(): pl.pallas_call(fetch_row_kernel, out_shape=out, in_specs=[in_hbm()], out_...]
  transfers between devices with their start and end apart: 12 -> 12, of which waited for: 11 -> 10; matrix products, arithmetic and copies ran while one was open for 0% -> 0% of each run, Pallas kernels for 14% -> 15%
where the time goes in v7:
time: 54.7 us; the launch traced here: 54.6 us
  Pallas kernels  19.4 us (35%)
  starting transfers between devices  17.6 us (32%)
  waiting for transfers between devices  17.2 us (31%)
    ppermute x11, starting transfers between devices, permute(): return lax.ppermute(x, ('track', 'strip'), pairs)  15 us
    ppermute x11, waiting for transfers between devices, permute(): return lax.ppermute(x, ('track', 'strip'), pairs)  13.1 us
    pallas_call x1, Pallas kernels, moments(): pl.pallas_call(moments_kernel, out_shape=[pltpu.VMEM((pixels, 2 * W), BF1...  8.07 us
    pallas_call x1, Pallas kernels, apply_filter(): pl.pallas_call(filter_kernel, out_shape=jax.ShapeDtypeStruct(shape, F32),...  5.86 us
    ppermute x1, waiting for transfers between devices, per_device(): lax.ppermute(final_row(mask, cube), 'track', [(i, (i + 1) % size) for i i...  4.1 us
    pallas_call x1, Pallas kernels, solve(): pl.pallas_call(functools.partial(solve_kernel, bands), out_shape=pltpu.VM...  3.76 us
    ppermute x1, starting transfers between devices, per_device(): lax.ppermute(final_row(mask, cube), 'track', [(i, (i + 1) % size) for i i...  2.54 us
  transfers between devices with their start and end apart: 12, of which 10 were waited for; matrix products, arithmetic and copies ran while one was open for 0% of the time, Pallas kernels for 15%

profile of v7, /device:TPU:1, one launch (start us, length us, event | category | flops | bytes accessed | tf_op | source)
XLA Modules:
  0.0 54.6 jit_solution(4183698109329272835)
XLA Ops:
  0.0 0.0 copy-start
  0.0 1.0 %fetch_row.1.row_ref = f32[328,224]{1,0:T(8,128)S(1)} custom-call(f32[32,320,224]{2,1,0:T(8,128)} %cube_hbm.3), custom_call_target="tpu_custom_call" | custom-call | tf_op jit(solution)/shard_map/fetch_row/pallas_call | solution.py:90
  1.0 0.0 copy-done
  1.0 2.5 %collective-permute-start = (f32[328,224]{1,0:T(8,128)S(1)}, f32[328,224]{1,0:T(8,128)S(1)}, u32[]{:S(2)}, u32[]{:S(2)}) collective-permute-start(f32[328,224]{1,0:T(8,128)S(1)} %join_row.1), channel_id=1, source_target_pairs={{0,8},{8,16},{16,24},{24,32},{32,40},{40,48},{48,56},{56,64},{64,7... | collective-permute-start | bytes 881672 | tf_op jit(solution)/shard_map/ppermute | solution.py:527
  3.6 8.1 %moments.1 = (bf16[10240,512]{1,0:T(8,128)(2,1)S(1)}, f32[4,320,256]{2,1,0:T(8,128)S(1)}, f32[320,224]{1,0:T(8,128)S(1)}, f32[256,512]{1,0:T(8,128)S(1)}, f32[25...) custom-call(s32[4,40]{1,0:T(4,128)S(1)} %copy-done, f32[32,320,224]{2,1,0:T(8,128)} %cube_hbm.3), custom_call_target="tpu_custom_call" | custom-call | flops 4026531840 | bytes 10485760 | tf_op jit(solution)/shard_map/moments/pallas_call | solution.py:221
  11.6 4.1 %collective-permute-done.above_ref = f32[328,224]{1,0:T(8,128)S(1)} collective-permute-done((f32[328,224]{1,0:T(8,128)S(1)}, f32[328,224]{1,0:T(8,128)S(1)}, u32[]{:S(2)}, u32[]{:S(2)}) %collective-permute-start) | collective-permute-done | bytes 293920 | tf_op jit(solution)/shard_map/ppermute | solution.py:527
  15.7 0.8 %pack.1 = (f32[112,256]{1,0:T(8,128)S(1)}, f32[112,256]{1,0:T(8,128)S(1)}) custom-call(s32[1]{0:T(128)} %bitcast.core_ref, s32[1]{0:T(128)} %bitcast.1.track_ref, f32[4,320,256]{2,1,0:T(8,128)S(1)} %get-tuple-element.15.valid_ref, f32[320,224]{1,0:T(8,128)S(1)} %get-tuple-element.16.first_ref, f32[328,224]{1,0:T(8,128)S(1)} %collective-permute-done.above_ref, ...), custom_call_target="tpu_custom_call" | custom-call | tf_op jit(solution)/shard_map/pack/pallas_call | solution.py:304
  16.5 1.3 %collective-permute-start.1 = (f32[112,256]{1,0:T(8,128)S(1)}, f32[112,256]{1,0:T(8,128)S(1)}, u32[]{:S(2)}, u32[]{:S(2)}) collective-permute-start(f32[112,256]{1,0:T(8,128)S(1)} %get-tuple-element.22), channel_id=1, source_target_pairs={{0,1},{1,0},{2,3},{3,2},{4,5},{5,4},{6,7},{7,6},{8,9},{9,8},{10,11... | collective-permute-start | bytes 344072 | tf_op jit(solution)/shard_map/ppermute | solution.py:501
  17.8 1.0 %collective-permute-done.1 = f32[112,256]{1,0:T(8,128)S(1)} collective-permute-done((f32[112,256]{1,0:T(8,128)S(1)}, f32[112,256]{1,0:T(8,128)S(1)}, u32[]{:S(2)}, u32[]{:S(2)}) %collective-permute-start.1) | collective-permute-done | bytes 114720 | tf_op jit(solution)/shard_map/ppermute | solution.py:501
  18.8 0.1 collective-permute-start.4
  18.9 0.1 collective-permute-start.3
  19.0 3.1 %collective-permute-start.2 = (f32[112,256]{1,0:T(8,128)S(1)}, f32[112,256]{1,0:T(8,128)S(1)}, u32[]{:S(2)}, u32[]{:S(2)}) collective-permute-start(f32[112,256]{1,0:T(8,128)S(1)} %add.35), channel_id=1, source_target_pairs={{0,32},{1,25},{2,34},{3,27},{4,36},{5,29},{6,38},{7,31},{8,40},{9,... | collective-permute-start | bytes 344072 | tf_op jit(solution)/shard_map/ppermute | solution.py:501
  22.1 2.2 %collective-permute-done.4 = f32[112,256]{1,0:T(8,128)S(1)} collective-permute-done((f32[112,256]{1,0:T(8,128)S(1)}, f32[112,256]{1,0:T(8,128)S(1)}, u32[]{:S(2)}, u32[]{:S(2)}) %collective-permute-start.4) | collective-permute-done | bytes 114720 | tf_op jit(solution)/shard_map/ppermute | solution.py:501
  24.3 0.0 collective-permute-done.3
  24.3 1.2 %collective-permute-done.2 = f32[112,256]{1,0:T(8,128)S(1)} collective-permute-done((f32[112,256]{1,0:T(8,128)S(1)}, f32[112,256]{1,0:T(8,128)S(1)}, u32[]{:S(2)}, u32[]{:S(2)}) %collective-permute-start.2) | collective-permute-done | bytes 114720 | tf_op jit(solution)/shard_map/ppermute | solution.py:501
  25.6 2.8 %collective-permute-start.7 = (f32[112,256]{1,0:T(8,128)S(1)}, f32[112,256]{1,0:T(8,128)S(1)}, u32[]{:S(2)}, u32[]{:S(2)}) collective-permute-start(f32[112,256]{1,0:T(8,128)S(1)} %add_add_fusion.2), channel_id=1, source_target_pairs={{0,16},{1,5},{2,18},{3,7},{4,20},{5,1},{6,22},{7,3},{8,24},{9,13},... | collective-permute-start | bytes 344072 | tf_op jit(solution)/shard_map/ppermute | solution.py:501
  28.4 0.3 collective-permute-start.6
  28.7 0.5 %collective-permute-start.5 = (f32[112,256]{1,0:T(8,128)S(1)}, f32[112,256]{1,0:T(8,128)S(1)}, u32[]{:S(2)}, u32[]{:S(2)}) collective-permute-start(f32[112,256]{1,0:T(8,128)S(1)} %add_add_fusion.2), channel_id=1, source_target_pairs={{0,8},{1,7},{2,10},{3,5},{4,12},{5,3},{6,14},{7,1},{8,0},{9,15},{1... | collective-permute-start | bytes 344072 | tf_op jit(solution)/shard_map/ppermute | solution.py:501
  29.3 1.5 %collective-permute-done.7 = f32[112,256]{1,0:T(8,128)S(1)} collective-permute-done((f32[112,256]{1,0:T(8,128)S(1)}, f32[112,256]{1,0:T(8,128)S(1)}, u32[]{:S(2)}, u32[]{:S(2)}) %collective-permute-start.7) | collective-permute-done | bytes 114720 | tf_op jit(solution)/shard_map/ppermute | solution.py:501
  30.8 1.6 %collective-permute-done.6 = f32[112,256]{1,0:T(8,128)S(1)} collective-permute-done((f32[112,256]{1,0:T(8,128)S(1)}, f32[112,256]{1,0:T(8,128)S(1)}, u32[]{:S(2)}, u32[]{:S(2)}) %collective-permute-start.6) | collective-permute-done | bytes 114720 | tf_op jit(solution)/shard_map/ppermute | solution.py:501
  32.4 1.4 %collective-permute-done.5 = f32[112,256]{1,0:T(8,128)S(1)} collective-permute-done((f32[112,256]{1,0:T(8,128)S(1)}, f32[112,256]{1,0:T(8,128)S(1)}, u32[]{:S(2)}, u32[]{:S(2)}) %collective-permute-start.5) | collective-permute-done | bytes 114720 | tf_op jit(solution)/shard_map/ppermute | solution.py:501
  33.9 0.8 %collective-permute-start.10 = (f32[112,256]{1,0:T(8,128)S(1)}, f32[112,256]{1,0:T(8,128)S(1)}, u32[]{:S(2)}, u32[]{:S(2)}) collective-permute-start(f32[112,256]{1,0:T(8,128)S(1)} %add_add_fusion.1), channel_id=1, source_target_pairs={{0,4},{1,65},{2,6},{3,67},{4,0},{5,69},{6,2},{7,71},{8,12},{9,73},... | collective-permute-start | bytes 344072 | tf_op jit(solution)/shard_map/ppermute | solution.py:501
  34.7 0.7 %collective-permute-start.9 = (f32[112,256]{1,0:T(8,128)S(1)}, f32[112,256]{1,0:T(8,128)S(1)}, u32[]{:S(2)}, u32[]{:S(2)}) collective-permute-start(f32[112,256]{1,0:T(8,128)S(1)} %add_add_fusion.1), channel_id=1, source_target_pairs={{0,6},{1,33},{2,4},{3,35},{4,2},{5,37},{6,0},{7,39},{8,14},{9,41},... | collective-permute-start | bytes 344072 | tf_op jit(solution)/shard_map/ppermute | solution.py:501
  35.4 1.9 %collective-permute-start.8 = (f32[112,256]{1,0:T(8,128)S(1)}, f32[112,256]{1,0:T(8,128)S(1)}, u32[]{:S(2)}, u32[]{:S(2)}) collective-permute-start(f32[112,256]{1,0:T(8,128)S(1)} %add_add_fusion.1), channel_id=1, source_target_pairs={{0,2},{1,97},{2,0},{3,99},{4,6},{5,101},{6,4},{7,103},{8,10},{9,10... | collective-permute-start | bytes 344072 | tf_op jit(solution)/shard_map/ppermute | solution.py:501
  37.2 2.2 %collective-permute-done.10 = f32[112,256]{1,0:T(8,128)S(1)} collective-permute-done((f32[112,256]{1,0:T(8,128)S(1)}, f32[112,256]{1,0:T(8,128)S(1)}, u32[]{:S(2)}, u32[]{:S(2)}) %collective-permute-start.10) | collective-permute-done | bytes 114720 | tf_op jit(solution)/shard_map/ppermute | solution.py:501
  39.4 0.0 collective-permute-done.9
  39.4 1.0 %collective-permute-done.8 = f32[112,256]{1,0:T(8,128)S(1)} collective-permute-done((f32[112,256]{1,0:T(8,128)S(1)}, f32[112,256]{1,0:T(8,128)S(1)}, u32[]{:S(2)}, u32[]{:S(2)}) %collective-permute-start.8) | collective-permute-done | bytes 114720 | tf_op jit(solution)/shard_map/ppermute | solution.py:501
  40.5 3.4 %collective-permute-start.11 = (f32[112,256]{1,0:T(8,128)S(1)}, f32[112,256]{1,0:T(8,128)S(1)}, u32[]{:S(2)}, u32[]{:S(2)}) collective-permute-start(f32[112,256]{1,0:T(8,128)S(1)} %add_add_fusion.mine_ref), channel_id=1, source_target_pairs={{0,1},{1,0},{2,3},{3,2},{4,5},{5,4},{6,7},{7,6},{8,9},{9,8},{10,11... | collective-permute-start | bytes 344072 | tf_op jit(solution)/shard_map/ppermute | solution.py:501
  43.9 1.0 %collective-permute-done.11.other_ref = f32[112,256]{1,0:T(8,128)S(1)} collective-permute-done((f32[112,256]{1,0:T(8,128)S(1)}, f32[112,256]{1,0:T(8,128)S(1)}, u32[]{:S(2)}, u32[]{:S(2)}) %collective-permute-start.11) | collective-permute-done | bytes 114720 | tf_op jit(solution)/shard_map/ppermute | solution.py:501
  44.8 3.8 %solve.1.weights_ref = bf16[768,256]{1,0:T(8,128)(2,1)S(1)} custom-call(s32[1]{0:T(128)} %bitcast.core_ref, f32[112,256]{1,0:T(8,128)S(1)} %add_add_fusion.mine_ref, f32[112,256]{1,0:T(8,128)S(1)} %collective-permute-done.11.other_ref), custom_call_target="tpu_custom_call" | custom-call | tf_op jit(solution)/shard_map/solve/pallas_call | solution.py:444
  48.6 5.9 %filter.1 = f32[32,320,224]{2,1,0:T(8,128)} custom-call(bf16[10240,512]{1,0:T(8,128)(2,1)S(1)} %get-tuple-element.14.halves_ref, f32[4,320,256]{2,1,0:T(8,128)S(1)} %get-tuple-element.15.valid_ref, bf16[768,256]{1,0:T(8,128)(2,1)S(1)} %solve.1.weights_ref), custom_call_target="tpu_custom_call" | custom-call | flops 4026531840 | bytes 10485760 | tf_op jit(solution)/shard_map/filter/pallas_call | solution.py:479
  (5 shorter events, 0.1 us)
Async XLA Ops:
  0.0 1.0 %copy-start = (s32[4,40]{1,0:T(4,128)S(1)}, s32[4,40]{1,0:T(4,128)}, u32[]{:S(2)}) copy-start(s32[4,40]{1,0:T(4,128)} %mask_ref.1) | copy-start | bytes 1924
  1.0 14.7 %collective-permute-start = (f32[328,224]{1,0:T(8,128)S(1)}, f32[328,224]{1,0:T(8,128)S(1)}, u32[]{:S(2)}, u32[]{:S(2)}) collective-permute-start(f32[328,224]{1,0:T(8,128)S(1)} %join_row.1), channel_id=1, source_target_pairs={{0,8},{8,16},{16,24},{24,32},{32,40},{40,48},{48,56},{56,64},{64,7... | collective-permute-start | bytes 881672 | tf_op jit(solution)/shard_map/ppermute | solution.py:527
  16.5 2.3 %collective-permute-start.1 = (f32[112,256]{1,0:T(8,128)S(1)}, f32[112,256]{1,0:T(8,128)S(1)}, u32[]{:S(2)}, u32[]{:S(2)}) collective-permute-start(f32[112,256]{1,0:T(8,128)S(1)} %get-tuple-element.22), channel_id=1, source_target_pairs={{0,1},{1,0},{2,3},{3,2},{4,5},{5,4},{6,7},{7,6},{8,9},{9,8},{10,11... | collective-permute-start | bytes 344072 | tf_op jit(solution)/shard_map/ppermute | solution.py:501
  18.8 5.5 %collective-permute-start.4 = (f32[112,256]{1,0:T(8,128)S(1)}, f32[112,256]{1,0:T(8,128)S(1)}, u32[]{:S(2)}, u32[]{:S(2)}) collective-permute-start(f32[112,256]{1,0:T(8,128)S(1)} %add.35), channel_id=1, source_target_pairs={{0,64},{1,17},{2,66},{3,19},{4,68},{5,21},{6,70},{7,23},{8,72},{9,... | collective-permute-start | bytes 344072 | tf_op jit(solution)/shard_map/ppermute | solution.py:501
  18.9 5.4 %collective-permute-start.3 = (f32[112,256]{1,0:T(8,128)S(1)}, f32[112,256]{1,0:T(8,128)S(1)}, u32[]{:S(2)}, u32[]{:S(2)}) collective-permute-start(f32[112,256]{1,0:T(8,128)S(1)} %add.35), channel_id=1, source_target_pairs={{0,96},{1,9},{2,98},{3,11},{4,100},{5,13},{6,102},{7,15},{8,104},{... | collective-permute-start | bytes 344072 | tf_op jit(solution)/shard_map/ppermute | solution.py:501
  19.0 6.6 %collective-permute-start.2 = (f32[112,256]{1,0:T(8,128)S(1)}, f32[112,256]{1,0:T(8,128)S(1)}, u32[]{:S(2)}, u32[]{:S(2)}) collective-permute-start(f32[112,256]{1,0:T(8,128)S(1)} %add.35), channel_id=1, source_target_pairs={{0,32},{1,25},{2,34},{3,27},{4,36},{5,29},{6,38},{7,31},{8,40},{9,... | collective-permute-start | bytes 344072 | tf_op jit(solution)/shard_map/ppermute | solution.py:501
  25.6 5.2 %collective-permute-start.7 = (f32[112,256]{1,0:T(8,128)S(1)}, f32[112,256]{1,0:T(8,128)S(1)}, u32[]{:S(2)}, u32[]{:S(2)}) collective-permute-start(f32[112,256]{1,0:T(8,128)S(1)} %add_add_fusion.2), channel_id=1, source_target_pairs={{0,16},{1,5},{2,18},{3,7},{4,20},{5,1},{6,22},{7,3},{8,24},{9,13},... | collective-permute-start | bytes 344072 | tf_op jit(solution)/shard_map/ppermute | solution.py:501
  28.4 4.0 %collective-permute-start.6 = (f32[112,256]{1,0:T(8,128)S(1)}, f32[112,256]{1,0:T(8,128)S(1)}, u32[]{:S(2)}, u32[]{:S(2)}) collective-permute-start(f32[112,256]{1,0:T(8,128)S(1)} %add_add_fusion.2), channel_id=1, source_target_pairs={{0,24},{1,3},{2,26},{3,1},{4,28},{5,7},{6,30},{7,5},{8,16},{9,11},... | collective-permute-start | bytes 344072 | tf_op jit(solution)/shard_map/ppermute | solution.py:501
  28.7 5.1 %collective-permute-start.5 = (f32[112,256]{1,0:T(8,128)S(1)}, f32[112,256]{1,0:T(8,128)S(1)}, u32[]{:S(2)}, u32[]{:S(2)}) collective-permute-start(f32[112,256]{1,0:T(8,128)S(1)} %add_add_fusion.2), channel_id=1, source_target_pairs={{0,8},{1,7},{2,10},{3,5},{4,12},{5,3},{6,14},{7,1},{8,0},{9,15},{1... | collective-permute-start | bytes 344072 | tf_op jit(solution)/shard_map/ppermute | solution.py:501
  33.9 5.5 %collective-permute-start.10 = (f32[112,256]{1,0:T(8,128)S(1)}, f32[112,256]{1,0:T(8,128)S(1)}, u32[]{:S(2)}, u32[]{:S(2)}) collective-permute-start(f32[112,256]{1,0:T(8,128)S(1)} %add_add_fusion.1), channel_id=1, source_target_pairs={{0,4},{1,65},{2,6},{3,67},{4,0},{5,69},{6,2},{7,71},{8,12},{9,73},... | collective-permute-start | bytes 344072 | tf_op jit(solution)/shard_map/ppermute | solution.py:501
  34.7 4.8 %collective-permute-start.9 = (f32[112,256]{1,0:T(8,128)S(1)}, f32[112,256]{1,0:T(8,128)S(1)}, u32[]{:S(2)}, u32[]{:S(2)}) collective-permute-start(f32[112,256]{1,0:T(8,128)S(1)} %add_add_fusion.1), channel_id=1, source_target_pairs={{0,6},{1,33},{2,4},{3,35},{4,2},{5,37},{6,0},{7,39},{8,14},{9,41},... | collective-permute-start | bytes 344072 | tf_op jit(solution)/shard_map/ppermute | solution.py:501
  35.4 5.1 %collective-permute-start.8 = (f32[112,256]{1,0:T(8,128)S(1)}, f32[112,256]{1,0:T(8,128)S(1)}, u32[]{:S(2)}, u32[]{:S(2)}) collective-permute-start(f32[112,256]{1,0:T(8,128)S(1)} %add_add_fusion.1), channel_id=1, source_target_pairs={{0,2},{1,97},{2,0},{3,99},{4,6},{5,101},{6,4},{7,103},{8,10},{9,10... | collective-permute-start | bytes 344072 | tf_op jit(solution)/shard_map/ppermute | solution.py:501
  40.5 4.4 %collective-permute-start.11 = (f32[112,256]{1,0:T(8,128)S(1)}, f32[112,256]{1,0:T(8,128)S(1)}, u32[]{:S(2)}, u32[]{:S(2)}) collective-permute-start(f32[112,256]{1,0:T(8,128)S(1)} %add_add_fusion.mine_ref), channel_id=1, source_target_pairs={{0,1},{1,0},{2,3},{3,2},{4,5},{5,4},{6,7},{7,6},{8,9},{9,8},{10,11... | collective-permute-start | bytes 344072 | tf_op jit(solution)/shard_map/ppermute | solution.py:501

commit v8 on v7

--- a/solution.py
+++ b/solution.py
@@ -70,26 +70,41 @@
         out_ref[c * TILE : (c + 1) * TILE, :] = jnp.full((TILE, out_ref.shape[1]), value, F32)
 
 
+def folding(cols, bands):
+    keep = cols * bands // W
+    return keep, cols - keep, W - bands
+
+
 def fetch_row_kernel(cube_hbm, out_ref, sem):
-    rows, cols, _ = cube_hbm.shape
-    copy = pltpu.make_async_copy(cube_hbm.at[rows - 1], out_ref.at[pl.ds(0, cols)], sem)
+    copy = pltpu.make_async_copy(cube_hbm.at[cube_hbm.shape[0] - 1], out_ref, sem)
     copy.start()
     copy.wait()
 
 
-def join_row_kernel(mask_ref, row_ref, out_ref):
+def fold_row_kernel(mask_ref, row_ref, out_ref):
     rows, tiles = mask_ref.shape
-    spare = out_ref.shape[0] - tiles * TILE
+    cols, bands = row_ref.shape
+    keep, left, spare = folding(cols, bands)
+    out_ref[:keep, :bands] = row_ref[:keep, :]
+    for j in range(bands // spare):
+        out_ref[j * left : (j + 1) * left, bands:] = row_ref[keep:, j * spare : (j + 1) * spare]
     flags = mask_ref[rows - 1 : rows, :].astype(F32)
-    out_ref[tiles * TILE :, :tiles] = jnp.broadcast_to(flags, (spare, tiles))
+    out_ref[keep:, :tiles] = jnp.broadcast_to(flags, (out_ref.shape[0] - keep, tiles))
+
+
+def unfold_row(row_ref, out_ref):
+    cols, bands = out_ref.shape
+    keep, left, spare = folding(cols, bands)
+    out_ref[:keep, :] = row_ref[:keep, :bands]
+    for j in range(bands // spare):
+        out_ref[keep:, j * spare : (j + 1) * spare] = row_ref[j * left : (j + 1) * left, bands:]
 
 
 def final_row(mask, cube):
     _, cols, bands = cube.shape
-    out = pltpu.VMEM((cols + 8, bands), F32)
     row = pl.pallas_call(
         fetch_row_kernel,
-        out_shape=out,
+        out_shape=pltpu.VMEM((cols, bands), F32),
         in_specs=[in_hbm()],
         out_specs=in_vmem(),
         scratch_shapes=[pltpu.SemaphoreType.DMA],
@@ -97,13 +112,12 @@
         name="fetch_row",
     )(cube)
     return pl.pallas_call(
-        join_row_kernel,
-        out_shape=out,
+        fold_row_kernel,
+        out_shape=pltpu.VMEM((folding(cols, bands)[0] + 8, W), F32),
         in_specs=[in_vmem(), in_vmem()],
         out_specs=in_vmem(),
-        input_output_aliases={1: 0},
         compiler_params=params(12),
-        name="join_row",
+        name="fold_row",
     )(mask, row)
 
 
@@ -250,7 +264,7 @@
 
 
 def pack_kernel(
-    core_ref, track_ref, valid_ref, first_ref, above_ref, sums_ref, steps_ref, seams_ref, rest_ref, mine_ref, other_ref, packed, buffer
+    core_ref, track_ref, valid_ref, first_ref, above_ref, sums_ref, steps_ref, seams_ref, rest_ref, mine_ref, other_ref, packed, buffer, above_row
 ):
     bands = first_ref.shape[1]
     half = bands // 2
@@ -259,10 +273,12 @@
     first_valid = valid_ref[0]
     cols = first_valid.shape[0]
     pixel_row, tile = indices((cols, 128))
-    flags = jnp.where(tile == lax.shift_right_logical(pixel_row, 3), above_ref[cols : cols + 1, :128], 0.0)
+    keep = folding(cols, bands)[0]
+    unfold_row(above_ref, above_row)
+    flags = jnp.where(tile == lax.shift_right_logical(pixel_row, 3), above_ref[keep : keep + 1, :128], 0.0)
     flags = jnp.where(track_ref[0] > 0, jnp.sum(flags, 1, keepdims=True), 0.0)
     weight = first_valid * jnp.broadcast_to(flags, first_valid.shape)
-    difference = (first_ref[...] - above_ref[:cols, :]) * weight[:, :bands]
+    difference = (first_ref[...] - above_row[...]) * weight[:, :bands]
     high, low = split(difference)
     rest = difference - high.astype(F32)
     buffer[:, bands:W] = one_in(PAIR_ONE, buffer.shape[0], W - bands)
@@ -306,7 +322,7 @@
         out_shape=[half, half],
         in_specs=[pl.BlockSpec(memory_space=pltpu.SMEM)] * 2 + [in_vmem()] * 7,
         out_specs=[in_vmem()] * 2,
-        scratch_shapes=[pltpu.VMEM((W, W), F32), pltpu.VMEM((cols, 2 * W), BF16)],
+        scratch_shapes=[pltpu.VMEM((W, W), F32), pltpu.VMEM((cols, 2 * W), BF16), pltpu.VMEM((cols, bands), F32)],
         compiler_params=params(12),
         name="pack",
     )(core, track, valid, first, above, sums, steps, seams, rest)

time: 54.7 us -> 54.3 us (level)
  waiting for transfers between devices: 17.2 us -> 16.6 us
    ppermute x1, waiting for transfers between devices: 4.1 us -> 3.22 us  [per_device(): lax.ppermute(final_row(mask, cube), 'track', [(i, (i + 1) % size) for i i...]
where the time goes in v8:
time: 54.3 us; the launch traced here: 54.2 us
  Pallas kernels  19.7 us (36%)
  starting transfers between devices  17.6 us (32%)
  waiting for transfers between devices  16.6 us (31%)
    ppermute x11, starting transfers between devices, permute(): return lax.ppermute(x, ('track', 'strip'), pairs)  15 us
    ppermute x11, waiting for transfers between devices, permute(): return lax.ppermute(x, ('track', 'strip'), pairs)  13.4 us
    pallas_call x1, Pallas kernels, moments(): pl.pallas_call(moments_kernel, out_shape=[pltpu.VMEM((pixels, 2 * W), BF1...  8.07 us
    pallas_call x1, Pallas kernels, apply_filter(): pl.pallas_call(filter_kernel, out_shape=jax.ShapeDtypeStruct(shape, F32),...  5.86 us
    pallas_call x1, Pallas kernels, solve(): pl.pallas_call(functools.partial(solve_kernel, bands), out_shape=pltpu.VM...  3.75 us
    ppermute x1, waiting for transfers between devices, per_device(): lax.ppermute(final_row(mask, cube), 'track', [(i, (i + 1) % size) for i i...  3.22 us
    ppermute x1, starting transfers between devices, per_device(): lax.ppermute(final_row(mask, cube), 'track', [(i, (i + 1) % size) for i i...  2.54 us
  transfers between devices with their start and end apart: 12, of which 10 were waited for; matrix products, arithmetic and copies ran while one was open for 0% of the time, Pallas kernels for 15%

profile of v8, /device:TPU:1, one launch (start us, length us, event | category | flops | bytes accessed | tf_op | source)
XLA Modules:
  0.0 54.2 jit_solution(533657464965401648)
XLA Ops:
  0.0 0.0 copy-start
  0.0 1.0 %fetch_row.1.row_ref = f32[320,224]{1,0:T(8,128)S(1)} custom-call(f32[32,320,224]{2,1,0:T(8,128)} %cube_hbm.3), custom_call_target="tpu_custom_call" | custom-call | tf_op jit(solution)/shard_map/fetch_row/pallas_call | solution.py:105
  1.0 0.0 copy-done
  1.0 0.1 fold_row.1
  1.1 2.5 %collective-permute-start = (f32[288,256]{1,0:T(8,128)S(1)}, f32[288,256]{1,0:T(8,128)S(1)}, u32[]{:S(2)}, u32[]{:S(2)}) collective-permute-start(f32[288,256]{1,0:T(8,128)S(1)} %fold_row.1), channel_id=1, source_target_pairs={{0,8},{8,16},{16,24},{24,32},{32,40},{40,48},{48,56},{56,64},{64,7... | collective-permute-start | bytes 884744 | tf_op jit(solution)/shard_map/ppermute | solution.py:543
  3.7 8.1 %moments.1 = (bf16[10240,512]{1,0:T(8,128)(2,1)S(1)}, f32[4,320,256]{2,1,0:T(8,128)S(1)}, f32[320,224]{1,0:T(8,128)S(1)}, f32[256,512]{1,0:T(8,128)S(1)}, f32[25...) custom-call(s32[4,40]{1,0:T(4,128)S(1)} %copy-done, f32[32,320,224]{2,1,0:T(8,128)} %cube_hbm.3), custom_call_target="tpu_custom_call" | custom-call | flops 4026531840 | bytes 10485760 | tf_op jit(solution)/shard_map/moments/pallas_call | solution.py:235
  11.7 3.2 %collective-permute-done.above_ref = f32[288,256]{1,0:T(8,128)S(1)} collective-permute-done((f32[288,256]{1,0:T(8,128)S(1)}, f32[288,256]{1,0:T(8,128)S(1)}, u32[]{:S(2)}, u32[]{:S(2)}) %collective-permute-start) | collective-permute-done | bytes 294944 | tf_op jit(solution)/shard_map/ppermute | solution.py:543
  15.0 0.9 %pack.1 = (f32[112,256]{1,0:T(8,128)S(1)}, f32[112,256]{1,0:T(8,128)S(1)}) custom-call(s32[1]{0:T(128)} %bitcast.core_ref, s32[1]{0:T(128)} %bitcast.1.track_ref, f32[4,320,256]{2,1,0:T(8,128)S(1)} %get-tuple-element.15.valid_ref, f32[320,224]{1,0:T(8,128)S(1)} %get-tuple-element.16.first_ref, f32[288,256]{1,0:T(8,128)S(1)} %collective-permute-done.above_ref, ...), custom_call_target="tpu_custom_call" | custom-call | tf_op jit(solution)/shard_map/pack/pallas_call | solution.py:320
  15.8 1.3 %collective-permute-start.1 = (f32[112,256]{1,0:T(8,128)S(1)}, f32[112,256]{1,0:T(8,128)S(1)}, u32[]{:S(2)}, u32[]{:S(2)}) collective-permute-start(f32[112,256]{1,0:T(8,128)S(1)} %get-tuple-element.22), channel_id=1, source_target_pairs={{0,1},{1,0},{2,3},{3,2},{4,5},{5,4},{6,7},{7,6},{8,9},{9,8},{10,11... | collective-permute-start | bytes 344072 | tf_op jit(solution)/shard_map/ppermute | solution.py:517
  17.2 1.0 %collective-permute-done.1 = f32[112,256]{1,0:T(8,128)S(1)} collective-permute-done((f32[112,256]{1,0:T(8,128)S(1)}, f32[112,256]{1,0:T(8,128)S(1)}, u32[]{:S(2)}, u32[]{:S(2)}) %collective-permute-start.1) | collective-permute-done | bytes 114720 | tf_op jit(solution)/shard_map/ppermute | solution.py:517
  18.1 0.1 collective-permute-start.4
  18.2 0.1 collective-permute-start.3
  18.3 3.1 %collective-permute-start.2 = (f32[112,256]{1,0:T(8,128)S(1)}, f32[112,256]{1,0:T(8,128)S(1)}, u32[]{:S(2)}, u32[]{:S(2)}) collective-permute-start(f32[112,256]{1,0:T(8,128)S(1)} %add.35), channel_id=1, source_target_pairs={{0,32},{1,25},{2,34},{3,27},{4,36},{5,29},{6,38},{7,31},{8,40},{9,... | collective-permute-start | bytes 344072 | tf_op jit(solution)/shard_map/ppermute | solution.py:517
  21.5 2.2 %collective-permute-done.4 = f32[112,256]{1,0:T(8,128)S(1)} collective-permute-done((f32[112,256]{1,0:T(8,128)S(1)}, f32[112,256]{1,0:T(8,128)S(1)}, u32[]{:S(2)}, u32[]{:S(2)}) %collective-permute-start.4) | collective-permute-done | bytes 114720 | tf_op jit(solution)/shard_map/ppermute | solution.py:517
  23.7 0.0 collective-permute-done.3
  23.7 1.2 %collective-permute-done.2 = f32[112,256]{1,0:T(8,128)S(1)} collective-permute-done((f32[112,256]{1,0:T(8,128)S(1)}, f32[112,256]{1,0:T(8,128)S(1)}, u32[]{:S(2)}, u32[]{:S(2)}) %collective-permute-start.2) | collective-permute-done | bytes 114720 | tf_op jit(solution)/shard_map/ppermute | solution.py:517
  24.9 2.8 %collective-permute-start.7 = (f32[112,256]{1,0:T(8,128)S(1)}, f32[112,256]{1,0:T(8,128)S(1)}, u32[]{:S(2)}, u32[]{:S(2)}) collective-permute-start(f32[112,256]{1,0:T(8,128)S(1)} %add_add_fusion.2), channel_id=1, source_target_pairs={{0,16},{1,5},{2,18},{3,7},{4,20},{5,1},{6,22},{7,3},{8,24},{9,13},... | collective-permute-start | bytes 344072 | tf_op jit(solution)/shard_map/ppermute | solution.py:517
  27.8 0.3 collective-permute-start.6
  28.1 0.5 %collective-permute-start.5 = (f32[112,256]{1,0:T(8,128)S(1)}, f32[112,256]{1,0:T(8,128)S(1)}, u32[]{:S(2)}, u32[]{:S(2)}) collective-permute-start(f32[112,256]{1,0:T(8,128)S(1)} %add_add_fusion.2), channel_id=1, source_target_pairs={{0,8},{1,7},{2,10},{3,5},{4,12},{5,3},{6,14},{7,1},{8,0},{9,15},{1... | collective-permute-start | bytes 344072 | tf_op jit(solution)/shard_map/ppermute | solution.py:517
  28.6 1.5 %collective-permute-done.7 = f32[112,256]{1,0:T(8,128)S(1)} collective-permute-done((f32[112,256]{1,0:T(8,128)S(1)}, f32[112,256]{1,0:T(8,128)S(1)}, u32[]{:S(2)}, u32[]{:S(2)}) %collective-permute-start.7) | collective-permute-done | bytes 114720 | tf_op jit(solution)/shard_map/ppermute | solution.py:517
  30.2 1.6 %collective-permute-done.6 = f32[112,256]{1,0:T(8,128)S(1)} collective-permute-done((f32[112,256]{1,0:T(8,128)S(1)}, f32[112,256]{1,0:T(8,128)S(1)}, u32[]{:S(2)}, u32[]{:S(2)}) %collective-permute-start.6) | collective-permute-done | bytes 114720 | tf_op jit(solution)/shard_map/ppermute | solution.py:517
  31.8 1.4 %collective-permute-done.5 = f32[112,256]{1,0:T(8,128)S(1)} collective-permute-done((f32[112,256]{1,0:T(8,128)S(1)}, f32[112,256]{1,0:T(8,128)S(1)}, u32[]{:S(2)}, u32[]{:S(2)}) %collective-permute-start.5) | collective-permute-done | bytes 114720 | tf_op jit(solution)/shard_map/ppermute | solution.py:517
  33.2 1.0 %collective-permute-start.10 = (f32[112,256]{1,0:T(8,128)S(1)}, f32[112,256]{1,0:T(8,128)S(1)}, u32[]{:S(2)}, u32[]{:S(2)}) collective-permute-start(f32[112,256]{1,0:T(8,128)S(1)} %add_add_fusion.1), channel_id=1, source_target_pairs={{0,4},{1,65},{2,6},{3,67},{4,0},{5,69},{6,2},{7,71},{8,12},{9,73},... | collective-permute-start | bytes 344072 | tf_op jit(solution)/shard_map/ppermute | solution.py:517
  34.2 0.7 %collective-permute-start.9 = (f32[112,256]{1,0:T(8,128)S(1)}, f32[112,256]{1,0:T(8,128)S(1)}, u32[]{:S(2)}, u32[]{:S(2)}) collective-permute-start(f32[112,256]{1,0:T(8,128)S(1)} %add_add_fusion.1), channel_id=1, source_target_pairs={{0,6},{1,33},{2,4},{3,35},{4,2},{5,37},{6,0},{7,39},{8,14},{9,41},... | collective-permute-start | bytes 344072 | tf_op jit(solution)/shard_map/ppermute | solution.py:517
  34.9 1.6 %collective-permute-start.8 = (f32[112,256]{1,0:T(8,128)S(1)}, f32[112,256]{1,0:T(8,128)S(1)}, u32[]{:S(2)}, u32[]{:S(2)}) collective-permute-start(f32[112,256]{1,0:T(8,128)S(1)} %add_add_fusion.1), channel_id=1, source_target_pairs={{0,2},{1,97},{2,0},{3,99},{4,6},{5,101},{6,4},{7,103},{8,10},{9,10... | collective-permute-start | bytes 344072 | tf_op jit(solution)/shard_map/ppermute | solution.py:517
  36.6 1.9 %collective-permute-done.10 = f32[112,256]{1,0:T(8,128)S(1)} collective-permute-done((f32[112,256]{1,0:T(8,128)S(1)}, f32[112,256]{1,0:T(8,128)S(1)}, u32[]{:S(2)}, u32[]{:S(2)}) %collective-permute-start.10) | collective-permute-done | bytes 114720 | tf_op jit(solution)/shard_map/ppermute | solution.py:517
  38.5 0.0 collective-permute-done.9
  38.5 1.5 %collective-permute-done.8 = f32[112,256]{1,0:T(8,128)S(1)} collective-permute-done((f32[112,256]{1,0:T(8,128)S(1)}, f32[112,256]{1,0:T(8,128)S(1)}, u32[]{:S(2)}, u32[]{:S(2)}) %collective-permute-start.8) | collective-permute-done | bytes 114720 | tf_op jit(solution)/shard_map/ppermute | solution.py:517
  40.1 3.4 %collective-permute-start.11 = (f32[112,256]{1,0:T(8,128)S(1)}, f32[112,256]{1,0:T(8,128)S(1)}, u32[]{:S(2)}, u32[]{:S(2)}) collective-permute-start(f32[112,256]{1,0:T(8,128)S(1)} %add_add_fusion.mine_ref), channel_id=1, source_target_pairs={{0,1},{1,0},{2,3},{3,2},{4,5},{5,4},{6,7},{7,6},{8,9},{9,8},{10,11... | collective-permute-start | bytes 344072 | tf_op jit(solution)/shard_map/ppermute | solution.py:517
  43.5 1.0 %collective-permute-done.11.other_ref = f32[112,256]{1,0:T(8,128)S(1)} collective-permute-done((f32[112,256]{1,0:T(8,128)S(1)}, f32[112,256]{1,0:T(8,128)S(1)}, u32[]{:S(2)}, u32[]{:S(2)}) %collective-permute-start.11) | collective-permute-done | bytes 114720 | tf_op jit(solution)/shard_map/ppermute | solution.py:517
  44.4 3.7 %solve.1.weights_ref = bf16[768,256]{1,0:T(8,128)(2,1)S(1)} custom-call(s32[1]{0:T(128)} %bitcast.core_ref, f32[112,256]{1,0:T(8,128)S(1)} %add_add_fusion.mine_ref, f32[112,256]{1,0:T(8,128)S(1)} %collective-permute-done.11.other_ref), custom_call_target="tpu_custom_call" | custom-call | tf_op jit(solution)/shard_map/solve/pallas_call | solution.py:460
  48.2 5.9 %filter.1 = f32[32,320,224]{2,1,0:T(8,128)} custom-call(bf16[10240,512]{1,0:T(8,128)(2,1)S(1)} %get-tuple-element.14.halves_ref, f32[4,320,256]{2,1,0:T(8,128)S(1)} %get-tuple-element.15.valid_ref, bf16[768,256]{1,0:T(8,128)(2,1)S(1)} %solve.1.weights_ref), custom_call_target="tpu_custom_call" | custom-call | flops 4026531840 | bytes 10485760 | tf_op jit(solution)/shard_map/filter/pallas_call | solution.py:495
  (4 shorter events, 0.1 us)
Async XLA Ops:
  0.0 1.0 %copy-start = (s32[4,40]{1,0:T(4,128)S(1)}, s32[4,40]{1,0:T(4,128)}, u32[]{:S(2)}) copy-start(s32[4,40]{1,0:T(4,128)} %mask_ref.1) | copy-start | bytes 1924
  1.1 13.8 %collective-permute-start = (f32[288,256]{1,0:T(8,128)S(1)}, f32[288,256]{1,0:T(8,128)S(1)}, u32[]{:S(2)}, u32[]{:S(2)}) collective-permute-start(f32[288,256]{1,0:T(8,128)S(1)} %fold_row.1), channel_id=1, source_target_pairs={{0,8},{8,16},{16,24},{24,32},{32,40},{40,48},{48,56},{56,64},{64,7... | collective-permute-start | bytes 884744 | tf_op jit(solution)/shard_map/ppermute | solution.py:543
  15.8 2.3 %collective-permute-start.1 = (f32[112,256]{1,0:T(8,128)S(1)}, f32[112,256]{1,0:T(8,128)S(1)}, u32[]{:S(2)}, u32[]{:S(2)}) collective-permute-start(f32[112,256]{1,0:T(8,128)S(1)} %get-tuple-element.22), channel_id=1, source_target_pairs={{0,1},{1,0},{2,3},{3,2},{4,5},{5,4},{6,7},{7,6},{8,9},{9,8},{10,11... | collective-permute-start | bytes 344072 | tf_op jit(solution)/shard_map/ppermute | solution.py:517
  18.1 5.5 %collective-permute-start.4 = (f32[112,256]{1,0:T(8,128)S(1)}, f32[112,256]{1,0:T(8,128)S(1)}, u32[]{:S(2)}, u32[]{:S(2)}) collective-permute-start(f32[112,256]{1,0:T(8,128)S(1)} %add.35), channel_id=1, source_target_pairs={{0,64},{1,17},{2,66},{3,19},{4,68},{5,21},{6,70},{7,23},{8,72},{9,... | collective-permute-start | bytes 344072 | tf_op jit(solution)/shard_map/ppermute | solution.py:517
  18.2 5.4 %collective-permute-start.3 = (f32[112,256]{1,0:T(8,128)S(1)}, f32[112,256]{1,0:T(8,128)S(1)}, u32[]{:S(2)}, u32[]{:S(2)}) collective-permute-start(f32[112,256]{1,0:T(8,128)S(1)} %add.35), channel_id=1, source_target_pairs={{0,96},{1,9},{2,98},{3,11},{4,100},{5,13},{6,102},{7,15},{8,104},{... | collective-permute-start | bytes 344072 | tf_op jit(solution)/shard_map/ppermute | solution.py:517
  18.3 6.6 %collective-permute-start.2 = (f32[112,256]{1,0:T(8,128)S(1)}, f32[112,256]{1,0:T(8,128)S(1)}, u32[]{:S(2)}, u32[]{:S(2)}) collective-permute-start(f32[112,256]{1,0:T(8,128)S(1)} %add.35), channel_id=1, source_target_pairs={{0,32},{1,25},{2,34},{3,27},{4,36},{5,29},{6,38},{7,31},{8,40},{9,... | collective-permute-start | bytes 344072 | tf_op jit(solution)/shard_map/ppermute | solution.py:517
  24.9 5.2 %collective-permute-start.7 = (f32[112,256]{1,0:T(8,128)S(1)}, f32[112,256]{1,0:T(8,128)S(1)}, u32[]{:S(2)}, u32[]{:S(2)}) collective-permute-start(f32[112,256]{1,0:T(8,128)S(1)} %add_add_fusion.2), channel_id=1, source_target_pairs={{0,16},{1,5},{2,18},{3,7},{4,20},{5,1},{6,22},{7,3},{8,24},{9,13},... | collective-permute-start | bytes 344072 | tf_op jit(solution)/shard_map/ppermute | solution.py:517
  27.8 4.0 %collective-permute-start.6 = (f32[112,256]{1,0:T(8,128)S(1)}, f32[112,256]{1,0:T(8,128)S(1)}, u32[]{:S(2)}, u32[]{:S(2)}) collective-permute-start(f32[112,256]{1,0:T(8,128)S(1)} %add_add_fusion.2), channel_id=1, source_target_pairs={{0,24},{1,3},{2,26},{3,1},{4,28},{5,7},{6,30},{7,5},{8,16},{9,11},... | collective-permute-start | bytes 344072 | tf_op jit(solution)/shard_map/ppermute | solution.py:517
  28.1 5.1 %collective-permute-start.5 = (f32[112,256]{1,0:T(8,128)S(1)}, f32[112,256]{1,0:T(8,128)S(1)}, u32[]{:S(2)}, u32[]{:S(2)}) collective-permute-start(f32[112,256]{1,0:T(8,128)S(1)} %add_add_fusion.2), channel_id=1, source_target_pairs={{0,8},{1,7},{2,10},{3,5},{4,12},{5,3},{6,14},{7,1},{8,0},{9,15},{1... | collective-permute-start | bytes 344072 | tf_op jit(solution)/shard_map/ppermute | solution.py:517
  33.2 5.2 %collective-permute-start.10 = (f32[112,256]{1,0:T(8,128)S(1)}, f32[112,256]{1,0:T(8,128)S(1)}, u32[]{:S(2)}, u32[]{:S(2)}) collective-permute-start(f32[112,256]{1,0:T(8,128)S(1)} %add_add_fusion.1), channel_id=1, source_target_pairs={{0,4},{1,65},{2,6},{3,67},{4,0},{5,69},{6,2},{7,71},{8,12},{9,73},... | collective-permute-start | bytes 344072 | tf_op jit(solution)/shard_map/ppermute | solution.py:517
  34.2 4.2 %collective-permute-start.9 = (f32[112,256]{1,0:T(8,128)S(1)}, f32[112,256]{1,0:T(8,128)S(1)}, u32[]{:S(2)}, u32[]{:S(2)}) collective-permute-start(f32[112,256]{1,0:T(8,128)S(1)} %add_add_fusion.1), channel_id=1, source_target_pairs={{0,6},{1,33},{2,4},{3,35},{4,2},{5,37},{6,0},{7,39},{8,14},{9,41},... | collective-permute-start | bytes 344072 | tf_op jit(solution)/shard_map/ppermute | solution.py:517
  34.9 5.1 %collective-permute-start.8 = (f32[112,256]{1,0:T(8,128)S(1)}, f32[112,256]{1,0:T(8,128)S(1)}, u32[]{:S(2)}, u32[]{:S(2)}) collective-permute-start(f32[112,256]{1,0:T(8,128)S(1)} %add_add_fusion.1), channel_id=1, source_target_pairs={{0,2},{1,97},{2,0},{3,99},{4,6},{5,101},{6,4},{7,103},{8,10},{9,10... | collective-permute-start | bytes 344072 | tf_op jit(solution)/shard_map/ppermute | solution.py:517
  40.1 4.4 %collective-permute-start.11 = (f32[112,256]{1,0:T(8,128)S(1)}, f32[112,256]{1,0:T(8,128)S(1)}, u32[]{:S(2)}, u32[]{:S(2)}) collective-permute-start(f32[112,256]{1,0:T(8,128)S(1)} %add_add_fusion.mine_ref), channel_id=1, source_target_pairs={{0,1},{1,0},{2,3},{3,2},{4,5},{5,4},{6,7},{7,6},{8,9},{9,8},{10,11... | collective-permute-start | bytes 344072 | tf_op jit(solution)/shard_map/ppermute | solution.py:517

commit v9 on v8

--- a/solution.py
+++ b/solution.py
@@ -546,7 +546,7 @@
     halves, valid, first, sums, steps, seams, rest = moments(mask, cube)
     mine, other = pack(core, track, valid, first, above, sums, steps, seams, rest)
     total = mine + other_core(other)
-    for axes in ((0, 1), (1, 2), (2, 0)):
+    for axes in ((2, 0), (0, 1), (1, 2)):
         total = ring_sum(total, axes)
     weights = solve(core, total, other_core(total), bands)
     return apply_filter(halves, valid, weights, cube.shape)

time: 54.3 us -> 54.3 us (level)
  transfers between devices with their start and end apart: 12 -> 12, of which waited for: 10 -> 11; matrix products, arithmetic and copies ran while one was open for 0% -> 0% of each run, Pallas kernels for 15% -> 15%
where the time goes in v9:
time: 54.3 us; the launch traced here: 54.2 us
  Pallas kernels  19.7 us (36%)
  starting transfers between devices  17.9 us (33%)
  waiting for transfers between devices  16.3 us (30%)
    ppermute x11, starting transfers between devices, permute(): return lax.ppermute(x, ('track', 'strip'), pairs)  15.4 us
    ppermute x11, waiting for transfers between devices, permute(): return lax.ppermute(x, ('track', 'strip'), pairs)  13.1 us
    pallas_call x1, Pallas kernels, moments(): pl.pallas_call(moments_kernel, out_shape=[pltpu.VMEM((pixels, 2 * W), BF1...  8.07 us
    pallas_call x1, Pallas kernels, apply_filter(): pl.pallas_call(filter_kernel, out_shape=jax.ShapeDtypeStruct(shape, F32),...  5.86 us
    pallas_call x1, Pallas kernels, solve(): pl.pallas_call(functools.partial(solve_kernel, bands), out_shape=pltpu.VM...  3.75 us
    ppermute x1, waiting for transfers between devices, per_device(): lax.ppermute(final_row(mask, cube), 'track', [(i, (i + 1) % size) for i i...  3.22 us
    ppermute x1, starting transfers between devices, per_device(): lax.ppermute(final_row(mask, cube), 'track', [(i, (i + 1) % size) for i i...  2.54 us
  transfers between devices with their start and end apart: 12, of which 11 were waited for; matrix products, arithmetic and copies ran while one was open for 0% of the time, Pallas kernels for 15%

profile of v9, /device:TPU:1, one launch (start us, length us, event | category | flops | bytes accessed | tf_op | source)
XLA Modules:
  0.0 54.2 jit_solution(16177388410968199499)
XLA Ops:
  0.0 0.0 copy-start
  0.0 1.0 %fetch_row.1.row_ref = f32[320,224]{1,0:T(8,128)S(1)} custom-call(f32[32,320,224]{2,1,0:T(8,128)} %cube_hbm.3), custom_call_target="tpu_custom_call" | custom-call | tf_op jit(solution)/shard_map/fetch_row/pallas_call | solution.py:105
  1.0 0.0 copy-done
  1.0 0.1 fold_row.1
  1.1 2.5 %collective-permute-start = (f32[288,256]{1,0:T(8,128)S(1)}, f32[288,256]{1,0:T(8,128)S(1)}, u32[]{:S(2)}, u32[]{:S(2)}) collective-permute-start(f32[288,256]{1,0:T(8,128)S(1)} %fold_row.1), channel_id=1, source_target_pairs={{0,8},{8,16},{16,24},{24,32},{32,40},{40,48},{48,56},{56,64},{64,7... | collective-permute-start | bytes 884744 | tf_op jit(solution)/shard_map/ppermute | solution.py:543
  3.7 8.1 %moments.1 = (bf16[10240,512]{1,0:T(8,128)(2,1)S(1)}, f32[4,320,256]{2,1,0:T(8,128)S(1)}, f32[320,224]{1,0:T(8,128)S(1)}, f32[256,512]{1,0:T(8,128)S(1)}, f32[25...) custom-call(s32[4,40]{1,0:T(4,128)S(1)} %copy-done, f32[32,320,224]{2,1,0:T(8,128)} %cube_hbm.3), custom_call_target="tpu_custom_call" | custom-call | flops 4026531840 | bytes 10485760 | tf_op jit(solution)/shard_map/moments/pallas_call | solution.py:235
  11.7 3.2 %collective-permute-done.above_ref = f32[288,256]{1,0:T(8,128)S(1)} collective-permute-done((f32[288,256]{1,0:T(8,128)S(1)}, f32[288,256]{1,0:T(8,128)S(1)}, u32[]{:S(2)}, u32[]{:S(2)}) %collective-permute-start) | collective-permute-done | bytes 294944 | tf_op jit(solution)/shard_map/ppermute | solution.py:543
  15.0 0.9 %pack.1 = (f32[112,256]{1,0:T(8,128)S(1)}, f32[112,256]{1,0:T(8,128)S(1)}) custom-call(s32[1]{0:T(128)} %bitcast.core_ref, s32[1]{0:T(128)} %bitcast.1.track_ref, f32[4,320,256]{2,1,0:T(8,128)S(1)} %get-tuple-element.15.valid_ref, f32[320,224]{1,0:T(8,128)S(1)} %get-tuple-element.16.first_ref, f32[288,256]{1,0:T(8,128)S(1)} %collective-permute-done.above_ref, ...), custom_call_target="tpu_custom_call" | custom-call | tf_op jit(solution)/shard_map/pack/pallas_call | solution.py:320
  15.8 1.3 %collective-permute-start.1 = (f32[112,256]{1,0:T(8,128)S(1)}, f32[112,256]{1,0:T(8,128)S(1)}, u32[]{:S(2)}, u32[]{:S(2)}) collective-permute-start(f32[112,256]{1,0:T(8,128)S(1)} %get-tuple-element.22), channel_id=1, source_target_pairs={{0,1},{1,0},{2,3},{3,2},{4,5},{5,4},{6,7},{7,6},{8,9},{9,8},{10,11... | collective-permute-start | bytes 344072 | tf_op jit(solution)/shard_map/ppermute | solution.py:517
  17.2 1.0 %collective-permute-done.1 = f32[112,256]{1,0:T(8,128)S(1)} collective-permute-done((f32[112,256]{1,0:T(8,128)S(1)}, f32[112,256]{1,0:T(8,128)S(1)}, u32[]{:S(2)}, u32[]{:S(2)}) %collective-permute-start.1) | collective-permute-done | bytes 114720 | tf_op jit(solution)/shard_map/ppermute | solution.py:517
  18.1 0.4 collective-permute-start.4
  18.6 0.7 %collective-permute-start.3 = (f32[112,256]{1,0:T(8,128)S(1)}, f32[112,256]{1,0:T(8,128)S(1)}, u32[]{:S(2)}, u32[]{:S(2)}) collective-permute-start(f32[112,256]{1,0:T(8,128)S(1)} %add.35), channel_id=1, source_target_pairs={{0,6},{1,33},{2,4},{3,35},{4,2},{5,37},{6,0},{7,39},{8,14},{9,41},... | collective-permute-start | bytes 344072 | tf_op jit(solution)/shard_map/ppermute | solution.py:517
  19.3 2.2 %collective-permute-start.2 = (f32[112,256]{1,0:T(8,128)S(1)}, f32[112,256]{1,0:T(8,128)S(1)}, u32[]{:S(2)}, u32[]{:S(2)}) collective-permute-start(f32[112,256]{1,0:T(8,128)S(1)} %add.35), channel_id=1, source_target_pairs={{0,2},{1,97},{2,0},{3,99},{4,6},{5,101},{6,4},{7,103},{8,10},{9,10... | collective-permute-start | bytes 344072 | tf_op jit(solution)/shard_map/ppermute | solution.py:517
  21.5 2.2 %collective-permute-done.4 = f32[112,256]{1,0:T(8,128)S(1)} collective-permute-done((f32[112,256]{1,0:T(8,128)S(1)}, f32[112,256]{1,0:T(8,128)S(1)}, u32[]{:S(2)}, u32[]{:S(2)}) %collective-permute-start.4) | collective-permute-done | bytes 114720 | tf_op jit(solution)/shard_map/ppermute | solution.py:517
  23.7 0.0 collective-permute-done.3
  23.7 0.9 %collective-permute-done.2 = f32[112,256]{1,0:T(8,128)S(1)} collective-permute-done((f32[112,256]{1,0:T(8,128)S(1)}, f32[112,256]{1,0:T(8,128)S(1)}, u32[]{:S(2)}, u32[]{:S(2)}) %collective-permute-start.2) | collective-permute-done | bytes 114720 | tf_op jit(solution)/shard_map/ppermute | solution.py:517
  24.6 2.0 %collective-permute-start.7 = (f32[112,256]{1,0:T(8,128)S(1)}, f32[112,256]{1,0:T(8,128)S(1)}, u32[]{:S(2)}, u32[]{:S(2)}) collective-permute-start(f32[112,256]{1,0:T(8,128)S(1)} %add_add_fusion.2), channel_id=1, source_target_pairs={{0,64},{1,17},{2,66},{3,19},{4,68},{5,21},{6,70},{7,23},{8,72},{9,... | collective-permute-start | bytes 344072 | tf_op jit(solution)/shard_map/ppermute | solution.py:517
  26.6 0.0 collective-permute-start.6
  26.6 1.3 %collective-permute-start.5 = (f32[112,256]{1,0:T(8,128)S(1)}, f32[112,256]{1,0:T(8,128)S(1)}, u32[]{:S(2)}, u32[]{:S(2)}) collective-permute-start(f32[112,256]{1,0:T(8,128)S(1)} %add_add_fusion.2), channel_id=1, source_target_pairs={{0,32},{1,25},{2,34},{3,27},{4,36},{5,29},{6,38},{7,31},{8,40},{9,... | collective-permute-start | bytes 344072 | tf_op jit(solution)/shard_map/ppermute | solution.py:517
  28.0 1.9 %collective-permute-done.7 = f32[112,256]{1,0:T(8,128)S(1)} collective-permute-done((f32[112,256]{1,0:T(8,128)S(1)}, f32[112,256]{1,0:T(8,128)S(1)}, u32[]{:S(2)}, u32[]{:S(2)}) %collective-permute-start.7) | collective-permute-done | bytes 114720 | tf_op jit(solution)/shard_map/ppermute | solution.py:517
  29.9 0.4 collective-permute-done.6
  30.3 1.2 %collective-permute-done.5 = f32[112,256]{1,0:T(8,128)S(1)} collective-permute-done((f32[112,256]{1,0:T(8,128)S(1)}, f32[112,256]{1,0:T(8,128)S(1)}, u32[]{:S(2)}, u32[]{:S(2)}) %collective-permute-start.5) | collective-permute-done | bytes 114720 | tf_op jit(solution)/shard_map/ppermute | solution.py:517
  31.5 2.8 %collective-permute-start.10 = (f32[112,256]{1,0:T(8,128)S(1)}, f32[112,256]{1,0:T(8,128)S(1)}, u32[]{:S(2)}, u32[]{:S(2)}) collective-permute-start(f32[112,256]{1,0:T(8,128)S(1)} %add_add_fusion.1), channel_id=1, source_target_pairs={{0,16},{1,5},{2,18},{3,7},{4,20},{5,1},{6,22},{7,3},{8,24},{9,13},... | collective-permute-start | bytes 344072 | tf_op jit(solution)/shard_map/ppermute | solution.py:517
  34.3 0.5 collective-permute-start.9
  34.8 0.3 collective-permute-start.8
  35.2 1.5 %collective-permute-done.10 = f32[112,256]{1,0:T(8,128)S(1)} collective-permute-done((f32[112,256]{1,0:T(8,128)S(1)}, f32[112,256]{1,0:T(8,128)S(1)}, u32[]{:S(2)}, u32[]{:S(2)}) %collective-permute-start.10) | collective-permute-done | bytes 114720 | tf_op jit(solution)/shard_map/ppermute | solution.py:517
  36.7 1.5 %collective-permute-done.9 = f32[112,256]{1,0:T(8,128)S(1)} collective-permute-done((f32[112,256]{1,0:T(8,128)S(1)}, f32[112,256]{1,0:T(8,128)S(1)}, u32[]{:S(2)}, u32[]{:S(2)}) %collective-permute-start.9) | collective-permute-done | bytes 114720 | tf_op jit(solution)/shard_map/ppermute | solution.py:517
  38.3 1.4 %collective-permute-done.8 = f32[112,256]{1,0:T(8,128)S(1)} collective-permute-done((f32[112,256]{1,0:T(8,128)S(1)}, f32[112,256]{1,0:T(8,128)S(1)}, u32[]{:S(2)}, u32[]{:S(2)}) %collective-permute-start.8) | collective-permute-done | bytes 114720 | tf_op jit(solution)/shard_map/ppermute | solution.py:517
  39.7 3.7 %collective-permute-start.11 = (f32[112,256]{1,0:T(8,128)S(1)}, f32[112,256]{1,0:T(8,128)S(1)}, u32[]{:S(2)}, u32[]{:S(2)}) collective-permute-start(f32[112,256]{1,0:T(8,128)S(1)} %add_add_fusion.mine_ref), channel_id=1, source_target_pairs={{0,1},{1,0},{2,3},{3,2},{4,5},{5,4},{6,7},{7,6},{8,9},{9,8},{10,11... | collective-permute-start | bytes 344072 | tf_op jit(solution)/shard_map/ppermute | solution.py:517
  43.5 1.0 %collective-permute-done.11.other_ref = f32[112,256]{1,0:T(8,128)S(1)} collective-permute-done((f32[112,256]{1,0:T(8,128)S(1)}, f32[112,256]{1,0:T(8,128)S(1)}, u32[]{:S(2)}, u32[]{:S(2)}) %collective-permute-start.11) | collective-permute-done | bytes 114720 | tf_op jit(solution)/shard_map/ppermute | solution.py:517
  44.4 3.7 %solve.1.weights_ref = bf16[768,256]{1,0:T(8,128)(2,1)S(1)} custom-call(s32[1]{0:T(128)} %bitcast.core_ref, f32[112,256]{1,0:T(8,128)S(1)} %add_add_fusion.mine_ref, f32[112,256]{1,0:T(8,128)S(1)} %collective-permute-done.11.other_ref), custom_call_target="tpu_custom_call" | custom-call | tf_op jit(solution)/shard_map/solve/pallas_call | solution.py:460
  48.2 5.9 %filter.1 = f32[32,320,224]{2,1,0:T(8,128)} custom-call(bf16[10240,512]{1,0:T(8,128)(2,1)S(1)} %get-tuple-element.14.halves_ref, f32[4,320,256]{2,1,0:T(8,128)S(1)} %get-tuple-element.15.valid_ref, bf16[768,256]{1,0:T(8,128)(2,1)S(1)} %solve.1.weights_ref), custom_call_target="tpu_custom_call" | custom-call | flops 4026531840 | bytes 10485760 | tf_op jit(solution)/shard_map/filter/pallas_call | solution.py:495
  (4 shorter events, 0.1 us)
Async XLA Ops:
  0.0 1.0 %copy-start = (s32[4,40]{1,0:T(4,128)S(1)}, s32[4,40]{1,0:T(4,128)}, u32[]{:S(2)}) copy-start(s32[4,40]{1,0:T(4,128)} %mask_ref.1) | copy-start | bytes 1924
  1.1 13.8 %collective-permute-start = (f32[288,256]{1,0:T(8,128)S(1)}, f32[288,256]{1,0:T(8,128)S(1)}, u32[]{:S(2)}, u32[]{:S(2)}) collective-permute-start(f32[288,256]{1,0:T(8,128)S(1)} %fold_row.1), channel_id=1, source_target_pairs={{0,8},{8,16},{16,24},{24,32},{32,40},{40,48},{48,56},{56,64},{64,7... | collective-permute-start | bytes 884744 | tf_op jit(solution)/shard_map/ppermute | solution.py:543
  15.8 2.3 %collective-permute-start.1 = (f32[112,256]{1,0:T(8,128)S(1)}, f32[112,256]{1,0:T(8,128)S(1)}, u32[]{:S(2)}, u32[]{:S(2)}) collective-permute-start(f32[112,256]{1,0:T(8,128)S(1)} %get-tuple-element.22), channel_id=1, source_target_pairs={{0,1},{1,0},{2,3},{3,2},{4,5},{5,4},{6,7},{7,6},{8,9},{9,8},{10,11... | collective-permute-start | bytes 344072 | tf_op jit(solution)/shard_map/ppermute | solution.py:517
  18.1 5.5 %collective-permute-start.4 = (f32[112,256]{1,0:T(8,128)S(1)}, f32[112,256]{1,0:T(8,128)S(1)}, u32[]{:S(2)}, u32[]{:S(2)}) collective-permute-start(f32[112,256]{1,0:T(8,128)S(1)} %add.35), channel_id=1, source_target_pairs={{0,4},{1,65},{2,6},{3,67},{4,0},{5,69},{6,2},{7,71},{8,12},{9,73},... | collective-permute-start | bytes 344072 | tf_op jit(solution)/shard_map/ppermute | solution.py:517
  18.6 5.1 %collective-permute-start.3 = (f32[112,256]{1,0:T(8,128)S(1)}, f32[112,256]{1,0:T(8,128)S(1)}, u32[]{:S(2)}, u32[]{:S(2)}) collective-permute-start(f32[112,256]{1,0:T(8,128)S(1)} %add.35), channel_id=1, source_target_pairs={{0,6},{1,33},{2,4},{3,35},{4,2},{5,37},{6,0},{7,39},{8,14},{9,41},... | collective-permute-start | bytes 344072 | tf_op jit(solution)/shard_map/ppermute | solution.py:517
  19.3 5.3 %collective-permute-start.2 = (f32[112,256]{1,0:T(8,128)S(1)}, f32[112,256]{1,0:T(8,128)S(1)}, u32[]{:S(2)}, u32[]{:S(2)}) collective-permute-start(f32[112,256]{1,0:T(8,128)S(1)} %add.35), channel_id=1, source_target_pairs={{0,2},{1,97},{2,0},{3,99},{4,6},{5,101},{6,4},{7,103},{8,10},{9,10... | collective-permute-start | bytes 344072 | tf_op jit(solution)/shard_map/ppermute | solution.py:517
  24.6 5.2 %collective-permute-start.7 = (f32[112,256]{1,0:T(8,128)S(1)}, f32[112,256]{1,0:T(8,128)S(1)}, u32[]{:S(2)}, u32[]{:S(2)}) collective-permute-start(f32[112,256]{1,0:T(8,128)S(1)} %add_add_fusion.2), channel_id=1, source_target_pairs={{0,64},{1,17},{2,66},{3,19},{4,68},{5,21},{6,70},{7,23},{8,72},{9,... | collective-permute-start | bytes 344072 | tf_op jit(solution)/shard_map/ppermute | solution.py:517
  26.6 3.6 %collective-permute-start.6 = (f32[112,256]{1,0:T(8,128)S(1)}, f32[112,256]{1,0:T(8,128)S(1)}, u32[]{:S(2)}, u32[]{:S(2)}) collective-permute-start(f32[112,256]{1,0:T(8,128)S(1)} %add_add_fusion.2), channel_id=1, source_target_pairs={{0,96},{1,9},{2,98},{3,11},{4,100},{5,13},{6,102},{7,15},{8,104},{... | collective-permute-start | bytes 344072 | tf_op jit(solution)/shard_map/ppermute | solution.py:517
  26.6 4.9 %collective-permute-start.5 = (f32[112,256]{1,0:T(8,128)S(1)}, f32[112,256]{1,0:T(8,128)S(1)}, u32[]{:S(2)}, u32[]{:S(2)}) collective-permute-start(f32[112,256]{1,0:T(8,128)S(1)} %add_add_fusion.2), channel_id=1, source_target_pairs={{0,32},{1,25},{2,34},{3,27},{4,36},{5,29},{6,38},{7,31},{8,40},{9,... | collective-permute-start | bytes 344072 | tf_op jit(solution)/shard_map/ppermute | solution.py:517
  31.5 5.2 %collective-permute-start.10 = (f32[112,256]{1,0:T(8,128)S(1)}, f32[112,256]{1,0:T(8,128)S(1)}, u32[]{:S(2)}, u32[]{:S(2)}) collective-permute-start(f32[112,256]{1,0:T(8,128)S(1)} %add_add_fusion.1), channel_id=1, source_target_pairs={{0,16},{1,5},{2,18},{3,7},{4,20},{5,1},{6,22},{7,3},{8,24},{9,13},... | collective-permute-start | bytes 344072 | tf_op jit(solution)/shard_map/ppermute | solution.py:517
  34.3 3.9 %collective-permute-start.9 = (f32[112,256]{1,0:T(8,128)S(1)}, f32[112,256]{1,0:T(8,128)S(1)}, u32[]{:S(2)}, u32[]{:S(2)}) collective-permute-start(f32[112,256]{1,0:T(8,128)S(1)} %add_add_fusion.1), channel_id=1, source_target_pairs={{0,24},{1,3},{2,26},{3,1},{4,28},{5,7},{6,30},{7,5},{8,16},{9,11},... | collective-permute-start | bytes 344072 | tf_op jit(solution)/shard_map/ppermute | solution.py:517
  34.8 4.9 %collective-permute-start.8 = (f32[112,256]{1,0:T(8,128)S(1)}, f32[112,256]{1,0:T(8,128)S(1)}, u32[]{:S(2)}, u32[]{:S(2)}) collective-permute-start(f32[112,256]{1,0:T(8,128)S(1)} %add_add_fusion.1), channel_id=1, source_target_pairs={{0,8},{1,7},{2,10},{3,5},{4,12},{5,3},{6,14},{7,1},{8,0},{9,15},{1... | collective-permute-start | bytes 344072 | tf_op jit(solution)/shard_map/ppermute | solution.py:517
  39.7 4.7 %collective-permute-start.11 = (f32[112,256]{1,0:T(8,128)S(1)}, f32[112,256]{1,0:T(8,128)S(1)}, u32[]{:S(2)}, u32[]{:S(2)}) collective-permute-start(f32[112,256]{1,0:T(8,128)S(1)} %add_add_fusion.mine_ref), channel_id=1, source_target_pairs={{0,1},{1,0},{2,3},{3,2},{4,5},{5,4},{6,7},{7,6},{8,9},{9,8},{10,11... | collective-permute-start | bytes 344072 | tf_op jit(solution)/shard_map/ppermute | solution.py:517

commit v10 on v9

--- a/solution.py
+++ b/solution.py
@@ -546,7 +546,7 @@
     halves, valid, first, sums, steps, seams, rest = moments(mask, cube)
     mine, other = pack(core, track, valid, first, above, sums, steps, seams, rest)
     total = mine + other_core(other)
-    for axes in ((2, 0), (0, 1), (1, 2)):
+    for axes in ((2, 0), (0, 2), (1, 1)):
         total = ring_sum(total, axes)
     weights = solve(core, total, other_core(total), bands)
     return apply_filter(halves, valid, weights, cube.shape)

time: 54.3 us -> 54.3 us (level)
  transfers between devices with their start and end apart: 12 -> 12, of which waited for: 11 -> 10; matrix products, arithmetic and copies ran while one was open for 0% -> 0% of each run, Pallas kernels for 15% -> 15%
where the time goes in v10:
time: 54.3 us; the launch traced here: 54.2 us
  Pallas kernels  19.7 us (36%)
  starting transfers between devices  17.4 us (32%)
  waiting for transfers between devices  16.8 us (31%)
    ppermute x11, starting transfers between devices, permute(): return lax.ppermute(x, ('track', 'strip'), pairs)  14.9 us
    ppermute x11, waiting for transfers between devices, permute(): return lax.ppermute(x, ('track', 'strip'), pairs)  13.5 us
    pallas_call x1, Pallas kernels, moments(): pl.pallas_call(moments_kernel, out_shape=[pltpu.VMEM((pixels, 2 * W), BF1...  8.07 us
    pallas_call x1, Pallas kernels, apply_filter(): pl.pallas_call(filter_kernel, out_shape=jax.ShapeDtypeStruct(shape, F32),...  5.86 us
    pallas_call x1, Pallas kernels, solve(): pl.pallas_call(functools.partial(solve_kernel, bands), out_shape=pltpu.VM...  3.75 us
    ppermute x1, waiting for transfers between devices, per_device(): lax.ppermute(final_row(mask, cube), 'track', [(i, (i + 1) % size) for i i...  3.22 us
    ppermute x1, starting transfers between devices, per_device(): lax.ppermute(final_row(mask, cube), 'track', [(i, (i + 1) % size) for i i...  2.54 us
  transfers between devices with their start and end apart: 12, of which 10 were waited for; matrix products, arithmetic and copies ran while one was open for 0% of the time, Pallas kernels for 15%

profile of v10, /device:TPU:1, one launch (start us, length us, event | category | flops | bytes accessed | tf_op | source)
XLA Modules:
  0.0 54.2 jit_solution(2669358142453017746)
XLA Ops:
  0.0 0.0 copy-start
  0.0 1.0 %fetch_row.1.row_ref = f32[320,224]{1,0:T(8,128)S(1)} custom-call(f32[32,320,224]{2,1,0:T(8,128)} %cube_hbm.3), custom_call_target="tpu_custom_call" | custom-call | tf_op jit(solution)/shard_map/fetch_row/pallas_call | solution.py:105
  1.0 0.0 copy-done
  1.0 0.1 fold_row.1
  1.1 2.5 %collective-permute-start = (f32[288,256]{1,0:T(8,128)S(1)}, f32[288,256]{1,0:T(8,128)S(1)}, u32[]{:S(2)}, u32[]{:S(2)}) collective-permute-start(f32[288,256]{1,0:T(8,128)S(1)} %fold_row.1), channel_id=1, source_target_pairs={{0,8},{8,16},{16,24},{24,32},{32,40},{40,48},{48,56},{56,64},{64,7... | collective-permute-start | bytes 884744 | tf_op jit(solution)/shard_map/ppermute | solution.py:543
  3.7 8.1 %moments.1 = (bf16[10240,512]{1,0:T(8,128)(2,1)S(1)}, f32[4,320,256]{2,1,0:T(8,128)S(1)}, f32[320,224]{1,0:T(8,128)S(1)}, f32[256,512]{1,0:T(8,128)S(1)}, f32[25...) custom-call(s32[4,40]{1,0:T(4,128)S(1)} %copy-done, f32[32,320,224]{2,1,0:T(8,128)} %cube_hbm.3), custom_call_target="tpu_custom_call" | custom-call | flops 4026531840 | bytes 10485760 | tf_op jit(solution)/shard_map/moments/pallas_call | solution.py:235
  11.7 3.2 %collective-permute-done.above_ref = f32[288,256]{1,0:T(8,128)S(1)} collective-permute-done((f32[288,256]{1,0:T(8,128)S(1)}, f32[288,256]{1,0:T(8,128)S(1)}, u32[]{:S(2)}, u32[]{:S(2)}) %collective-permute-start) | collective-permute-done | bytes 294944 | tf_op jit(solution)/shard_map/ppermute | solution.py:543
  15.0 0.9 %pack.1 = (f32[112,256]{1,0:T(8,128)S(1)}, f32[112,256]{1,0:T(8,128)S(1)}) custom-call(s32[1]{0:T(128)} %bitcast.core_ref, s32[1]{0:T(128)} %bitcast.1.track_ref, f32[4,320,256]{2,1,0:T(8,128)S(1)} %get-tuple-element.15.valid_ref, f32[320,224]{1,0:T(8,128)S(1)} %get-tuple-element.16.first_ref, f32[288,256]{1,0:T(8,128)S(1)} %collective-permute-done.above_ref, ...), custom_call_target="tpu_custom_call" | custom-call | tf_op jit(solution)/shard_map/pack/pallas_call | solution.py:320
  15.8 1.3 %collective-permute-start.1 = (f32[112,256]{1,0:T(8,128)S(1)}, f32[112,256]{1,0:T(8,128)S(1)}, u32[]{:S(2)}, u32[]{:S(2)}) collective-permute-start(f32[112,256]{1,0:T(8,128)S(1)} %get-tuple-element.22), channel_id=1, source_target_pairs={{0,1},{1,0},{2,3},{3,2},{4,5},{5,4},{6,7},{7,6},{8,9},{9,8},{10,11... | collective-permute-start | bytes 344072 | tf_op jit(solution)/shard_map/ppermute | solution.py:517
  17.2 1.0 %collective-permute-done.1 = f32[112,256]{1,0:T(8,128)S(1)} collective-permute-done((f32[112,256]{1,0:T(8,128)S(1)}, f32[112,256]{1,0:T(8,128)S(1)}, u32[]{:S(2)}, u32[]{:S(2)}) %collective-permute-start.1) | collective-permute-done | bytes 114720 | tf_op jit(solution)/shard_map/ppermute | solution.py:517
  18.1 0.4 collective-permute-start.4
  18.6 0.7 %collective-permute-start.3 = (f32[112,256]{1,0:T(8,128)S(1)}, f32[112,256]{1,0:T(8,128)S(1)}, u32[]{:S(2)}, u32[]{:S(2)}) collective-permute-start(f32[112,256]{1,0:T(8,128)S(1)} %add.35), channel_id=1, source_target_pairs={{0,6},{1,33},{2,4},{3,35},{4,2},{5,37},{6,0},{7,39},{8,14},{9,41},... | collective-permute-start | bytes 344072 | tf_op jit(solution)/shard_map/ppermute | solution.py:517
  19.3 2.2 %collective-permute-start.2 = (f32[112,256]{1,0:T(8,128)S(1)}, f32[112,256]{1,0:T(8,128)S(1)}, u32[]{:S(2)}, u32[]{:S(2)}) collective-permute-start(f32[112,256]{1,0:T(8,128)S(1)} %add.35), channel_id=1, source_target_pairs={{0,2},{1,97},{2,0},{3,99},{4,6},{5,101},{6,4},{7,103},{8,10},{9,10... | collective-permute-start | bytes 344072 | tf_op jit(solution)/shard_map/ppermute | solution.py:517
  21.5 2.2 %collective-permute-done.4 = f32[112,256]{1,0:T(8,128)S(1)} collective-permute-done((f32[112,256]{1,0:T(8,128)S(1)}, f32[112,256]{1,0:T(8,128)S(1)}, u32[]{:S(2)}, u32[]{:S(2)}) %collective-permute-start.4) | collective-permute-done | bytes 114720 | tf_op jit(solution)/shard_map/ppermute | solution.py:517
  23.7 0.0 collective-permute-done.3
  23.7 0.9 %collective-permute-done.2 = f32[112,256]{1,0:T(8,128)S(1)} collective-permute-done((f32[112,256]{1,0:T(8,128)S(1)}, f32[112,256]{1,0:T(8,128)S(1)}, u32[]{:S(2)}, u32[]{:S(2)}) %collective-permute-start.2) | collective-permute-done | bytes 114720 | tf_op jit(solution)/shard_map/ppermute | solution.py:517
  24.6 2.8 %collective-permute-start.7 = (f32[112,256]{1,0:T(8,128)S(1)}, f32[112,256]{1,0:T(8,128)S(1)}, u32[]{:S(2)}, u32[]{:S(2)}) collective-permute-start(f32[112,256]{1,0:T(8,128)S(1)} %add_add_fusion.2), channel_id=1, source_target_pairs={{0,64},{1,5},{2,66},{3,7},{4,68},{5,1},{6,70},{7,3},{8,72},{9,13},... | collective-permute-start | bytes 344072 | tf_op jit(solution)/shard_map/ppermute | solution.py:517
  27.5 0.6 %collective-permute-start.6 = (f32[112,256]{1,0:T(8,128)S(1)}, f32[112,256]{1,0:T(8,128)S(1)}, u32[]{:S(2)}, u32[]{:S(2)}) collective-permute-start(f32[112,256]{1,0:T(8,128)S(1)} %add_add_fusion.2), channel_id=1, source_target_pairs={{0,96},{1,3},{2,98},{3,1},{4,100},{5,7},{6,102},{7,5},{8,104},{9,1... | collective-permute-start | bytes 344072 | tf_op jit(solution)/shard_map/ppermute | solution.py:517
  28.1 0.3 collective-permute-start.5
  28.3 1.5 %collective-permute-done.7 = f32[112,256]{1,0:T(8,128)S(1)} collective-permute-done((f32[112,256]{1,0:T(8,128)S(1)}, f32[112,256]{1,0:T(8,128)S(1)}, u32[]{:S(2)}, u32[]{:S(2)}) %collective-permute-start.7) | collective-permute-done | bytes 114720 | tf_op jit(solution)/shard_map/ppermute | solution.py:517
  29.9 1.6 %collective-permute-done.6 = f32[112,256]{1,0:T(8,128)S(1)} collective-permute-done((f32[112,256]{1,0:T(8,128)S(1)}, f32[112,256]{1,0:T(8,128)S(1)}, u32[]{:S(2)}, u32[]{:S(2)}) %collective-permute-start.6) | collective-permute-done | bytes 114720 | tf_op jit(solution)/shard_map/ppermute | solution.py:517
  31.5 1.7 %collective-permute-done.5 = f32[112,256]{1,0:T(8,128)S(1)} collective-permute-done((f32[112,256]{1,0:T(8,128)S(1)}, f32[112,256]{1,0:T(8,128)S(1)}, u32[]{:S(2)}, u32[]{:S(2)}) %collective-permute-start.5) | collective-permute-done | bytes 114720 | tf_op jit(solution)/shard_map/ppermute | solution.py:517
  33.2 1.1 %collective-permute-start.10 = (f32[112,256]{1,0:T(8,128)S(1)}, f32[112,256]{1,0:T(8,128)S(1)}, u32[]{:S(2)}, u32[]{:S(2)}) collective-permute-start(f32[112,256]{1,0:T(8,128)S(1)} %add_add_fusion.1), channel_id=1, source_target_pairs={{0,16},{1,17},{2,18},{3,19},{4,20},{5,21},{6,22},{7,23},{8,24},{9,... | collective-permute-start | bytes 344072 | tf_op jit(solution)/shard_map/ppermute | solution.py:517
  34.3 0.0 collective-permute-start.9
  34.3 2.2 %collective-permute-start.8 = (f32[112,256]{1,0:T(8,128)S(1)}, f32[112,256]{1,0:T(8,128)S(1)}, u32[]{:S(2)}, u32[]{:S(2)}) collective-permute-start(f32[112,256]{1,0:T(8,128)S(1)} %add_add_fusion.1), channel_id=1, source_target_pairs={{0,8},{1,25},{2,10},{3,27},{4,12},{5,29},{6,14},{7,31},{8,0},{9,17... | collective-permute-start | bytes 344072 | tf_op jit(solution)/shard_map/ppermute | solution.py:517
  36.6 1.9 %collective-permute-done.10 = f32[112,256]{1,0:T(8,128)S(1)} collective-permute-done((f32[112,256]{1,0:T(8,128)S(1)}, f32[112,256]{1,0:T(8,128)S(1)}, u32[]{:S(2)}, u32[]{:S(2)}) %collective-permute-start.10) | collective-permute-done | bytes 114720 | tf_op jit(solution)/shard_map/ppermute | solution.py:517
  38.5 0.0 collective-permute-done.9
  38.5 1.7 %collective-permute-done.8 = f32[112,256]{1,0:T(8,128)S(1)} collective-permute-done((f32[112,256]{1,0:T(8,128)S(1)}, f32[112,256]{1,0:T(8,128)S(1)}, u32[]{:S(2)}, u32[]{:S(2)}) %collective-permute-start.8) | collective-permute-done | bytes 114720 | tf_op jit(solution)/shard_map/ppermute | solution.py:517
  40.2 3.2 %collective-permute-start.11 = (f32[112,256]{1,0:T(8,128)S(1)}, f32[112,256]{1,0:T(8,128)S(1)}, u32[]{:S(2)}, u32[]{:S(2)}) collective-permute-start(f32[112,256]{1,0:T(8,128)S(1)} %add_add_fusion.mine_ref), channel_id=1, source_target_pairs={{0,1},{1,0},{2,3},{3,2},{4,5},{5,4},{6,7},{7,6},{8,9},{9,8},{10,11... | collective-permute-start | bytes 344072 | tf_op jit(solution)/shard_map/ppermute | solution.py:517
  43.5 1.0 %collective-permute-done.11.other_ref = f32[112,256]{1,0:T(8,128)S(1)} collective-permute-done((f32[112,256]{1,0:T(8,128)S(1)}, f32[112,256]{1,0:T(8,128)S(1)}, u32[]{:S(2)}, u32[]{:S(2)}) %collective-permute-start.11) | collective-permute-done | bytes 114720 | tf_op jit(solution)/shard_map/ppermute | solution.py:517
  44.4 3.7 %solve.1.weights_ref = bf16[768,256]{1,0:T(8,128)(2,1)S(1)} custom-call(s32[1]{0:T(128)} %bitcast.core_ref, f32[112,256]{1,0:T(8,128)S(1)} %add_add_fusion.mine_ref, f32[112,256]{1,0:T(8,128)S(1)} %collective-permute-done.11.other_ref), custom_call_target="tpu_custom_call" | custom-call | tf_op jit(solution)/shard_map/solve/pallas_call | solution.py:460
  48.2 5.9 %filter.1 = f32[32,320,224]{2,1,0:T(8,128)} custom-call(bf16[10240,512]{1,0:T(8,128)(2,1)S(1)} %get-tuple-element.14.halves_ref, f32[4,320,256]{2,1,0:T(8,128)S(1)} %get-tuple-element.15.valid_ref, bf16[768,256]{1,0:T(8,128)(2,1)S(1)} %solve.1.weights_ref), custom_call_target="tpu_custom_call" | custom-call | flops 4026531840 | bytes 10485760 | tf_op jit(solution)/shard_map/filter/pallas_call | solution.py:495
  (4 shorter events, 0.1 us)
Async XLA Ops:
  0.0 1.0 %copy-start = (s32[4,40]{1,0:T(4,128)S(1)}, s32[4,40]{1,0:T(4,128)}, u32[]{:S(2)}) copy-start(s32[4,40]{1,0:T(4,128)} %mask_ref.1) | copy-start | bytes 1924
  1.1 13.8 %collective-permute-start = (f32[288,256]{1,0:T(8,128)S(1)}, f32[288,256]{1,0:T(8,128)S(1)}, u32[]{:S(2)}, u32[]{:S(2)}) collective-permute-start(f32[288,256]{1,0:T(8,128)S(1)} %fold_row.1), channel_id=1, source_target_pairs={{0,8},{8,16},{16,24},{24,32},{32,40},{40,48},{48,56},{56,64},{64,7... | collective-permute-start | bytes 884744 | tf_op jit(solution)/shard_map/ppermute | solution.py:543
  15.8 2.3 %collective-permute-start.1 = (f32[112,256]{1,0:T(8,128)S(1)}, f32[112,256]{1,0:T(8,128)S(1)}, u32[]{:S(2)}, u32[]{:S(2)}) collective-permute-start(f32[112,256]{1,0:T(8,128)S(1)} %get-tuple-element.22), channel_id=1, source_target_pairs={{0,1},{1,0},{2,3},{3,2},{4,5},{5,4},{6,7},{7,6},{8,9},{9,8},{10,11... | collective-permute-start | bytes 344072 | tf_op jit(solution)/shard_map/ppermute | solution.py:517
  18.1 5.5 %collective-permute-start.4 = (f32[112,256]{1,0:T(8,128)S(1)}, f32[112,256]{1,0:T(8,128)S(1)}, u32[]{:S(2)}, u32[]{:S(2)}) collective-permute-start(f32[112,256]{1,0:T(8,128)S(1)} %add.35), channel_id=1, source_target_pairs={{0,4},{1,65},{2,6},{3,67},{4,0},{5,69},{6,2},{7,71},{8,12},{9,73},... | collective-permute-start | bytes 344072 | tf_op jit(solution)/shard_map/ppermute | solution.py:517
  18.6 5.1 %collective-permute-start.3 = (f32[112,256]{1,0:T(8,128)S(1)}, f32[112,256]{1,0:T(8,128)S(1)}, u32[]{:S(2)}, u32[]{:S(2)}) collective-permute-start(f32[112,256]{1,0:T(8,128)S(1)} %add.35), channel_id=1, source_target_pairs={{0,6},{1,33},{2,4},{3,35},{4,2},{5,37},{6,0},{7,39},{8,14},{9,41},... | collective-permute-start | bytes 344072 | tf_op jit(solution)/shard_map/ppermute | solution.py:517
  19.3 5.3 %collective-permute-start.2 = (f32[112,256]{1,0:T(8,128)S(1)}, f32[112,256]{1,0:T(8,128)S(1)}, u32[]{:S(2)}, u32[]{:S(2)}) collective-permute-start(f32[112,256]{1,0:T(8,128)S(1)} %add.35), channel_id=1, source_target_pairs={{0,2},{1,97},{2,0},{3,99},{4,6},{5,101},{6,4},{7,103},{8,10},{9,10... | collective-permute-start | bytes 344072 | tf_op jit(solution)/shard_map/ppermute | solution.py:517
  24.6 5.2 %collective-permute-start.7 = (f32[112,256]{1,0:T(8,128)S(1)}, f32[112,256]{1,0:T(8,128)S(1)}, u32[]{:S(2)}, u32[]{:S(2)}) collective-permute-start(f32[112,256]{1,0:T(8,128)S(1)} %add_add_fusion.2), channel_id=1, source_target_pairs={{0,64},{1,5},{2,66},{3,7},{4,68},{5,1},{6,70},{7,3},{8,72},{9,13},... | collective-permute-start | bytes 344072 | tf_op jit(solution)/shard_map/ppermute | solution.py:517
  27.5 4.0 %collective-permute-start.6 = (f32[112,256]{1,0:T(8,128)S(1)}, f32[112,256]{1,0:T(8,128)S(1)}, u32[]{:S(2)}, u32[]{:S(2)}) collective-permute-start(f32[112,256]{1,0:T(8,128)S(1)} %add_add_fusion.2), channel_id=1, source_target_pairs={{0,96},{1,3},{2,98},{3,1},{4,100},{5,7},{6,102},{7,5},{8,104},{9,1... | collective-permute-start | bytes 344072 | tf_op jit(solution)/shard_map/ppermute | solution.py:517
  28.1 5.1 %collective-permute-start.5 = (f32[112,256]{1,0:T(8,128)S(1)}, f32[112,256]{1,0:T(8,128)S(1)}, u32[]{:S(2)}, u32[]{:S(2)}) collective-permute-start(f32[112,256]{1,0:T(8,128)S(1)} %add_add_fusion.2), channel_id=1, source_target_pairs={{0,32},{1,7},{2,34},{3,5},{4,36},{5,3},{6,38},{7,1},{8,40},{9,15},... | collective-permute-start | bytes 344072 | tf_op jit(solution)/shard_map/ppermute | solution.py:517
  33.2 5.3 %collective-permute-start.10 = (f32[112,256]{1,0:T(8,128)S(1)}, f32[112,256]{1,0:T(8,128)S(1)}, u32[]{:S(2)}, u32[]{:S(2)}) collective-permute-start(f32[112,256]{1,0:T(8,128)S(1)} %add_add_fusion.1), channel_id=1, source_target_pairs={{0,16},{1,17},{2,18},{3,19},{4,20},{5,21},{6,22},{7,23},{8,24},{9,... | collective-permute-start | bytes 344072 | tf_op jit(solution)/shard_map/ppermute | solution.py:517
  34.3 4.2 %collective-permute-start.9 = (f32[112,256]{1,0:T(8,128)S(1)}, f32[112,256]{1,0:T(8,128)S(1)}, u32[]{:S(2)}, u32[]{:S(2)}) collective-permute-start(f32[112,256]{1,0:T(8,128)S(1)} %add_add_fusion.1), channel_id=1, source_target_pairs={{0,24},{1,9},{2,26},{3,11},{4,28},{5,13},{6,30},{7,15},{8,16},{9,1... | collective-permute-start | bytes 344072 | tf_op jit(solution)/shard_map/ppermute | solution.py:517
  34.3 5.8 %collective-permute-start.8 = (f32[112,256]{1,0:T(8,128)S(1)}, f32[112,256]{1,0:T(8,128)S(1)}, u32[]{:S(2)}, u32[]{:S(2)}) collective-permute-start(f32[112,256]{1,0:T(8,128)S(1)} %add_add_fusion.1), channel_id=1, source_target_pairs={{0,8},{1,25},{2,10},{3,27},{4,12},{5,29},{6,14},{7,31},{8,0},{9,17... | collective-permute-start | bytes 344072 | tf_op jit(solution)/shard_map/ppermute | solution.py:517
  40.2 4.2 %collective-permute-start.11 = (f32[112,256]{1,0:T(8,128)S(1)}, f32[112,256]{1,0:T(8,128)S(1)}, u32[]{:S(2)}, u32[]{:S(2)}) collective-permute-start(f32[112,256]{1,0:T(8,128)S(1)} %add_add_fusion.mine_ref), channel_id=1, source_target_pairs={{0,1},{1,0},{2,3},{3,2},{4,5},{5,4},{6,7},{7,6},{8,9},{9,8},{10,11... | collective-permute-start | bytes 344072 | tf_op jit(solution)/shard_map/ppermute | solution.py:517
